TPU v7x, 256 devices: a whole 4x4x8 slice. The times are simulated.
256 devices in a mesh: seq: 8 (over z_lo, y), frm: 32 (over x, z_hi, core).
Axes of the slice: x: 4, y: 4, z: 8 (z_hi: 4, z_lo: 2; z = z_hi * 2 + z_lo), core: 2. Of those that a mesh axis runs over, the one named last changes fastest.
Arguments:
- queries: bfloat16 [64, 128, 5120], P('frm', 'seq'), may hold values from -26.4 to 26.4
- keys: bfloat16 [64, 128, 5120], P('frm', 'seq'), may hold values from -8.4 to 8.4
- values: bfloat16 [64, 128, 5120], P('frm', 'seq'), may hold values from -6 to 6
- clip_ids: int32 [64], replicated, may hold values from 0 to 4, never falling along the last dimension, each value on 1 to 33 neighbouring positions
- w_head: bfloat16 [5120, 64], replicated, may hold values from -1 to 1
- b_head: float32 [64], replicated, may hold values from -3 to 3
- w_in: bfloat16 [432, 384], replicated, may hold values from -0.3125 to 0.3125
- b_in: float32 [384], replicated, may hold values from -3 to 3
- gain_in: float32 [384], replicated, may hold values from 0.25 to 1.75
- w_up: bfloat16 [3456, 192], replicated, may hold values from -0.109375 to 0.109375
- b_up: float32 [192], replicated, may hold values from -3 to 3
Outputs:
- decoded: bfloat16 [64, 32, 12288], P('frm', 'seq')
Inputs may be any that keep to these rules, and one draw needn't show every extreme that they name: `clip_ids`: frames of one clip are consecutive and clip numbers never fall; every clip has 1 to 33 frames and one has exactly 33.
All inputs are finite; a program needn't handle non-finite values.
Results may differ from a plain program's by a relative error of at most 0.014.
Values may be sent and summed in bfloat16 or wider, within the bound.
No kernel may reach another device: no remote copies, remote signals or barrier semaphores. Data moves between devices by JAX's collectives and lax.ppermute only.
A program may use at most 128 MiB of HBM per device.

v0:
```python
import math

import jax
import jax.numpy as jnp
from jax import lax
from jax.sharding import PartitionSpec as P

HEADS = 40
HD = 128
LC = 16
C1 = 384
CO = 192
PW = 16


def passed_along(value, axis, by):
    peers = lax.axis_size(axis)
    pairs = [(i, i + by) for i in range(peers) if 0 <= i + by < peers]
    return lax.ppermute(value, axis, pairs)


def with_halo(cells, sides, width):
    for axis, dim in sides:
        count = lax.axis_size(axis)
        ends = count - 1
        head = lax.slice_in_dim(cells, 0, width, axis=dim)
        tail = lax.slice_in_dim(cells, cells.shape[dim] - width, cells.shape[dim], axis=dim)
        cells = jnp.concatenate(
            [
                lax.ppermute(tail, axis, [(i, (i + 1) % count) for i in range(ends)]),
                cells,
                lax.ppermute(head, axis, [((i + 1) % count, i) for i in range(ends)]),
            ],
            axis=dim,
        )
    return cells


def conv_layer(padded, frame_keep, out_rows, w_in, b_in, gain_in):
    frames = padded.shape[0] - 2
    lat_cols = padded.shape[2] - 2
    tap_list = []
    for time_tap in range(3):
        for row_tap in range(3):
            for col_tap in range(3):
                tap_list.append(
                    padded[
                        time_tap : time_tap + frames,
                        row_tap : row_tap + out_rows,
                        col_tap : col_tap + lat_cols,
                        :,
                    ]
                    * frame_keep[time_tap]
                )
    columns = jnp.concatenate(tap_list, axis=-1)
    hidden = (
        jnp.dot(columns.reshape(-1, columns.shape[-1]), w_in, preferred_element_type=jnp.float32)
        + b_in
    )
    mean_square = jnp.mean(hidden * hidden, axis=-1, keepdims=True)
    normed = hidden * lax.rsqrt(mean_square + 1e-06) * gain_in
    return jax.nn.silu(normed).astype(jnp.bfloat16).reshape(frames, out_rows, lat_cols, C1)


def shards(queries, keys, values, clip_ids, w_head, b_head, w_in, b_in, gain_in, w_up, b_up):
    groups = lax.axis_size("seq")
    frame_devices = lax.axis_size("frm")
    local_heads = HEADS // groups
    head_width = local_heads * HD
    q_all, k_all, v_all = (
        lax.all_to_all(queries, "seq", split_axis=2, concat_axis=1, tiled=True),
        lax.all_to_all(keys, "seq", split_axis=2, concat_axis=1, tiled=True),
        lax.all_to_all(values, "seq", split_axis=2, concat_axis=1, tiled=True),
    )
    frames = q_all.shape[0]
    frame_tok = q_all.shape[1]
    query_rows = frames * frame_tok
    total_frames = frames * frame_devices
    frame_position = lax.axis_index("frm")
    first_frame = frame_position * frames
    query_flat = q_all.reshape(query_rows, local_heads, HD)
    own_frames_clip = lax.dynamic_slice_in_dim(clip_ids, first_frame, frames, 0)
    own_clip = jnp.repeat(own_frames_clip, frame_tok)
    score_scale = 1.0 / math.sqrt(HD)
    initial = (
        jnp.full((local_heads, query_rows), -1e30, jnp.float32),
        jnp.zeros((local_heads, query_rows), jnp.float32),
        jnp.zeros((query_rows, local_heads, HD), jnp.float32),
    )
    carried = initial
    key_piece = lax.all_gather(k_all, "frm", axis=0, tiled=True)
    value_piece = lax.all_gather(v_all, "frm", axis=0, tiled=True)
    piece_frames = key_piece.shape[0]
    frame_step = math.gcd(piece_frames, 4)
    key_blocks = key_piece.reshape(
        piece_frames // frame_step, frame_step * frame_tok, local_heads, HD
    )
    value_blocks = value_piece.reshape(
        piece_frames // frame_step, frame_step * frame_tok, local_heads, HD
    )
    anchors = jnp.arange(piece_frames // frame_step, dtype=jnp.int32) * frame_step

    def absorb_block(running, block_item):
        key_block, value_block, anchor = block_item
        frame_ids = anchor + jnp.arange(frame_step, dtype=jnp.int32)
        in_range = (frame_ids >= 0) & (frame_ids < total_frames)
        key_frames_clip = jnp.where(
            in_range, lax.dynamic_slice_in_dim(clip_ids, anchor, frame_step, 0), -1
        )
        touches = jnp.any(own_frames_clip[:, None] == key_frames_clip[None, :])

        def attend_block(state):
            row_top, row_total, mixed_sum = state
            key_clip = jnp.repeat(key_frames_clip, frame_tok)
            scores = (
                jnp.einsum(
                    "qhd,khd->hqk", query_flat, key_block, preferred_element_type=jnp.float32
                )
                * score_scale
            )
            same_clip = (own_clip[:, None] == key_clip[None, :])[None]
            new_top = jnp.maximum(row_top, jnp.max(jnp.where(same_clip, scores, -1e30), axis=2))
            fading = jnp.exp(row_top - new_top)
            weights = jnp.where(same_clip, jnp.exp(scores - new_top[..., None]), 0.0)
            row_total = row_total * fading + jnp.sum(weights, axis=2)
            mixed_sum = mixed_sum * fading.T[..., None] + jnp.einsum(
                "hqk,khd->qhd",
                weights.astype(jnp.bfloat16),
                value_block,
                preferred_element_type=jnp.float32,
            )
            return (new_top, row_total, mixed_sum)

        def keep_block(state):
            return state

        return (lax.cond(touches, attend_block, keep_block, running), None)

    carried, unused = lax.scan(absorb_block, carried, (key_blocks, value_blocks, anchors))
    row_top, row_total, mixed_sum = carried
    attended = (
        (mixed_sum / row_total.T[..., None])
        .astype(jnp.bfloat16)
        .reshape(frames, frame_tok, head_width)
    )
    tokens_back = lax.all_to_all(attended, "seq", split_axis=1, concat_axis=2, tiled=True)
    latent = (
        jnp.einsum("ftd,dc->ftc", tokens_back, w_head, preferred_element_type=jnp.float32) + b_head
    )
    latent = latent.astype(jnp.bfloat16)
    patch_rows = latent.shape[1] // PW
    lat_rows = 2 * patch_rows
    lat_cols = 2 * PW
    latent_grid = (
        latent.reshape(frames, patch_rows, PW, 2, 2, LC)
        .transpose(0, 1, 3, 2, 4, 5)
        .reshape(frames, lat_rows, lat_cols, LC)
    )
    earlier = passed_along(latent_grid, "frm", 1)
    stacked = jnp.concatenate([earlier, latent_grid], axis=0)
    clip_padded = jnp.concatenate([jnp.full((2,), -1, jnp.int32), clip_ids])
    frame_keep = []
    for time_tap in range(3):
        earlier_clip = lax.dynamic_slice_in_dim(clip_padded, first_frame + time_tap, frames, 0)
        frame_keep.append(
            (earlier_clip == own_frames_clip).astype(jnp.bfloat16)[:, None, None, None]
        )
    padded = with_halo(stacked, (("seq", 1),), 1)
    padded = jnp.pad(padded, ((0, 0), (0, 0), (1, 1), (0, 0)))
    active = conv_layer(padded, frame_keep, lat_rows, w_in, b_in, gain_in)
    border = with_halo(active, (("seq", 1),), 1)
    middle = jnp.repeat(border[:, 1:-1], 2, axis=1)
    upsampled = jnp.concatenate([border[:, :1], middle, border[:, -1:]], axis=1)
    upsampled = jnp.repeat(upsampled, 2, axis=2)
    upsampled = jnp.pad(upsampled, ((0, 0), (0, 0), (1, 1), (0, 0)))
    up_rows = 2 * lat_rows
    up_cols = 2 * lat_cols
    tap_list = []
    for row_tap in range(3):
        for col_tap in range(3):
            tap_list.append(
                upsampled[:, row_tap : row_tap + up_rows, col_tap : col_tap + up_cols, :]
            )
    columns = jnp.concatenate(tap_list, axis=-1)
    result = jnp.dot(columns.reshape(-1, 9 * C1), w_up, preferred_element_type=jnp.float32) + b_up
    return result.astype(jnp.bfloat16).reshape(frames, up_rows, up_cols * CO)


def solution(mesh):
    in_specs = (
        P("frm", "seq", None),
        P("frm", "seq", None),
        P("frm", "seq", None),
        P(),
        P(),
        P(),
        P(),
        P(),
        P(),
        P(),
        P(),
    )
    out_specs = P("frm", "seq", None)
    return jax.shard_map(shards, mesh=mesh, in_specs=in_specs, out_specs=out_specs, check_vma=False)
```

profile of v0, /device:TPU:158, one launch (start us, length us, event | category | flops | bytes accessed | tf_op | source)
XLA Modules:
  0.0 443.3 jit_solution(8262532766673365746)
XLA Ops:
  6.5 5.7 %copy.80 = bf16[2,16,5120]{1,0,2:T(2,128)(2,1)} copy(bf16[2,16,5120]{2,1,0:T(8,128)(2,1)} %param.16) | data formatting | bytes 655360 | tf_op args[1]
  12.2 8.1 %reshape.110 = bf16[8,2,10240]{2,1,0:T(2,128)(2,1)S(1)} reshape(bf16[5120,2,16]{2,1,0:T(2,128)(2,1)} %bitcast.86) | data formatting | bytes 655360
  20.3 11.1 %all_to_all.69 = bf16[8,2,10240]{2,1,0:T(2,128)(2,1)S(1)} all-to-all(bf16[8,2,10240]{2,1,0:T(2,128)(2,1)S(1)} %reshape.110), channel_id=1, replica_groups=mesh['seq'=8,'frm'=32] {'seq'}, dimensions={0} | all-to-all | bytes 655360 | tf_op jit(solution)/shard_map/all_to_all | solution.py:72
  31.4 2.9 reshape.111
  34.3 5.9 %copy.101 = bf16[2,16,8,640]{3,1,2,0:T(8,128)(2,1)} copy(bf16[2,16,8,640]{1,0,3,2:T(2,128)(2,1)} %bitcast.83) | data formatting | bytes 655360 | tf_op jit(solution)/shard_map/all_to_all | solution.py:72
  40.3 4.1 copy.86
  44.4 8.1 %reshape.114 = bf16[8,2,10240]{2,1,0:T(2,128)(2,1)S(1)} reshape(bf16[5120,2,16]{2,1,0:T(2,128)(2,1)} %bitcast.87) | data formatting | bytes 655360
  52.5 17.3 %all_to_all.70 = bf16[8,2,10240]{2,1,0:T(2,128)(2,1)S(1)} all-to-all(bf16[8,2,10240]{2,1,0:T(2,128)(2,1)S(1)} %reshape.114), channel_id=1, replica_groups=mesh['seq'=8,'frm'=32] {'seq'}, dimensions={0} | all-to-all | bytes 655360 | tf_op jit(solution)/shard_map/all_to_all | solution.py:73
  69.8 2.9 reshape.115
  72.7 5.9 %copy.105 = bf16[2,16,8,640]{3,1,2,0:T(8,128)(2,1)} copy(bf16[2,16,8,640]{1,0,3,2:T(2,128)(2,1)} %bitcast.84) | data formatting | bytes 655360 | tf_op jit(solution)/shard_map/all_to_all | solution.py:73
  78.6 4.1 copy.84
  82.7 8.7 %reshape.112 = bf16[8,2,10240]{2,1,0:T(2,128)(2,1)} reshape(bf16[5120,2,16]{2,1,0:T(2,128)(2,1)} %bitcast.88) | data formatting | bytes 655360
  91.4 5.6 %all-to-all-start.1 = ((bf16[8,2,10240]{2,1,0:T(2,128)(2,1)}), bf16[8,2,10240]{2,1,0:T(2,128)(2,1)S(1)}, u32[]{:S(2)}, u32[]{:S(2)}) async-start(bf16[8,2,10240]{2,1,0:T(2,128)(2,1)} %reshape.112), calls=%async_computation.1 | async-start | bytes 655360 | tf_op jit(solution)/shard_map/all_to_all | solution.py:71
  97.0 18.7 %all-to-all-done.1 = bf16[8,2,10240]{2,1,0:T(2,128)(2,1)S(1)} async-done(((bf16[8,2,10240]{2,1,0:T(2,128)(2,1)}), bf16[8,2,10240]{2,1,0:T(2,128)(2,1)S(1)}, u32[]{:S(2)}, u32[]{:S(2)}) %all-to-all-start.1) | async-done | bytes 327712 | tf_op jit(solution)/shard_map/all_to_all | solution.py:71
  115.8 2.9 reshape.113
  118.7 4.8 %copy.85 = bf16[2,16,8,640]{3,1,2,0:T(8,128)(2,1)S(1)} copy(bf16[2,16,8,640]{1,0,3,2:T(2,128)(2,1)} %bitcast.85) | data formatting | bytes 655360 | tf_op jit(solution)/shard_map/all_to_all | solution.py:71
  124.0 8.3 %all-gather.3.cloned.1.call-done = bf16[64,128,640]{2,1,0:T(8,128)(2,1)} async-done(((bf16[2,128,640]{2,1,0:T(8,128)(2,1)}), bf16[64,128,640]{2,1,0:T(8,128)(2,1)}) %all-gather.3.cloned.1.call-update) | async-done | bytes 10485776 | tf_op jit(solution)/shard_map/all_gather | solution.py:91
  132.3 23.6 %reshape.108 = bf16[16,512,5,128]{3,2,1,0:T(8,128)(2,1)} reshape(bf16[64,128,640]{2,1,0:T(8,128)(2,1)} %all-gather.3.cloned.1.call-done) | data formatting | bytes 20971520 | tf_op jit(solution)/shard_map/reshape | solution.py:95
  155.9 12.4 %copy.90 = bf16[16,512,5,128]{3,1,2,0:T(8,128)(2,1)} copy(bf16[16,512,5,128]{3,2,1,0:T(8,128)(2,1)} %reshape.108) | data formatting | bytes 20971520
  168.2 54.7 %all-gather.5.cloned.1.call-done = bf16[64,128,640]{2,1,0:T(8,128)(2,1)} async-done(((bf16[2,128,640]{2,1,0:T(8,128)(2,1)}), bf16[64,128,640]{2,1,0:T(8,128)(2,1)}) %all-gather.5.cloned.1.call-update) | async-done | bytes 10485776 | tf_op jit(solution)/shard_map/all_gather | solution.py:92
  223.0 23.5 %reshape.109 = bf16[16,512,5,128]{3,2,1,0:T(8,128)(2,1)} reshape(bf16[64,128,640]{2,1,0:T(8,128)(2,1)} %all-gather.5.cloned.1.call-done) | data formatting | bytes 20971520 | tf_op jit(solution)/shard_map/reshape | solution.py:98
  246.5 12.4 %copy.92 = bf16[16,512,5,128]{3,1,2,0:T(8,128)(2,1)} copy(bf16[16,512,5,128]{3,2,1,0:T(8,128)(2,1)} %reshape.109) | data formatting | bytes 20971520
  259.0 94.6 %while.16 = (s32[]{:T(128)}, f32[5,256]{1,0:T(8,128)S(1)}, f32[5,256]{1,0:T(8,128)S(1)}, f32[256,5,128]{2,0,1:T(8,128)S(1)}, s32[2]{0:T(128)S(1)}, /*index=5*/s3...) while((s32[]{:T(128)}, f32[5,256]{1,0:T(8,128)S(1)}, ...), condition=%wide.region_6.7_spmd.clone.clone, body=%wide.region_0.6_spmd.clone.clone.sunk | while | flops 343215904 | bytes 11427209 | solution.py:139
  262.5 0.8 compare_reduce_fusion.2
  267.6 0.8 compare_reduce_fusion.2
  277.6 0.8 compare_reduce_fusion.2
  302.7 0.8 compare_reduce_fusion.2
  329.4 4.7 %conditional.4 = ((f32[5,256]{1,0:T(8,128)S(1)}, f32[5,256]{1,0:T(8,128)S(1)}, f32[256,5,128]{2,0,1:T(8,128)S(1)})) conditional(s32[]{:T(128)} %convert_element_type.56, (f32[5,256]{1,0:T(8,128)S(1)}, f32[5,256]{1,0:T(8,128)S(1)}, f32[256,5,128]{2,0,1:T(8,128)S(1)}) %tuple.93, (s32[2]{0:T(128)S(1)}, s32[4]{0:T(128)S(1)}, ...), branch_computations={%region_2.2_spmd, %region_3.5_spmd} | conditional | flops 343215872 | bytes 11426872 | solution.py:137
  329.7 1.7 fusion.2
  331.9 2.2 fusion.16
  339.1 4.7 %conditional.4 = ((f32[5,256]{1,0:T(8,128)S(1)}, f32[5,256]{1,0:T(8,128)S(1)}, f32[256,5,128]{2,0,1:T(8,128)S(1)})) conditional(s32[]{:T(128)} %convert_element_type.56, (f32[5,256]{1,0:T(8,128)S(1)}, f32[5,256]{1,0:T(8,128)S(1)}, f32[256,5,128]{2,0,1:T(8,128)S(1)}) %tuple.93, (s32[2]{0:T(128)S(1)}, s32[4]{0:T(128)S(1)}, ...), branch_computations={%region_2.2_spmd, %region_3.5_spmd} | conditional | flops 343215872 | bytes 11426872 | solution.py:137
  339.4 1.7 fusion.2
  341.7 2.2 fusion.16
  348.9 4.7 %conditional.4 = ((f32[5,256]{1,0:T(8,128)S(1)}, f32[5,256]{1,0:T(8,128)S(1)}, f32[256,5,128]{2,0,1:T(8,128)S(1)})) conditional(s32[]{:T(128)} %convert_element_type.56, (f32[5,256]{1,0:T(8,128)S(1)}, f32[5,256]{1,0:T(8,128)S(1)}, f32[256,5,128]{2,0,1:T(8,128)S(1)}) %tuple.93, (s32[2]{0:T(128)S(1)}, s32[4]{0:T(128)S(1)}, ...), branch_computations={%region_2.2_spmd, %region_3.5_spmd} | conditional | flops 343215872 | bytes 11426872 | solution.py:137
  349.2 1.7 fusion.2
  351.4 2.2 fusion.16
  354.2 1.0 copy.94
  355.2 10.9 %all_to_all.71 = bf16[2,128,640]{2,0,1:T(2,128)(2,1)S(1)} all-to-all(bf16[2,128,640]{2,0,1:T(2,128)(2,1)S(1)} %copy.94), channel_id=1, replica_groups=mesh['seq'=8,'frm'=32] {'seq'}, dimensions={1} | all-to-all | bytes 655360 | tf_op jit(solution)/shard_map/all_to_all | solution.py:146
  366.7 1.9 collective-permute-start
  368.6 40.2 %collective-permute-done = bf16[2,2,32,16]{3,2,1,0:T(8,128)(2,1)S(1)} collective-permute-done((bf16[2,2,32,16]{3,2,1,0:T(8,128)(2,1)S(1)}, bf16[2,2,32,16]{3,2,1,0:T(8,128)(2,1)S(1)}, u32[]{:S(2)}, u32[]{:S(2)}) %collective-permute-start) | collective-permute-done | bytes 4128 | tf_op jit(solution)/shard_map/ppermute | solution.py:19
  408.8 4.3 collective-permute-start.1
  413.1 1.9 collective-permute-start.2
  415.1 5.9 %collective-permute-done.2 = bf16[4,1,32,16]{3,2,1,0:T(8,128)(2,1)S(1)} collective-permute-done((bf16[4,1,32,16]{3,2,1,0:T(8,128)(2,1)S(1)}, bf16[4,1,32,16]{3,2,1,0:T(8,128)(2,1)S(1)}, u32[]{:S(2)}, u32[]{:S(2)}) %collective-permute-start.2) | collective-permute-done | bytes 4128 | tf_op jit(solution)/shard_map/ppermute | solution.py:32
  422.2 1.9 collective-permute-start.3
  424.1 4.1 collective-permute-start.4
  428.3 3.9 collective-permute-done.4
  434.0 1.3 fusion.29
  435.4 1.0 reshape.106
  (144 shorter events, 39.8 us)
Async XLA Ops:
  6.5 427.4 %copy-start = (bf16[3456,192]{0,1:T(8,128)(2,1)S(1)}, bf16[3456,192]{0,1:T(8,128)(2,1)}, u32[]{:S(2)}) copy-start(bf16[3456,192]{0,1:T(8,128)(2,1)} %param.24) | copy-start | bytes 3981316
  6.5 125.7 %all-gather.3.cloned.1.call-start = ((), (), s32[]{:S(2)}) async-start(), calls=%async_computation.4 | async-start | bytes 10813440 | tf_op jit(solution)/shard_map/all_gather | solution.py:91
  20.3 20.0 %copy-start.3 = (bf16[2,16,5120]{2,1,0:T(8,128)(2,1)S(1)}, bf16[2,16,5120]{2,1,0:T(8,128)(2,1)}, u32[]{:S(2)}) copy-start(bf16[2,16,5120]{2,1,0:T(8,128)(2,1)} %param.17) | copy-start | bytes 983044
  40.2 182.7 %all-gather.5.cloned.1.call-start = ((), (), s32[]{:S(2)}) async-start(), calls=%async_computation.5 | async-start | bytes 10813440 | tf_op jit(solution)/shard_map/all_gather | solution.py:92
  52.4 26.1 %copy-start.4 = (bf16[2,16,5120]{2,1,0:T(8,128)(2,1)S(1)}, bf16[2,16,5120]{2,1,0:T(8,128)(2,1)}, u32[]{:S(2)}) copy-start(bf16[2,16,5120]{2,1,0:T(8,128)(2,1)} %param.15) | copy-start | bytes 983044
  78.6 18.4 %copy-start.5 = (s32[64]{0:T(128)S(1)}, s32[64]{0:T(128)}, u32[]{:S(2)}) copy-start(s32[64]{0:T(128)} %param.18) | copy-start | bytes 772
  91.4 24.4 %all-to-all-start.1 = ((bf16[8,2,10240]{2,1,0:T(2,128)(2,1)}), bf16[8,2,10240]{2,1,0:T(2,128)(2,1)S(1)}, u32[]{:S(2)}, u32[]{:S(2)}) async-start(bf16[8,2,10240]{2,1,0:T(2,128)(2,1)} %reshape.112), calls=%async_computation.1 | async-start | bytes 655360 | tf_op jit(solution)/shard_map/all_to_all | solution.py:71
  353.6 12.6 %copy-start.1 = (bf16[5120,64]{0,1:T(8,128)(2,1)S(1)}, bf16[5120,64]{0,1:T(8,128)(2,1)}, u32[]{:S(2)}) copy-start(bf16[5120,64]{0,1:T(8,128)(2,1)} %param.19) | copy-start | bytes 1966084
  353.6 12.6 %copy-start.8 = (f32[64]{0:T(128)S(1)}, f32[64]{0:T(128)}, u32[]{:S(2)}) copy-start(f32[64]{0:T(128)} %param.20) | copy-start | bytes 772
  354.2 67.6 %copy-start.2 = (bf16[432,384]{1,0:T(8,128)(2,1)S(1)}, bf16[432,384]{1,0:T(8,128)(2,1)}, u32[]{:S(2)}) copy-start(bf16[432,384]{1,0:T(8,128)(2,1)} %param.21) | copy-start | bytes 995332
  354.2 67.6 %copy-start.6 = (f32[384]{0:T(512)S(1)}, f32[384]{0:T(512)}, u32[]{:S(2)}) copy-start(f32[384]{0:T(512)} %param.22) | copy-start | bytes 4612
  355.2 66.8 %copy-start.7 = (f32[384]{0:T(512)S(1)}, f32[384]{0:T(512)}, u32[]{:S(2)}) copy-start(f32[384]{0:T(512)} %param.23) | copy-start | bytes 4612
  366.7 42.1 %collective-permute-start = (bf16[2,2,32,16]{3,2,1,0:T(8,128)(2,1)S(1)}, bf16[2,2,32,16]{3,2,1,0:T(8,128)(2,1)S(1)}, u32[]{:S(2)}, u32[]{:S(2)}) collective-permute-start(bf16[2,2,32,16]{3,2,1,0:T(8,128)(2,1)S(1)} %bitcast.96), channel_id=1, source_target_pairs={{0,1},{1,2},{2,3},{3,4},{4,5},{5,6},{6,7},{7,8},{8,9},{9,10},{10,1... | collective-permute-start | bytes 12296 | tf_op jit(solution)/shard_map/ppermute | solution.py:19
  408.8 6.4 %collective-permute-start.1 = (bf16[4,1,32,16]{3,2,1,0:T(8,128)(2,1)S(1)}, bf16[4,1,32,16]{3,2,1,0:T(8,128)(2,1)S(1)}, u32[]{:S(2)}, u32[]{:S(2)}) collective-permute-start(bf16[4,1,32,16]{3,2,1,0:T(8,128)(2,1)S(1)} %get-tuple-element.314), channel_id=1, source_target_pairs={{0,32},{32,64},{64,96},{96,128},{128,160},{160,192},{192,224},{1,3... | collective-permute-start | bytes 12296 | tf_op jit(solution)/shard_map/ppermute | solution.py:30
  413.1 7.9 %collective-permute-start.2 = (bf16[4,1,32,16]{3,2,1,0:T(8,128)(2,1)S(1)}, bf16[4,1,32,16]{3,2,1,0:T(8,128)(2,1)S(1)}, u32[]{:S(2)}, u32[]{:S(2)}) collective-permute-start(bf16[4,1,32,16]{3,2,1,0:T(8,128)(2,1)S(1)} %get-tuple-element.315), channel_id=1, source_target_pairs={{32,0},{64,32},{96,64},{128,96},{160,128},{192,160},{224,192},{33,... | collective-permute-start | bytes 12296 | tf_op jit(solution)/shard_map/ppermute | solution.py:32
  422.2 6.1 %collective-permute-start.3 = (bf16[2,1,32,384]{3,2,1,0:T(8,128)(2,1)S(1)}, bf16[2,1,32,384]{3,2,1,0:T(8,128)(2,1)S(1)}, u32[]{:S(2)}, u32[]{:S(2)}) collective-permute-start(bf16[2,1,32,384]{3,2,1,0:T(8,128)(2,1)S(1)} %get-tuple-element.304), channel_id=1, source_target_pairs={{0,32},{32,64},{64,96},{96,128},{128,160},{160,192},{192,224},{1,3... | collective-permute-start | bytes 147464 | tf_op jit(solution)/shard_map/ppermute | solution.py:30
  424.1 8.1 %collective-permute-start.4 = (bf16[2,1,32,384]{3,2,1,0:T(8,128)(2,1)S(1)}, bf16[2,1,32,384]{3,2,1,0:T(8,128)(2,1)S(1)}, u32[]{:S(2)}, u32[]{:S(2)}) collective-permute-start(bf16[2,1,32,384]{3,2,1,0:T(8,128)(2,1)S(1)} %get-tuple-element.305), channel_id=1, source_target_pairs={{32,0},{64,32},{96,64},{128,96},{160,128},{192,160},{224,192},{33,... | collective-permute-start | bytes 147464 | tf_op jit(solution)/shard_map/ppermute | solution.py:32
  433.0 0.9 copy-start.9
Sparse Core Ops, SparseCore 0:
  40.3 91.8 all-gather.2
  134.8 88.0 all-gather.4
where the time goes:
time: 448 us; the launch traced here: 443 us
  local copies, waits for them, and re-layouts  152 us (34%)
  waiting for transfers between devices  132 us (29%)
  loops' own time  45.1 us (10%)
  blocking collectives  39.3 us (9%)
  other arithmetic  27.9 us (6%)
  starting transfers between devices  19.8 us (4%)
  between operations  13.9 us (3%)
  matrix products  13.4 us (3%)
    unnamed x40, local copies, waits for them, and re-layouts  73.1 us
    all_gather x1, waiting for transfers between devices, shards(): value_piece = lax.all_gather(v_all, 'frm', axis=0, tiled=True)  54.7 us
    another operation x1, loops' own time, shards(): lax.scan(absorb_block, carried, (key_blocks, value_blocks, anchors))  44.7 us
    ppermute x1, waiting for transfers between devices, passed_along(): return lax.ppermute(value, axis, pairs)  40.2 us
    reshape x1, local copies, waits for them, and re-layouts, shards(): key_piece.reshape(piece_frames // frame_step, frame_step * frame_tok, loc...  23.6 us
    reshape x1, local copies, waits for them, and re-layouts, shards(): value_piece.reshape(piece_frames // frame_step, frame_step * frame_tok, l...  23.5 us
    all_to_all x1, waiting for transfers between devices, shards(): lax.all_to_all(queries, 'seq', split_axis=2, concat_axis=1, tiled=True)  18.7 us
    all_to_all x1, blocking collectives, shards(): lax.all_to_all(values, 'seq', split_axis=2, concat_axis=1, tiled=True)  17.3 us
  transfers between devices with their start and end apart: 8, of which 6 were waited for; matrix products, arithmetic and copies ran while one was open for 18% of the time, Pallas kernels for 0%

commit v1 on v0

v1 whole, which is shorter than its diff:
```python
import math

import jax
import jax.numpy as jnp
from jax import lax
from jax.experimental import pallas as pl
from jax.experimental.pallas import tpu as pltpu
from jax.sharding import PartitionSpec as P

HEADS = 40
HD = 128
LC = 16
C1 = 384
CO = 192
PW = 16
SEQ = 8
FRM = 32
GROUPS = 5
SLOT = 32
LAT = 64
TILE_F = 4
TILES = FRM // TILE_F
TILE_Q = TILE_F * 64
BLOCK_F = 2
BLOCK_K = BLOCK_F * 128
MAX_BLOCKS = FRM // BLOCK_F
COEF = math.log2(math.e) / math.sqrt(HD)
FAR = -1e30


def pack_kernel(q_ref, k_ref, v_ref, w_ref, out_ref):
    low = lax.broadcasted_iota(jnp.int32, (8, HD), 1) < LAT
    for s in range(SEQ):
        cols = slice(s * HD, (s + 1) * HD)
        w = w_ref[cols, :]
        w2 = jnp.concatenate([w, w], axis=1)
        v = jnp.concatenate([v_ref[0, :, cols], v_ref[1, :, cols]], axis=0)
        proj = jnp.dot(v, w2, preferred_element_type=jnp.float32)
        for c in range(2):
            top = proj[c * 16 : c * 16 + 8]
            bottom = proj[c * 16 + 8 : c * 16 + 16]
            packed = jnp.where(low, top, bottom)
            k = k_ref[c, :, cols]
            q = q_ref[c, :, cols].astype(jnp.float32)
            for ab in range(2):
                tail = jnp.concatenate([packed, q[ab * 8 : ab * 8 + 8]], axis=0)
                out_ref[0, ab, c, s, 0:16, :] = k
                out_ref[0, ab, c, s, 16:32, :] = tail.astype(jnp.bfloat16)


def pack(queries, keys, values, w_head):
    span = SEQ * HD
    act = pl.BlockSpec((2, 16, span), lambda i: (0, 0, i))
    return pl.pallas_call(
        pack_kernel,
        grid=(GROUPS,),
        in_specs=[act, act, act, pl.BlockSpec((span, LAT), lambda i: (i, 0))],
        out_specs=pl.BlockSpec((1, 2, 2, SEQ, SLOT, HD), lambda i: (i, 0, 0, 0, 0, 0)),
        out_shape=jax.ShapeDtypeStruct((8, 2, 2, SEQ, SLOT, HD), jnp.bfloat16),
        compiler_params=pltpu.CompilerParams(vmem_limit_bytes=32 * 1024 * 1024),
    )(queries, keys, values, w_head)


def attend_kernel(meta_ref, own_ref, other_ref, out_ref, vt_ref, s_ref):
    lane = lax.broadcasted_iota(jnp.int32, (8, HD), 1)
    low = lane < LAT

    def spread(i, carry):
        for side, ref in enumerate((own_ref, other_ref)):
            rows = []
            for s in range(SEQ):
                packed = ref[i, s, 16:32, :].astype(jnp.float32)[0:8]
                rows.append(jnp.where(low, packed, 1.0))
                rows.append(jnp.where(low, pltpu.roll(packed, LAT, 1), 1.0))
            block = jnp.concatenate(rows, axis=0)
            vt_ref[side, i] = block.T.astype(jnp.bfloat16)
        return carry

    lax.fori_loop(0, FRM, spread, 0)

    q_frame = lax.broadcasted_iota(jnp.int32, (1, TILE_Q), 1) // 64
    row_top = lax.broadcasted_iota(jnp.int32, (8, HD), 0) < 4

    def tile(t, carry):
        first = meta_ref[2 * FRM + t]
        last = meta_ref[2 * FRM + TILES + t]
        blocks = lax.div(last - first + (BLOCK_F - 1), BLOCK_F)
        q = own_ref[pl.ds(t * TILE_F, TILE_F), :, 16:32, :].astype(jnp.float32)
        q = q[:, :, 8:16].reshape(TILE_Q, HD).astype(jnp.bfloat16)
        q_clip = jnp.zeros((1, TILE_Q), jnp.int32)
        for j in range(TILE_F):
            q_clip = jnp.where(q_frame == j, meta_ref[t * TILE_F + j], q_clip)

        def score(b, top):
            begin = first + b * BLOCK_F
            start = jnp.minimum(begin, FRM - BLOCK_F)
            for side, ref in enumerate((own_ref, other_ref)):
                k = ref[pl.ds(start, BLOCK_F), :, 0:16, :].reshape(BLOCK_K, HD)
                s = lax.dot_general(
                    k, q, (((1,), (1,)), ((), ())), preferred_element_type=jnp.float32
                )
                for j in range(BLOCK_F):
                    clip = meta_ref[side * FRM + start + j]
                    clip = jnp.where(start + j >= begin, clip, -1)
                    bias = jnp.where(q_clip == clip, 0.0, FAR)
                    part = s[j * 128 : (j + 1) * 128] + bias
                    s_ref[b, side, pl.ds(j * 128, 128), :] = part
                    top = jnp.maximum(top, jnp.max(part.reshape(16, 8, TILE_Q), axis=0))
            return top

        top = lax.fori_loop(0, blocks, score, jnp.full((8, TILE_Q), FAR, jnp.float32))
        top = jnp.max(top, axis=0, keepdims=True)

        def mix(b, total):
            start = jnp.minimum(first + b * BLOCK_F, FRM - BLOCK_F)
            for side in range(2):
                weights = jnp.exp2((s_ref[b, side] - top) * COEF).astype(jnp.bfloat16)
                for j in range(BLOCK_F):
                    total = total + jnp.dot(
                        vt_ref[side, start + j],
                        weights[j * 128 : (j + 1) * 128],
                        preferred_element_type=jnp.float32,
                    )
            return total

        total = lax.fori_loop(0, blocks, mix, jnp.zeros((HD, TILE_Q), jnp.float32))
        mixed = total[:LAT] / total[LAT : LAT + 1]
        tokens = jnp.concatenate([mixed, mixed], axis=0).T
        for j in range(TILE_Q // 16):
            a = tokens[j * 16 : j * 16 + 8]
            b = tokens[j * 16 + 8 : j * 16 + 16]
            a = jnp.where(low, a, pltpu.roll(a, 4, 0))
            b = jnp.where(low, pltpu.roll(b, 4, 0), b)
            out_ref[t, j] = jnp.where(row_top, a, b).astype(jnp.bfloat16)
        return carry

    lax.fori_loop(0, TILES, tile, 0)


def attend(meta, own, other):
    vmem = pl.BlockSpec(memory_space=pltpu.VMEM)
    return pl.pallas_call(
        attend_kernel,
        in_specs=[pl.BlockSpec(memory_space=pltpu.SMEM), vmem, vmem],
        out_specs=vmem,
        out_shape=jax.ShapeDtypeStruct((TILES, TILE_Q // 16, 8, HD), jnp.bfloat16),
        scratch_shapes=[
            pltpu.VMEM((2, FRM, HD, 128), jnp.bfloat16),
            pltpu.VMEM((MAX_BLOCKS, 2, BLOCK_K, TILE_Q), jnp.float32),
        ],
        compiler_params=pltpu.CompilerParams(vmem_limit_bytes=48 * 1024 * 1024),
    )(meta, own, other)


def passed_along(value, axis, by):
    peers = lax.axis_size(axis)
    pairs = [(i, i + by) for i in range(peers) if 0 <= i + by < peers]
    return lax.ppermute(value, axis, pairs)


def with_halo(cells, sides, width):
    for axis, dim in sides:
        count = lax.axis_size(axis)
        ends = count - 1
        head = lax.slice_in_dim(cells, 0, width, axis=dim)
        tail = lax.slice_in_dim(cells, cells.shape[dim] - width, cells.shape[dim], axis=dim)
        cells = jnp.concatenate(
            [
                lax.ppermute(tail, axis, [(i, (i + 1) % count) for i in range(ends)]),
                cells,
                lax.ppermute(head, axis, [((i + 1) % count, i) for i in range(ends)]),
            ],
            axis=dim,
        )
    return cells


def conv_layer(padded, frame_keep, out_rows, w_in, b_in, gain_in):
    frames = padded.shape[0] - 2
    lat_cols = padded.shape[2] - 2
    tap_list = []
    for time_tap in range(3):
        for row_tap in range(3):
            for col_tap in range(3):
                tap_list.append(
                    padded[
                        time_tap : time_tap + frames,
                        row_tap : row_tap + out_rows,
                        col_tap : col_tap + lat_cols,
                        :,
                    ]
                    * frame_keep[time_tap]
                )
    columns = jnp.concatenate(tap_list, axis=-1)
    hidden = (
        jnp.dot(columns.reshape(-1, columns.shape[-1]), w_in, preferred_element_type=jnp.float32)
        + b_in
    )
    mean_square = jnp.mean(hidden * hidden, axis=-1, keepdims=True)
    normed = hidden * lax.rsqrt(mean_square + 1e-06) * gain_in
    return jax.nn.silu(normed).astype(jnp.bfloat16).reshape(frames, out_rows, lat_cols, C1)


def shards(queries, keys, values, clip_ids, w_head, b_head, w_in, b_in, gain_in, w_up, b_up):
    frames = 2
    frame_position = lax.axis_index("frm")
    first_frame = frame_position * frames
    core = lax.rem(frame_position, 2)

    slots = pack(queries, keys, values, w_head).reshape(FRM * SEQ, SLOT, HD)
    own = lax.all_to_all(slots, ("frm", "seq"), 0, 0, tiled=True)
    other = lax.ppermute(own, "frm", [(i, i ^ 1) for i in range(FRM)])

    pairs = clip_ids.reshape(FRM, 2)
    own_clip = jnp.where(core == 0, pairs[:, 0], pairs[:, 1])
    other_clip = jnp.where(core == 0, pairs[:, 1], pairs[:, 0])
    below = jnp.sum(clip_ids[None, :] < own_clip[::TILE_F, None], axis=1, dtype=jnp.int32)
    upto = jnp.sum(
        clip_ids[None, :] <= own_clip[TILE_F - 1 :: TILE_F, None], axis=1, dtype=jnp.int32
    )
    meta = jnp.concatenate([own_clip, other_clip, below // 2, (upto + 1) // 2])
    mixed = attend(
        meta, own.reshape(FRM, SEQ, SLOT, HD), other.reshape(FRM, SEQ, SLOT, HD)
    ).reshape(FRM * SEQ, 4, HD)
    back = lax.all_to_all(mixed, ("frm", "seq"), 0, 0, tiled=True)
    back = back.reshape(8, 2, 2, SEQ, 4, HD)[:GROUPS].astype(jnp.float32)
    summed = jnp.sum(back, axis=(0, 3)).reshape(2, 2, 4, 2, LAT)
    latent = summed.transpose(1, 0, 3, 2, 4).reshape(frames, 16, LAT) + b_head
    latent = latent.astype(jnp.bfloat16)

    own_frames_clip = lax.dynamic_slice_in_dim(clip_ids, first_frame, frames, 0)
    patch_rows = latent.shape[1] // PW
    lat_rows = 2 * patch_rows
    lat_cols = 2 * PW
    latent_grid = (
        latent.reshape(frames, patch_rows, PW, 2, 2, LC)
        .transpose(0, 1, 3, 2, 4, 5)
        .reshape(frames, lat_rows, lat_cols, LC)
    )
    earlier = passed_along(latent_grid, "frm", 1)
    stacked = jnp.concatenate([earlier, latent_grid], axis=0)
    clip_padded = jnp.concatenate([jnp.full((2,), -1, jnp.int32), clip_ids])
    frame_keep = []
    for time_tap in range(3):
        earlier_clip = lax.dynamic_slice_in_dim(clip_padded, first_frame + time_tap, frames, 0)
        frame_keep.append(
            (earlier_clip == own_frames_clip).astype(jnp.bfloat16)[:, None, None, None]
        )
    padded = with_halo(stacked, (("seq", 1),), 1)
    padded = jnp.pad(padded, ((0, 0), (0, 0), (1, 1), (0, 0)))
    active = conv_layer(padded, frame_keep, lat_rows, w_in, b_in, gain_in)
    border = with_halo(active, (("seq", 1),), 1)
    middle = jnp.repeat(border[:, 1:-1], 2, axis=1)
    upsampled = jnp.concatenate([border[:, :1], middle, border[:, -1:]], axis=1)
    upsampled = jnp.repeat(upsampled, 2, axis=2)
    upsampled = jnp.pad(upsampled, ((0, 0), (0, 0), (1, 1), (0, 0)))
    up_rows = 2 * lat_rows
    up_cols = 2 * lat_cols
    tap_list = []
    for row_tap in range(3):
        for col_tap in range(3):
            tap_list.append(
                upsampled[:, row_tap : row_tap + up_rows, col_tap : col_tap + up_cols, :]
            )
    columns = jnp.concatenate(tap_list, axis=-1)
    result = jnp.dot(columns.reshape(-1, 9 * C1), w_up, preferred_element_type=jnp.float32) + b_up
    return result.astype(jnp.bfloat16).reshape(frames, up_rows, up_cols * CO)


def solution(mesh):
    in_specs = (
        P("frm", "seq", None),
        P("frm", "seq", None),
        P("frm", "seq", None),
        P(),
        P(),
        P(),
        P(),
        P(),
        P(),
        P(),
        P(),
    )
    out_specs = P("frm", "seq", None)
    return jax.shard_map(shards, mesh=mesh, in_specs=in_specs, out_specs=out_specs, check_vma=False)
```

time: 448 us -> 173 us (0.39)
  the two profiles are of different devices: /device:TPU:158 before, /device:TPU:26 now
where the time goes in v1:
time: 173 us
  blocking collectives  66 us (38%)
  Pallas kernels  38 us (22%)
  waiting for transfers between devices  32.6 us (19%)
  starting transfers between devices  23.7 us (14%)
  local copies, waits for them, and re-layouts  9.11 us (5%)
    all_to_all x1, blocking collectives, shards(): own = lax.all_to_all(slots, ('frm', 'seq'), 0, 0, tiled=True)  66 us
    pallas_call x1, Pallas kernels, attend(): pl.pallas_call(attend_kernel, in_specs=[pl.BlockSpec(memory_space=pltpu.S...  36.6 us
    all_to_all x1, waiting for transfers between devices, shards(): back = lax.all_to_all(mixed, ('frm', 'seq'), 0, 0, tiled=True)  12.8 us
    ppermute x2, waiting for transfers between devices, with_halo(): lax.ppermute(head, axis, [((i + 1) % count, i) for i in range(ends)])  9.93 us
    all_to_all x1, starting transfers between devices, shards(): back = lax.all_to_all(mixed, ('frm', 'seq'), 0, 0, tiled=True)  9.18 us
    ppermute x2, starting transfers between devices, with_halo(): lax.ppermute(tail, axis, [(i, (i + 1) % count) for i in range(ends)])  6.73 us
    ppermute x1, waiting for transfers between devices, passed_along(): return lax.ppermute(value, axis, pairs)  6.31 us
    unnamed x31, local copies, waits for them, and re-layouts  6.22 us
  transfers between devices with their start and end apart: 7, of which 6 were waited for; matrix products, arithmetic and copies ran while one was open for 1% of the time, Pallas kernels for 0%

profile of v1, /device:TPU:26, one launch (start us, length us, event | category | flops | bytes accessed | tf_op | source)
XLA Modules:
  0.0 172.6 jit_solution(3703305232546634060)
XLA Ops:
  0.0 1.8 %copy.20.w_ref = bf16[5120,64]{1,0:T(8,128)(2,1)S(1)} copy(bf16[5120,64]{0,1:T(8,128)(2,1)} %param.15) | data formatting | bytes 1310720 | tf_op args[4]
  1.8 1.0 copy-done.2
  2.7 1.0 copy-done.3
  3.7 1.0 copy-done.4
  4.7 1.4 shard_map.109
  6.1 66.0 %all_to_all.10 = bf16[256,32,128]{2,1,0:T(8,128)(2,1)S(1)} all-to-all(bf16[256,32,128]{2,1,0:T(8,128)(2,1)S(1)} %bitcast.19), channel_id=1, replica_groups=mesh['seq'=8,'frm'=32] {'frm','seq'}, dimensions={0} | all-to-all | bytes 4194304 | tf_op jit(solution)/shard_map/all_to_all | solution.py:211
  72.1 0.1 reshape.84
  72.2 0.2 select_reduce_fusion
  72.4 0.1 slice.158
  72.5 0.1 slice.157
  72.6 0.2 convert_reduce_fusion.2
  72.8 0.1 pad_add_fusion.meta_ref
  72.9 3.5 %collective-permute-done = bf16[256,32,128]{2,1,0:T(8,128)(2,1)} collective-permute-done((bf16[256,32,128]{2,1,0:T(8,128)(2,1)S(1)}, bf16[256,32,128]{2,1,0:T(8,128)(2,1)}, u32[]{:S(2)}, u32[]{:S(2)}) %collective-permute-start) | collective-permute-done | bytes 2097184 | tf_op jit(solution)/shard_map/ppermute | solution.py:212
  76.4 36.6 %shard_map.110 = bf16[8,16,8,128]{3,2,1,0:T(8,128)(2,1)S(1)} custom-call(s32[80]{0:T(128)S(1)} %pad_add_fusion.meta_ref, bf16[32,8,32,128]{3,2,1,0:T(8,128)(2,1)S(1)} %bitcast.18, bf16[32,8,32,128]{3,2,1,0:T(8,128)(2,1)} %bitcast.2.other_ref), custom_call_target="tpu_custom_call" | custom-call | tf_op jit(solution)/shard_map/pallas_call | solution.py:142
  113.0 0.7 copy-done.1
  113.7 9.2 %all-to-all-start.1 = ((bf16[256,4,128]{2,1,0:T(4,128)(2,1)}), bf16[256,4,128]{2,1,0:T(4,128)(2,1)S(1)}, u32[]{:S(2)}, u32[]{:S(2)}) async-start(bf16[256,4,128]{2,1,0:T(4,128)(2,1)} %bitcast.20), calls=%async_computation.1 | async-start | bytes 524288 | tf_op jit(solution)/shard_map/all_to_all | solution.py:225
  122.9 0.1 add.82
  122.9 12.8 %all-to-all-done.1 = bf16[256,4,128]{2,1,0:T(4,128)(2,1)S(1)} async-done(((bf16[256,4,128]{2,1,0:T(4,128)(2,1)}), bf16[256,4,128]{2,1,0:T(4,128)(2,1)S(1)}, u32[]{:S(2)}, u32[]{:S(2)}) %all-to-all-start.1) | async-done | bytes 262176 | tf_op jit(solution)/shard_map/all_to_all | solution.py:225
  135.8 0.1 convert_reduce_fusion
  135.9 0.1 reshape.89
  136.0 0.1 reshape.90
  136.2 1.9 %collective-permute-start.1 = (bf16[2,2,32,16]{3,2,1,0:T(8,128)(2,1)S(1)}, bf16[2,2,32,16]{3,2,1,0:T(8,128)(2,1)S(1)}, u32[]{:S(2)}, u32[]{:S(2)}) collective-permute-start(bf16[2,2,32,16]{3,2,1,0:T(8,128)(2,1)S(1)} %bitcast.23), channel_id=1, source_target_pairs={{0,1},{1,2},{2,3},{3,4},{4,5},{5,6},{6,7},{7,8},{8,9},{9,10},{10,1... | collective-permute-start | bytes 12296 | tf_op jit(solution)/shard_map/ppermute | solution.py:158
  138.1 6.3 %collective-permute-done.1 = bf16[2,2,32,16]{3,2,1,0:T(8,128)(2,1)S(1)} collective-permute-done((bf16[2,2,32,16]{3,2,1,0:T(8,128)(2,1)S(1)}, bf16[2,2,32,16]{3,2,1,0:T(8,128)(2,1)S(1)}, u32[]{:S(2)}, u32[]{:S(2)}) %collective-permute-start.1) | collective-permute-done | bytes 4128 | tf_op jit(solution)/shard_map/ppermute | solution.py:158
  144.4 4.8 %collective-permute-start.2 = (bf16[4,1,32,16]{3,2,1,0:T(8,128)(2,1)S(1)}, bf16[4,1,32,16]{3,2,1,0:T(8,128)(2,1)S(1)}, u32[]{:S(2)}, u32[]{:S(2)}) collective-permute-start(bf16[4,1,32,16]{3,2,1,0:T(8,128)(2,1)S(1)} %get-tuple-element.43), channel_id=1, source_target_pairs={{0,32},{32,64},{64,96},{96,128},{128,160},{160,192},{192,224},{1,3... | collective-permute-start | bytes 12296 | tf_op jit(solution)/shard_map/ppermute | solution.py:169
  149.2 1.9 %collective-permute-start.3 = (bf16[4,1,32,16]{3,2,1,0:T(8,128)(2,1)S(1)}, bf16[4,1,32,16]{3,2,1,0:T(8,128)(2,1)S(1)}, u32[]{:S(2)}, u32[]{:S(2)}) collective-permute-start(bf16[4,1,32,16]{3,2,1,0:T(8,128)(2,1)S(1)} %get-tuple-element.44), channel_id=1, source_target_pairs={{32,0},{64,32},{96,64},{128,96},{160,128},{192,160},{224,192},{33,... | collective-permute-start | bytes 12296 | tf_op jit(solution)/shard_map/ppermute | solution.py:171
  151.2 0.1 compare_convert_fusion
  151.3 5.9 %collective-permute-done.3 = bf16[4,1,32,16]{3,2,1,0:T(8,128)(2,1)S(1)} collective-permute-done((bf16[4,1,32,16]{3,2,1,0:T(8,128)(2,1)S(1)}, bf16[4,1,32,16]{3,2,1,0:T(8,128)(2,1)S(1)}, u32[]{:S(2)}, u32[]{:S(2)}) %collective-permute-start.3) | collective-permute-done | bytes 4128 | tf_op jit(solution)/shard_map/ppermute | solution.py:171
  157.2 0.1 select_maximum_fusion
  157.2 0.1 slice_multiply_fusion
  157.4 0.1 broadcast_multiply_fusion
  157.5 0.3 concatenate.37
  157.9 0.3 multiply_reduce_fusion
  158.2 0.1 multiply_convert_fusion
  158.4 1.9 %collective-permute-start.4 = (bf16[2,1,32,384]{3,2,1,0:T(8,128)(2,1)S(1)}, bf16[2,1,32,384]{3,2,1,0:T(8,128)(2,1)S(1)}, u32[]{:S(2)}, u32[]{:S(2)}) collective-permute-start(bf16[2,1,32,384]{3,2,1,0:T(8,128)(2,1)S(1)} %get-tuple-element.33), channel_id=1, source_target_pairs={{0,32},{32,64},{64,96},{96,128},{128,160},{160,192},{192,224},{1,3... | collective-permute-start | bytes 147464 | tf_op jit(solution)/shard_map/ppermute | solution.py:169
  160.3 3.9 %collective-permute-start.5 = (bf16[2,1,32,384]{3,2,1,0:T(8,128)(2,1)S(1)}, bf16[2,1,32,384]{3,2,1,0:T(8,128)(2,1)S(1)}, u32[]{:S(2)}, u32[]{:S(2)}) collective-permute-start(bf16[2,1,32,384]{3,2,1,0:T(8,128)(2,1)S(1)} %get-tuple-element.34), channel_id=1, source_target_pairs={{32,0},{64,32},{96,64},{128,96},{160,128},{192,160},{224,192},{33,... | collective-permute-start | bytes 147464 | tf_op jit(solution)/shard_map/ppermute | solution.py:171
  164.2 0.1 collective-permute-done.4
  164.3 4.0 %collective-permute-done.5 = bf16[2,1,32,384]{3,2,1,0:T(8,128)(2,1)S(1)} collective-permute-done((bf16[2,1,32,384]{3,2,1,0:T(8,128)(2,1)S(1)}, bf16[2,1,32,384]{3,2,1,0:T(8,128)(2,1)S(1)}, u32[]{:S(2)}, u32[]{:S(2)}) %collective-permute-start.5) | collective-permute-done | bytes 49184 | tf_op jit(solution)/shard_map/ppermute | solution.py:171
  168.5 0.4 broadcast_in_dim.5
  168.8 0.2 reshape.95
  169.1 0.1 fusion.1
  169.3 0.1 fusion.2
  169.4 0.1 fusion.3
  169.6 0.1 fusion.4
  169.8 0.1 fusion.5
  170.0 0.1 fusion.6
  170.1 1.3 fusion
  171.4 0.1 copy.23
  171.6 1.0 reshape.97
  (34 shorter events, 0.5 us)
Async XLA Ops:
  0.0 170.1 %copy-start = (bf16[3456,192]{0,1:T(8,128)(2,1)S(1)}, bf16[3456,192]{0,1:T(8,128)(2,1)}, u32[]{:S(2)}) copy-start(bf16[3456,192]{0,1:T(8,128)(2,1)} %param.20) | copy-start | bytes 3981316
  1.8 1.0 copy-start.2
  2.7 1.0 copy-start.3
  3.7 1.0 copy-start.4
  4.7 67.4 %copy-start.6 = (s32[64]{0:T(128)S(1)}, s32[64]{0:T(128)}, u32[]{:S(2)}) copy-start(s32[64]{0:T(128)} %param.14) | copy-start | bytes 772
  72.1 50.8 %copy-start.9 = (f32[64]{0:T(128)S(1)}, f32[64]{0:T(128)}, u32[]{:S(2)}) copy-start(f32[64]{0:T(128)} %param.16) | copy-start | bytes 772
  72.1 4.3 %collective-permute-start = (bf16[256,32,128]{2,1,0:T(8,128)(2,1)S(1)}, bf16[256,32,128]{2,1,0:T(8,128)(2,1)}, u32[]{:S(2)}, u32[]{:S(2)}) collective-permute-start(bf16[256,32,128]{2,1,0:T(8,128)(2,1)S(1)} %all_to_all.10), channel_id=1, source_target_pairs={{0,1},{1,0},{2,3},{3,2},{4,5},{5,4},{6,7},{7,6},{8,9},{9,8},{10,11... | collective-permute-start | bytes 6291464 | tf_op jit(solution)/shard_map/ppermute | solution.py:212
  112.9 0.7 copy-start.1
  113.7 44.2 %copy-start.5 = (bf16[432,384]{1,0:T(8,128)(2,1)S(1)}, bf16[432,384]{1,0:T(8,128)(2,1)}, u32[]{:S(2)}) copy-start(bf16[432,384]{1,0:T(8,128)(2,1)} %param.17) | copy-start | bytes 995332
  113.7 44.2 %copy-start.7 = (f32[384]{0:T(512)S(1)}, f32[384]{0:T(512)}, u32[]{:S(2)}) copy-start(f32[384]{0:T(512)} %param.18) | copy-start | bytes 4612
  113.7 44.5 %copy-start.8 = (f32[384]{0:T(512)S(1)}, f32[384]{0:T(512)}, u32[]{:S(2)}) copy-start(f32[384]{0:T(512)} %param.19) | copy-start | bytes 4612
  113.7 22.1 %all-to-all-start.1 = ((bf16[256,4,128]{2,1,0:T(4,128)(2,1)}), bf16[256,4,128]{2,1,0:T(4,128)(2,1)S(1)}, u32[]{:S(2)}, u32[]{:S(2)}) async-start(bf16[256,4,128]{2,1,0:T(4,128)(2,1)} %bitcast.20), calls=%async_computation.1 | async-start | bytes 524288 | tf_op jit(solution)/shard_map/all_to_all | solution.py:225
  136.2 8.2 %collective-permute-start.1 = (bf16[2,2,32,16]{3,2,1,0:T(8,128)(2,1)S(1)}, bf16[2,2,32,16]{3,2,1,0:T(8,128)(2,1)S(1)}, u32[]{:S(2)}, u32[]{:S(2)}) collective-permute-start(bf16[2,2,32,16]{3,2,1,0:T(8,128)(2,1)S(1)} %bitcast.23), channel_id=1, source_target_pairs={{0,1},{1,2},{2,3},{3,4},{4,5},{5,6},{6,7},{7,8},{8,9},{9,10},{10,1... | collective-permute-start | bytes 12296 | tf_op jit(solution)/shard_map/ppermute | solution.py:158
  144.4 6.8 %collective-permute-start.2 = (bf16[4,1,32,16]{3,2,1,0:T(8,128)(2,1)S(1)}, bf16[4,1,32,16]{3,2,1,0:T(8,128)(2,1)S(1)}, u32[]{:S(2)}, u32[]{:S(2)}) collective-permute-start(bf16[4,1,32,16]{3,2,1,0:T(8,128)(2,1)S(1)} %get-tuple-element.43), channel_id=1, source_target_pairs={{0,32},{32,64},{64,96},{96,128},{128,160},{160,192},{192,224},{1,3... | collective-permute-start | bytes 12296 | tf_op jit(solution)/shard_map/ppermute | solution.py:169
  149.2 7.9 %collective-permute-start.3 = (bf16[4,1,32,16]{3,2,1,0:T(8,128)(2,1)S(1)}, bf16[4,1,32,16]{3,2,1,0:T(8,128)(2,1)S(1)}, u32[]{:S(2)}, u32[]{:S(2)}) collective-permute-start(bf16[4,1,32,16]{3,2,1,0:T(8,128)(2,1)S(1)} %get-tuple-element.44), channel_id=1, source_target_pairs={{32,0},{64,32},{96,64},{128,96},{160,128},{192,160},{224,192},{33,... | collective-permute-start | bytes 12296 | tf_op jit(solution)/shard_map/ppermute | solution.py:171
  158.4 6.0 %collective-permute-start.4 = (bf16[2,1,32,384]{3,2,1,0:T(8,128)(2,1)S(1)}, bf16[2,1,32,384]{3,2,1,0:T(8,128)(2,1)S(1)}, u32[]{:S(2)}, u32[]{:S(2)}) collective-permute-start(bf16[2,1,32,384]{3,2,1,0:T(8,128)(2,1)S(1)} %get-tuple-element.33), channel_id=1, source_target_pairs={{0,32},{32,64},{64,96},{96,128},{128,160},{160,192},{192,224},{1,3... | collective-permute-start | bytes 147464 | tf_op jit(solution)/shard_map/ppermute | solution.py:169
  160.3 8.1 %collective-permute-start.5 = (bf16[2,1,32,384]{3,2,1,0:T(8,128)(2,1)S(1)}, bf16[2,1,32,384]{3,2,1,0:T(8,128)(2,1)S(1)}, u32[]{:S(2)}, u32[]{:S(2)}) collective-permute-start(bf16[2,1,32,384]{3,2,1,0:T(8,128)(2,1)S(1)} %get-tuple-element.34), channel_id=1, source_target_pairs={{32,0},{64,32},{96,64},{128,96},{160,128},{192,160},{224,192},{33,... | collective-permute-start | bytes 147464 | tf_op jit(solution)/shard_map/ppermute | solution.py:171
  169.2 0.9 copy-start.10

commit v2 on v1

v2 whole, which is shorter than its diff:
```python
import math

import jax
import jax.numpy as jnp
from jax import lax
from jax.experimental import pallas as pl
from jax.experimental.pallas import tpu as pltpu
from jax.sharding import PartitionSpec as P

HEADS = 40
HD = 128
LC = 16
C1 = 384
CO = 192
PW = 16
SEQ = 8
FRM = 32
GROUPS = 5
PARTS = 3
SHARE = 6
STEP = 5
SLOT = 32
LAT = 64
FRAME_Q = SEQ * SHARE
GATHER_F = 4
GATHER_Q = GATHER_F * FRAME_Q
TILE_Q = 256
TILES = FRM * FRAME_Q // TILE_Q
TILE_SPAN = -(-TILE_Q // FRAME_Q) + 1
BLOCK_F = 9
BLOCK_K = BLOCK_F * 128
MAX_BLOCKS = -(-FRM // BLOCK_F)
COEF = math.log2(math.e) / math.sqrt(HD)
FAR = -1e30
MIB = 1024 * 1024


def pack_kernel(q_ref, k_ref, v_ref, w_ref, out_ref):
    low = lax.broadcasted_iota(jnp.int32, (8, HD), 1) < LAT
    for s in range(SEQ):
        cols = slice(s * HD, (s + 1) * HD)
        w = w_ref[cols, :]
        w2 = jnp.concatenate([w, w], axis=1)
        v = jnp.concatenate([v_ref[0, :, cols], v_ref[1, :, cols]], axis=0)
        proj = jnp.dot(v, w2, preferred_element_type=jnp.float32)
        for c in range(2):
            packed = jnp.where(low, proj[c * 8 : c * 8 + 8], proj[16 + c * 8 : 24 + c * 8])
            k = k_ref[c, :, cols]
            q = q_ref[c, :, cols].astype(jnp.float32)
            for part in range(PARTS):
                own = q if part == 0 else pltpu.roll(q, 16 - part * STEP, 0)
                tail = jnp.concatenate([packed, own[:8]], axis=0)
                out_ref[part, c, s, 0:16, :] = k
                out_ref[part, c, s, 16:32, :] = tail.astype(jnp.bfloat16)


def pack(queries, keys, values, w_head):
    span = SEQ * HD
    act = pl.BlockSpec((2, 16, span), lambda i: (0, 0, i))
    return pl.pallas_call(
        pack_kernel,
        grid=(GROUPS,),
        in_specs=[act, act, act, pl.BlockSpec((span, LAT), lambda i: (i, 0))],
        out_specs=pl.BlockSpec((PARTS, 2, SEQ, SLOT, HD), lambda i: (i, 0, 0, 0, 0)),
        out_shape=jax.ShapeDtypeStruct((FRM // 2, 2, SEQ, SLOT, HD), jnp.bfloat16),
        compiler_params=pltpu.CompilerParams(vmem_limit_bytes=32 * MIB),
    )(queries, keys, values, w_head)


def attend_kernel(
    meta_ref, own_ref, other_ref, out_ref, q_ref, vt_ref, s_ref, done_ref, pick_ref, place_ref
):
    core = meta_ref[2 * FRM + 2 * TILES]

    row = lax.broadcasted_iota(jnp.int32, (GATHER_Q, GATHER_F * 128), 0)
    col = lax.broadcasted_iota(jnp.int32, (GATHER_Q, GATHER_F * 128), 1)
    inner = lax.bitwise_and(col, 15) - 8
    hit = (row == SHARE * lax.shift_right_logical(col, 4) + inner) & (inner >= 0) & (inner < SHARE)
    pick_ref[...] = jnp.where(hit, 1.0, 0.0).astype(jnp.bfloat16)
    row = lax.broadcasted_iota(jnp.int32, (GATHER_F * 32, GATHER_F * 24), 0)
    col = lax.broadcasted_iota(jnp.int32, (GATHER_F * 32, GATHER_F * 24), 1)
    inner = lax.bitwise_and(row, 7)
    hit = (col == SHARE * lax.shift_right_logical(row, 3) + inner) & (inner < SHARE)
    place_ref[...] = jnp.where(hit, 1.0, 0.0).astype(jnp.bfloat16)

    def gather(i, carry):
        q = own_ref[pl.ds(i * GATHER_F, GATHER_F), :, 16:32, :].reshape(GATHER_F * 128, HD)
        q = jnp.dot(pick_ref[...], q, preferred_element_type=jnp.float32)
        q_ref[pl.ds(pl.multiple_of(i * GATHER_Q, GATHER_Q), GATHER_Q), :] = q.astype(jnp.bfloat16)
        return carry

    lax.fori_loop(0, FRM // GATHER_F, gather, 0)

    def spread(one, two):
        def body(i, carry):
            top = one[i, :, 16:32, :].astype(jnp.float32)[:, :8]
            bottom = two[i, :, 16:32, :].astype(jnp.float32)[:, :8]
            block = jnp.concatenate([top, bottom], axis=1).reshape(128, HD).T
            ones = jnp.ones((16, HD), jnp.float32)
            for parity in range(2):
                rows = jnp.concatenate([block[parity * LAT : (parity + 1) * LAT], ones], axis=0)
                vt_ref[parity, i] = rows.astype(jnp.bfloat16)
            return carry

        lax.fori_loop(0, FRM, body, 0)

    pl.when(core == 0)(lambda: spread(own_ref, other_ref))
    pl.when(core != 0)(lambda: spread(other_ref, own_ref))

    lane = lax.broadcasted_iota(jnp.int32, (1, TILE_Q), 1)

    def tile(t, carry):
        first = meta_ref[2 * FRM + t]
        last = meta_ref[2 * FRM + TILES + t]
        blocks = lax.div(last - first + (BLOCK_F - 1), BLOCK_F)
        rows = pl.multiple_of(t * TILE_Q, TILE_Q)
        q = q_ref[pl.ds(rows, TILE_Q), :]
        begin_f = lax.div(rows, FRAME_Q)
        q_clip = jnp.zeros((1, TILE_Q), jnp.int32)
        for j in range(TILE_SPAN):
            f = begin_f + j
            q_clip = jnp.where(
                lane + rows >= f * FRAME_Q, meta_ref[jnp.minimum(f, FRM - 1)], q_clip
            )

        def score(b, top):
            begin = first + b * BLOCK_F
            start = jnp.minimum(begin, FRM - BLOCK_F)
            for side, ref in enumerate((own_ref, other_ref)):
                k = ref[pl.ds(start, BLOCK_F), :, 0:16, :].reshape(BLOCK_K, HD)
                s = lax.dot_general(
                    k, q, (((1,), (1,)), ((), ())), preferred_element_type=jnp.float32
                )
                for j in range(BLOCK_F):
                    clip = meta_ref[side * FRM + start + j]
                    clip = jnp.where(start + j >= begin, clip, -1)
                    bias = jnp.where(q_clip == clip, 0.0, FAR)
                    part = s[j * 128 : (j + 1) * 128] + bias
                    s_ref[b, side, j * 128 : (j + 1) * 128, :] = part
                    top = jnp.maximum(top, jnp.max(part.reshape(16, 8, TILE_Q), axis=0))
            return top

        top = lax.fori_loop(0, blocks, score, jnp.full((8, TILE_Q), FAR, jnp.float32))
        top = jnp.max(top, axis=0, keepdims=True)

        def mix(b, total):
            start = jnp.minimum(first + b * BLOCK_F, FRM - BLOCK_F)
            for side in range(2):
                weights = jnp.exp2((s_ref[b, side] - top) * COEF).astype(jnp.bfloat16)
                parity = core if side == 0 else 1 - core
                vt = jnp.concatenate([vt_ref[parity, start + j] for j in range(BLOCK_F)], axis=1)
                total = total + jnp.dot(vt, weights, preferred_element_type=jnp.float32)
            return total

        total = lax.fori_loop(0, blocks, mix, jnp.zeros((LAT + 16, TILE_Q), jnp.float32))
        mixed = total[:LAT] / total[LAT : LAT + 1]
        done_ref[pl.ds(rows, TILE_Q), :] = jnp.concatenate([mixed, mixed], axis=0).T
        return carry

    lax.fori_loop(0, TILES, tile, 0)

    wide_low = lax.broadcasted_iota(jnp.int32, (FRAME_Q, HD), 1) < LAT

    def finish(i, carry):
        ratio = done_ref[pl.ds(pl.multiple_of(i * GATHER_Q, GATHER_Q), GATHER_Q), :]
        packed = []
        for j in range(0, GATHER_F, 2):
            even = ratio[j * FRAME_Q : (j + 1) * FRAME_Q]
            odd = ratio[(j + 1) * FRAME_Q : (j + 2) * FRAME_Q]
            packed.append(jnp.where(wide_low, even, odd))
        packed = jnp.concatenate(packed, axis=0).astype(jnp.bfloat16)
        placed = jnp.dot(place_ref[...], packed, preferred_element_type=jnp.float32)
        placed = placed.astype(jnp.bfloat16).reshape(GATHER_F // 2, SEQ, 8, HD)
        for j in range(GATHER_F // 2):
            for s in range(SEQ):
                for halo in range(3):
                    owner = s + 1 - halo
                    if 0 <= owner < SEQ:
                        out_ref[owner, halo, i * (GATHER_F // 2) + j] = placed[j, s]
        return carry

    lax.fori_loop(0, FRM // GATHER_F, finish, 0)


def attend(meta, own, other):
    vmem = pl.BlockSpec(memory_space=pltpu.VMEM)
    return pl.pallas_call(
        attend_kernel,
        in_specs=[pl.BlockSpec(memory_space=pltpu.SMEM), vmem, vmem],
        out_specs=vmem,
        out_shape=jax.ShapeDtypeStruct((SEQ, 3, FRM // 2, 8, HD), jnp.bfloat16),
        scratch_shapes=[
            pltpu.VMEM((FRM * FRAME_Q, HD), jnp.bfloat16),
            pltpu.VMEM((2, FRM, LAT + 16, HD), jnp.bfloat16),
            pltpu.VMEM((MAX_BLOCKS, 2, BLOCK_K, TILE_Q), jnp.float32),
            pltpu.VMEM((FRM * FRAME_Q, HD), jnp.float32),
            pltpu.VMEM((GATHER_Q, GATHER_F * 128), jnp.bfloat16),
            pltpu.VMEM((GATHER_F * 32, GATHER_F * 24), jnp.bfloat16),
        ],
        compiler_params=pltpu.CompilerParams(vmem_limit_bytes=48 * MIB),
    )(meta, own, other)


def merge_kernel(in_ref, out_ref):
    low = lax.broadcasted_iota(jnp.int32, (FRM // 2, 8, HD), 2) < LAT
    for halo in range(3):
        total = in_ref[0, halo].astype(jnp.float32)
        for head in range(1, SEQ):
            total = total + in_ref[head, halo].astype(jnp.float32)
        before = jnp.concatenate([total[:1], total[:-1]], axis=0)
        out_ref[:, 0, halo] = jnp.where(low, total, before).astype(jnp.bfloat16)
        out_ref[:, 1, halo] = total.astype(jnp.bfloat16)


def merge(parts):
    vmem = pl.BlockSpec(memory_space=pltpu.VMEM)
    return pl.pallas_call(
        merge_kernel,
        in_specs=[vmem],
        out_specs=vmem,
        out_shape=jax.ShapeDtypeStruct((FRM // 2, 2, 3, 8, HD), jnp.bfloat16),
        compiler_params=pltpu.CompilerParams(vmem_limit_bytes=32 * MIB),
    )(parts)


def conv_layer(padded, frame_keep, out_rows, w_in, b_in, gain_in):
    frames = padded.shape[0] - 2
    lat_cols = padded.shape[2] - 2
    tap_list = []
    for time_tap in range(3):
        kept = jnp.where(frame_keep[time_tap], padded[time_tap : time_tap + frames], 0)
        for row_tap in range(3):
            for col_tap in range(3):
                tap_list.append(
                    kept[:, row_tap : row_tap + out_rows, col_tap : col_tap + lat_cols, :]
                )
    columns = jnp.concatenate(tap_list, axis=-1)
    hidden = (
        jnp.dot(columns.reshape(-1, columns.shape[-1]), w_in, preferred_element_type=jnp.float32)
        + b_in
    )
    mean_square = jnp.mean(hidden * hidden, axis=-1, keepdims=True)
    normed = hidden * lax.rsqrt(mean_square + 1e-06) * gain_in
    return jax.nn.silu(normed).astype(jnp.bfloat16).reshape(frames, out_rows, lat_cols, C1)


def shards(queries, keys, values, clip_ids, w_head, b_head, w_in, b_in, gain_in, w_up, b_up):
    frames = 2
    frame_position = lax.axis_index("frm")
    row_position = lax.axis_index("seq")
    first_frame = frame_position * frames
    core = lax.rem(frame_position, 2)

    slots = pack(queries, keys, values, w_head).reshape(FRM * SEQ, SLOT, HD)
    own = lax.all_to_all(slots, ("frm", "seq"), 0, 0, tiled=True)
    other = lax.ppermute(own, "frm", [(i, i ^ 1) for i in range(FRM)])

    pairs = clip_ids.reshape(FRM, 2)
    own_clip = jnp.where(core == 0, pairs[:, 0], pairs[:, 1])
    other_clip = jnp.where(core == 0, pairs[:, 1], pairs[:, 0])
    head_clip = own_clip[jnp.array([t * TILE_Q // FRAME_Q for t in range(TILES)])]
    tail_clip = own_clip[jnp.array([((t + 1) * TILE_Q - 1) // FRAME_Q for t in range(TILES)])]
    below = jnp.sum(clip_ids[None, :] < head_clip[:, None], axis=1, dtype=jnp.int32)
    upto = jnp.sum(clip_ids[None, :] <= tail_clip[:, None], axis=1, dtype=jnp.int32)
    meta = jnp.concatenate([own_clip, other_clip, below // 2, (upto + 1) // 2, core[None]])
    mixed = attend(
        meta, own.reshape(FRM, SEQ, SLOT, HD), other.reshape(FRM, SEQ, SLOT, HD)
    ).reshape(SEQ, -1, HD)
    by_row = lax.all_to_all(mixed, "seq", 0, 0, tiled=True)
    merged = merge(by_row.reshape(SEQ, 3, FRM // 2, 8, HD)).reshape(FRM, 24, HD)
    back = lax.all_to_all(merged, "frm", 0, 0, tiled=True)

    back = back[: 2 * PARTS * GROUPS].reshape(GROUPS, PARTS, 2, 3, 8, 2, LAT)
    summed = jnp.sum(back.astype(jnp.float32), axis=0)
    summed = jnp.concatenate([summed[0, :, :, :6], summed[1, :, :, 1:6], summed[2, :, :, 1:6]], axis=2)
    halves = (summed[:, :, :, 0], summed[:, :, :, 1])
    stacked = jnp.concatenate(
        [jnp.where(core == 0, halves[1], halves[0]), jnp.where(core == 0, halves[0], halves[1])],
        axis=0,
    )
    latent = (stacked + b_head).astype(jnp.bfloat16)
    inside = row_position + jnp.arange(3) - 1
    inside = (inside >= 0) & (inside < SEQ)
    latent = jnp.where(inside[None, :, None, None], latent, 0)
    lat_cols = 2 * PW
    grid = (
        latent.reshape(2 * frames, 3, PW, 2, 2, LC)
        .transpose(0, 1, 3, 2, 4, 5)
        .reshape(2 * frames, 6, lat_cols, LC)
    )
    own_frames_clip = lax.dynamic_slice_in_dim(clip_ids, first_frame, frames, 0)
    clip_padded = jnp.concatenate([jnp.full((2,), -1, jnp.int32), clip_ids])
    frame_keep = []
    for time_tap in range(3):
        earlier_clip = lax.dynamic_slice_in_dim(clip_padded, first_frame + time_tap, frames, 0)
        frame_keep.append((earlier_clip == own_frames_clip)[:, None, None, None])
    padded = jnp.pad(grid, ((0, 0), (0, 0), (1, 1), (0, 0)))
    border = conv_layer(padded, frame_keep, 4, w_in, b_in, gain_in)
    seen = 2 * row_position + jnp.arange(4) - 1
    seen = (seen >= 0) & (seen < 2 * SEQ)
    border = jnp.where(seen[None, :, None, None], border, 0)
    middle = jnp.repeat(border[:, 1:-1], 2, axis=1)
    upsampled = jnp.concatenate([border[:, :1], middle, border[:, -1:]], axis=1)
    upsampled = jnp.repeat(upsampled, 2, axis=2)
    upsampled = jnp.pad(upsampled, ((0, 0), (0, 0), (1, 1), (0, 0)))
    up_rows = 4
    up_cols = 2 * lat_cols
    tap_list = []
    for row_tap in range(3):
        for col_tap in range(3):
            tap_list.append(
                upsampled[:, row_tap : row_tap + up_rows, col_tap : col_tap + up_cols, :]
            )
    columns = jnp.concatenate(tap_list, axis=-1)
    result = jnp.dot(columns.reshape(-1, 9 * C1), w_up, preferred_element_type=jnp.float32) + b_up
    return result.astype(jnp.bfloat16).reshape(frames, up_rows, up_cols * CO)


def solution(mesh):
    in_specs = (
        P("frm", "seq", None),
        P("frm", "seq", None),
        P("frm", "seq", None),
        P(),
        P(),
        P(),
        P(),
        P(),
        P(),
        P(),
        P(),
    )
    out_specs = P("frm", "seq", None)
    return jax.shard_map(shards, mesh=mesh, in_specs=in_specs, out_specs=out_specs, check_vma=False)
```

time: 173 us -> 145 us (0.84)
  the two profiles are of different devices: /device:TPU:26 before, /device:TPU:1 now
where the time goes in v2:
time: 145 us; the launch traced here: 144 us
  blocking collectives  84.2 us (58%)
  Pallas kernels  22.9 us (16%)
  waiting for transfers between devices  13.7 us (9%)
  local copies, waits for them, and re-layouts  12.4 us (9%)
  starting transfers between devices  6.56 us (5%)
  other arithmetic  2.18 us (2%)
  matrix products  1.69 us (1%)
    all_to_all x1, blocking collectives, shards(): own = lax.all_to_all(slots, ('frm', 'seq'), 0, 0, tiled=True)  70.1 us
    pallas_call x1, Pallas kernels, attend(): pl.pallas_call(attend_kernel, in_specs=[pl.BlockSpec(memory_space=pltpu.S...  20.2 us
    all_to_all x1, blocking collectives, shards(): by_row = lax.all_to_all(mixed, 'seq', 0, 0, tiled=True)  14 us
    all_to_all x1, waiting for transfers between devices, shards(): back = lax.all_to_all(merged, 'frm', 0, 0, tiled=True)  11.7 us
    all_to_all x1, starting transfers between devices, shards(): back = lax.all_to_all(merged, 'frm', 0, 0, tiled=True)  5.59 us
    unnamed x33, local copies, waits for them, and re-layouts  5.54 us
  transfers between devices with their start and end apart: 2, of which 2 were waited for; matrix products, arithmetic and copies ran while one was open for 1% of the time, Pallas kernels for 0%

profile of v2, /device:TPU:1, one launch (start us, length us, event | category | flops | bytes accessed | tf_op | source)
XLA Modules:
  0.0 144.0 jit_solution(9171897771616856320)
XLA Ops:
  0.0 1.8 %copy.23.w_ref = bf16[5120,64]{1,0:T(8,128)(2,1)S(1)} copy(bf16[5120,64]{0,1:T(8,128)(2,1)} %param.17) | data formatting | bytes 1310720 | tf_op args[4]
  1.8 1.0 copy-done.1
  2.7 1.0 copy-done.2
  3.7 1.0 copy-done.3
  4.7 1.9 %shard_map.127 = bf16[16,2,8,32,128]{4,3,2,1,0:T(8,128)(2,1)S(1)} custom-call(bf16[2,16,5120]{2,1,0:T(8,128)(2,1)S(1)} %copy-done.1, bf16[2,16,5120]{2,1,0:T(8,128)(2,1)S(1)} %copy-done.2, bf16[2,16,5120]{2,1,0:T(8,128)(2,1)S(1)} %copy-done.3, bf16[5120,64]{1,0:T(8,128)(2,1)S(1)} %copy.23.w_ref), custom_call_target="tpu_custom_call" | custom-call | tf_op jit(solution)/shard_map/pallas_call | solution.py:60
  6.6 70.1 %all_to_all.15 = bf16[256,32,128]{2,1,0:T(8,128)(2,1)S(1)} all-to-all(bf16[256,32,128]{2,1,0:T(8,128)(2,1)S(1)} %bitcast.29), channel_id=1, replica_groups=mesh['seq'=8,'frm'=32] {'frm','seq'}, dimensions={0} | all-to-all | bytes 4194304 | tf_op jit(solution)/shard_map/all_to_all | solution.py:255
  76.7 1.0 collective-permute-start
  77.7 0.1 reshape.96
  77.8 0.2 select_reduce_fusion
  78.0 0.6 gather_fusion.1
  78.7 0.6 gather_fusion
  79.3 0.2 convert_reduce_fusion
  79.6 0.1 concatenate.23.meta_ref
  79.6 2.0 %collective-permute-done = bf16[256,32,128]{2,1,0:T(8,128)(2,1)} collective-permute-done((bf16[256,32,128]{2,1,0:T(8,128)(2,1)S(1)}, bf16[256,32,128]{2,1,0:T(8,128)(2,1)}, u32[]{:S(2)}, u32[]{:S(2)}) %collective-permute-start) | collective-permute-done | bytes 2097184 | tf_op jit(solution)/shard_map/ppermute | solution.py:256
  81.6 20.2 %shard_map.128 = bf16[8,3,16,8,128]{4,3,2,1,0:T(8,128)(2,1)S(1)} custom-call(s32[77]{0:T(128)S(1)} %concatenate.23.meta_ref, bf16[32,8,32,128]{3,2,1,0:T(8,128)(2,1)S(1)} %bitcast.28, bf16[32,8,32,128]{3,2,1,0:T(8,128)(2,1)} %bitcast.3.other_ref), custom_call_target="tpu_custom_call" | custom-call | tf_op jit(solution)/shard_map/pallas_call | solution.py:187
  101.9 14.0 %all_to_all.16 = bf16[8,384,128]{2,1,0:T(8,128)(2,1)S(1)} all-to-all(bf16[8,384,128]{2,1,0:T(8,128)(2,1)S(1)} %bitcast.30), channel_id=1, replica_groups=mesh['seq'=8,'frm'=32] {'seq'}, dimensions={0} | all-to-all | bytes 1572864 | tf_op jit(solution)/shard_map/all_to_all | solution.py:269
  115.9 0.8 shard_map.129
  116.7 5.6 %all-to-all-start.2 = ((bf16[32,24,128]{2,1,0:T(8,128)(2,1)}), bf16[32,24,128]{2,1,0:T(8,128)(2,1)S(1)}, u32[]{:S(2)}, u32[]{:S(2)}) async-start(bf16[32,24,128]{2,1,0:T(8,128)(2,1)} %bitcast.6), calls=%async_computation.2 | async-start | bytes 393216 | tf_op jit(solution)/shard_map/all_to_all | solution.py:271
  122.3 0.1 add.120
  122.4 0.1 dynamic-slice_compare_fusion
  122.5 11.7 %all-to-all-done.2 = bf16[32,24,128]{2,1,0:T(8,128)(2,1)S(1)} async-done(((bf16[32,24,128]{2,1,0:T(8,128)(2,1)}), bf16[32,24,128]{2,1,0:T(8,128)(2,1)S(1)}, u32[]{:S(2)}, u32[]{:S(2)}) %all-to-all-start.2) | async-done | bytes 196640 | tf_op jit(solution)/shard_map/all_to_all | solution.py:271
  134.3 0.4 reshape.110
  134.7 0.5 reduce_sum.38
  135.3 0.3 fusion.12
  135.6 0.2 select_n.96
  135.8 0.2 select_n.98
  136.0 0.3 fusion.8
  136.4 0.2 copy.24
  136.5 0.2 fusion.11
  136.7 0.1 fusion.15
  136.8 0.1 fusion.16
  136.9 0.7 fusion.17
  137.6 1.5 %concatenate.26 = bf16[2,4,32,432]{3,2,1,0:T(8,128)(2,1)S(1)} concatenate(bf16[2,4,32,16]{3,2,1,0:T(8,128)(2,1)} %get-tuple-element.44, bf16[2,4,32,16]{3,2,1,0:T(8,128)(2,1)} %get-tuple-element.43, bf16[2,4,32,16]{3,2,1,0:T(8,128)(2,1)} %get-tuple-element.42, bf16[2,4,32,16]{3,2,1,0:T(8,128)(2,1)S(1)} %get-tuple-element.41, bf16[2,4,32,16]{3,2,1,0:T(8,128)(2,1)S(1)} %get-tuple-element.40, ...), dimensions={3} | concatenate | bytes 442368 | tf_op jit(solution)/shard_map/concatenate | solution.py:237
  139.1 0.4 multiply_reduce_fusion
  139.5 0.2 multiply_convert_fusion
  139.7 0.1 broadcast_select_fusion.1
  139.9 0.4 broadcast_in_dim.89
  140.3 0.2 reshape.107
  140.5 0.1 fusion.1
  140.6 0.1 slice_dynamic-update-slice_fusion.2
  140.7 0.1 fusion.2
  140.9 0.1 fusion.3
  141.1 0.1 fusion.4
  141.2 0.1 fusion.5
  141.4 0.1 fusion.6
  141.6 1.3 fusion
  142.9 0.1 copy.25
  143.0 1.0 reshape.109
  (37 shorter events, 0.4 us)
Async XLA Ops:
  0.0 141.6 %copy-start = (bf16[3456,192]{0,1:T(8,128)(2,1)S(1)}, bf16[3456,192]{0,1:T(8,128)(2,1)}, u32[]{:S(2)}) copy-start(bf16[3456,192]{0,1:T(8,128)(2,1)} %param.22) | copy-start | bytes 3981316
  1.8 1.0 copy-start.1
  2.7 1.0 copy-start.2
  3.7 1.0 copy-start.3
  4.7 73.0 %copy-start.5 = (s32[64]{0:T(128)S(1)}, s32[64]{0:T(128)}, u32[]{:S(2)}) copy-start(s32[64]{0:T(128)} %param.16) | copy-start | bytes 772
  4.7 73.1 %copy-start.9 = (s32[6]{0:T(128)S(1)}, s32[6]{0:T(128)}, u32[]{:S(2)}) copy-start(s32[6]{0:T(128)} %constant.94) | copy-start | bytes 76
  4.7 73.1 %copy-start.10 = (s32[6]{0:T(128)S(1)}, s32[6]{0:T(128)}, u32[]{:S(2)}) copy-start(s32[6]{0:T(128)} %constant.93) | copy-start | bytes 76
  76.7 4.9 %collective-permute-start = (bf16[256,32,128]{2,1,0:T(8,128)(2,1)S(1)}, bf16[256,32,128]{2,1,0:T(8,128)(2,1)}, u32[]{:S(2)}, u32[]{:S(2)}) collective-permute-start(bf16[256,32,128]{2,1,0:T(8,128)(2,1)S(1)} %all_to_all.15), channel_id=1, source_target_pairs={{0,1},{1,0},{2,3},{3,2},{4,5},{5,4},{6,7},{7,6},{8,9},{9,8},{10,11... | collective-permute-start | bytes 6291464 | tf_op jit(solution)/shard_map/ppermute | solution.py:256
  81.6 40.7 %copy-start.8 = (f32[64]{0:T(128)S(1)}, f32[64]{0:T(128)}, u32[]{:S(2)}) copy-start(f32[64]{0:T(128)} %param.18) | copy-start | bytes 772
  116.7 17.5 %all-to-all-start.2 = ((bf16[32,24,128]{2,1,0:T(8,128)(2,1)}), bf16[32,24,128]{2,1,0:T(8,128)(2,1)S(1)}, u32[]{:S(2)}, u32[]{:S(2)}) async-start(bf16[32,24,128]{2,1,0:T(8,128)(2,1)} %bitcast.6), calls=%async_computation.2 | async-start | bytes 393216 | tf_op jit(solution)/shard_map/all_to_all | solution.py:271
  136.0 3.1 %copy-start.4 = (bf16[432,384]{1,0:T(8,128)(2,1)S(1)}, bf16[432,384]{1,0:T(8,128)(2,1)}, u32[]{:S(2)}) copy-start(bf16[432,384]{1,0:T(8,128)(2,1)} %param.19) | copy-start | bytes 995332
  136.0 3.1 %copy-start.6 = (f32[384]{0:T(512)S(1)}, f32[384]{0:T(512)}, u32[]{:S(2)}) copy-start(f32[384]{0:T(512)} %param.20) | copy-start | bytes 4612
  136.5 3.0 %copy-start.7 = (f32[384]{0:T(512)S(1)}, f32[384]{0:T(512)}, u32[]{:S(2)}) copy-start(f32[384]{0:T(512)} %param.21) | copy-start | bytes 4612
  140.6 0.9 copy-start.11

commit v3 on v2

v3 whole, which is shorter than its diff:
```python
import math

import jax
import jax.numpy as jnp
import numpy as np
from jax import lax
from jax.experimental import pallas as pl
from jax.experimental.pallas import tpu as pltpu
from jax.sharding import PartitionSpec as P

HEADS = 40
HD = 128
LC = 16
C1 = 384
CO = 192
SEQ = 8
FRM = 32
GROUPS = 5
PARTS = 3
SHARE = 6
STEP = 5
SLOT = 32
LAT = 64
SPAN = SEQ * HD
FRAME_Q = SEQ * SHARE
GATHER_F = 4
GATHER_Q = GATHER_F * FRAME_Q
TILE_Q = 256
TILES = FRM * FRAME_Q // TILE_Q
TILE_SPAN = -(-TILE_Q // FRAME_Q) + 1
BLOCK_F = 9
BLOCK_K = BLOCK_F * 128
MAX_BLOCKS = -(-FRM // BLOCK_F)
COEF = math.log2(math.e) / math.sqrt(HD)
FAR = -1e30
MIB = 1024 * 1024
NT = (((1,), (1,)), ((), ()))


def pack_kernel(q_hbm, k_hbm, v_hbm, w_hbm, out_ref, q_ref, k_ref, v_ref, w_ref, sems):
    copies = []
    for g in range(GROUPS):
        cols = slice(g * SPAN, (g + 1) * SPAN)
        group = []
        for i, (src, dst) in enumerate(
            ((v_hbm, v_ref), (k_hbm, k_ref), (q_hbm, q_ref), (w_hbm, w_ref))
        ):
            where = (slice(None), cols) if i == 3 else (slice(None), slice(None), cols)
            copy = pltpu.make_async_copy(src.at[where], dst.at[where], sems.at[g, i])
            copy.start()
            group.append(copy)
        copies.append(group)
    low = lax.broadcasted_iota(jnp.int32, (8, HD), 1) < LAT
    for g in range(GROUPS):
        for copy in copies[g]:
            copy.wait()
        for s in range(SEQ):
            cols = slice(g * SPAN + s * HD, g * SPAN + (s + 1) * HD)
            w = w_ref[:, cols]
            w2 = jnp.concatenate([w, w], axis=0)
            v = jnp.concatenate([v_ref[0, :, cols], v_ref[1, :, cols]], axis=0)
            proj = lax.dot_general(v, w2, NT, preferred_element_type=jnp.float32)
            keys = [k_ref[p, :, cols].astype(jnp.float32) for p in range(2)]
            for c in range(2):
                half = slice(c * 8, c * 8 + 8)
                k = jnp.concatenate([keys[0][half], keys[1][half]], axis=0).astype(jnp.bfloat16)
                packed = jnp.where(low, proj[c * 8 : c * 8 + 8], proj[16 + c * 8 : 24 + c * 8])
                q = q_ref[c, :, cols].astype(jnp.float32)
                for part in range(PARTS):
                    own = q if part == 0 else pltpu.roll(q, 16 - part * STEP, 0)
                    tail = jnp.concatenate([packed, own[:8]], axis=0)
                    out_ref[g * PARTS + part, c, s, 0:16, :] = k
                    out_ref[g * PARTS + part, c, s, 16:32, :] = tail.astype(jnp.bfloat16)


def pack(queries, keys, values, w_head):
    hbm = pl.BlockSpec(memory_space=pltpu.HBM)
    act = pltpu.VMEM((2, 16, HEADS * HD), jnp.bfloat16)
    return pl.pallas_call(
        pack_kernel,
        in_specs=[hbm, hbm, hbm, hbm],
        out_specs=pl.BlockSpec(memory_space=pltpu.VMEM),
        out_shape=pltpu.VMEM((FRM // 2, 2, SEQ, SLOT, HD), jnp.bfloat16),
        scratch_shapes=[
            act,
            act,
            act,
            pltpu.VMEM((LAT, HEADS * HD), jnp.bfloat16),
            pltpu.SemaphoreType.DMA((GROUPS, 4)),
        ],
        compiler_params=pltpu.CompilerParams(vmem_limit_bytes=12 * MIB),
    )(*(pltpu.with_memory_space_constraint(x, pltpu.HBM) for x in (queries, keys, values, w_head.T)))


def prepare_kernel(in_ref, kv_ref, q_ref, pick_ref):
    row = lax.broadcasted_iota(jnp.int32, (2 * FRAME_Q, 256), 0)
    col = lax.broadcasted_iota(jnp.int32, (2 * FRAME_Q, 256), 1)
    inner = lax.bitwise_and(col, 15) - 8
    hit = (row == SHARE * lax.shift_right_logical(col, 4) + inner) & (inner >= 0) & (inner < SHARE)
    pick_ref[...] = jnp.where(hit, 1.0, 0.0).astype(jnp.bfloat16)

    def body(i, carry):
        for j in range(2):
            f = 2 * i + j
            kv_ref[f, 0:128, :] = in_ref[f, :, 0:16, :].reshape(128, HD)
            packed = in_ref[f, :, 16:32, :].astype(jnp.float32)[:, :8]
            rolled = pltpu.roll(packed.reshape(SEQ * 8, HD), LAT, 1).reshape(SEQ, 8, HD)
            block = jnp.concatenate([packed, rolled], axis=1).reshape(128, HD).T
            kv_ref[f, 128:192, :] = block[:LAT].astype(jnp.bfloat16)
        q = in_ref[pl.ds(2 * i, 2), :, 16:32, :].reshape(256, HD)
        q = jnp.dot(pick_ref[...], q, preferred_element_type=jnp.float32)
        rows = pl.multiple_of(i * 2 * FRAME_Q, 2 * FRAME_Q)
        q_ref[pl.ds(rows, 2 * FRAME_Q), :] = q.astype(jnp.bfloat16)
        return carry

    lax.fori_loop(0, FRM // 2, body, 0)


def prepare(own):
    vmem = pl.BlockSpec(memory_space=pltpu.VMEM)
    return pl.pallas_call(
        prepare_kernel,
        in_specs=[vmem],
        out_specs=[vmem, vmem],
        out_shape=[
            pltpu.VMEM((FRM, 128 + LAT, HD), jnp.bfloat16),
            pltpu.VMEM((FRM * FRAME_Q, HD), jnp.bfloat16),
        ],
        scratch_shapes=[pltpu.VMEM((2 * FRAME_Q, 256), jnp.bfloat16)],
        compiler_params=pltpu.CompilerParams(vmem_limit_bytes=12 * MIB),
    )(own)


def attend_kernel(meta_ref, q_ref, own_ref, other_ref, out_ref, s_ref, done_ref, place_ref):
    core = meta_ref[3, 0]
    row = lax.broadcasted_iota(jnp.int32, (GATHER_F * 32, GATHER_F * 24), 0)
    col = lax.broadcasted_iota(jnp.int32, (GATHER_F * 32, GATHER_F * 24), 1)
    inner = lax.bitwise_and(row, 7)
    hit = (col == SHARE * lax.shift_right_logical(row, 3) + inner) & (inner < SHARE)
    place_ref[...] = jnp.where(hit, 1.0, 0.0).astype(jnp.bfloat16)
    ones = jnp.ones((16, BLOCK_K), jnp.bfloat16)
    lane = lax.broadcasted_iota(jnp.int32, (8, TILE_Q), 1)

    def tile(t, carry):
        rows = pl.multiple_of(t * TILE_Q, TILE_Q)
        q = q_ref[pl.ds(rows, TILE_Q), :]
        begin_f = lax.div(rows, FRAME_Q)
        end_f = lax.div(rows + (TILE_Q - 1), FRAME_Q)
        first = lax.shift_right_logical(meta_ref[1, 2 * begin_f + core], 1)
        last = lax.shift_right_logical(meta_ref[2, 2 * end_f + core] + 1, 1)
        blocks = lax.div(last - first + (BLOCK_F - 1), BLOCK_F)
        q_clip = jnp.zeros((8, TILE_Q), jnp.int32)
        for j in range(TILE_SPAN):
            f = begin_f + j
            clip = meta_ref[0, jnp.minimum(2 * f + core, 2 * FRM - 1)]
            q_clip = jnp.where(lane + rows >= f * FRAME_Q, clip, q_clip)

        def score(b, top):
            begin = first + b * BLOCK_F
            start = jnp.minimum(begin, FRM - BLOCK_F)
            biases = []
            for j in range(BLOCK_F):
                pair = []
                for p in range(2):
                    clip = meta_ref[0, 2 * (start + j) + p]
                    clip = jnp.where(start + j >= begin, clip, -1)
                    pair.append(jnp.where(q_clip == clip, 0.0, FAR))
                biases.append(jnp.concatenate(pair, axis=0)[None])
            for side, ref in enumerate((own_ref, other_ref)):
                k = ref[pl.ds(start, BLOCK_F), 0:128, :].reshape(BLOCK_K, HD)
                s = lax.dot_general(k, q, NT, preferred_element_type=jnp.float32)
                for j in range(BLOCK_F):
                    part = s[j * 128 : (j + 1) * 128].reshape(SEQ, 16, TILE_Q) + biases[j]
                    s_ref[b, side, j * 128 : (j + 1) * 128, :] = part.reshape(128, TILE_Q)
                    top = jnp.maximum(top, jnp.max(part.reshape(16, 8, TILE_Q), axis=0))
            return top

        top = lax.fori_loop(0, blocks, score, jnp.full((8, TILE_Q), FAR, jnp.float32))
        top = jnp.max(top, axis=0, keepdims=True)

        def mix(b, total):
            start = jnp.minimum(first + b * BLOCK_F, FRM - BLOCK_F)
            for side, ref in enumerate((own_ref, other_ref)):
                weights = jnp.exp2((s_ref[b, side] - top) * COEF).astype(jnp.bfloat16)
                vt = [ref[start + j, 128 : 128 + LAT, :] for j in range(BLOCK_F)]
                vt = jnp.concatenate([jnp.concatenate(vt, axis=1), ones], axis=0)
                total = total + jnp.dot(vt, weights, preferred_element_type=jnp.float32)
            return total

        total = lax.fori_loop(0, blocks, mix, jnp.zeros((LAT + 16, TILE_Q), jnp.float32))
        mixed = total[:LAT] / total[LAT : LAT + 1]
        done_ref[pl.ds(rows, TILE_Q), :] = jnp.concatenate([mixed, mixed], axis=0).T
        return carry

    lax.fori_loop(0, TILES, tile, 0)

    wide_low = lax.broadcasted_iota(jnp.int32, (FRAME_Q, HD), 1) < LAT

    def finish(i, carry):
        ratio = done_ref[pl.ds(pl.multiple_of(i * GATHER_Q, GATHER_Q), GATHER_Q), :]
        packed = []
        for j in range(0, GATHER_F, 2):
            even = ratio[j * FRAME_Q : (j + 1) * FRAME_Q]
            odd = ratio[(j + 1) * FRAME_Q : (j + 2) * FRAME_Q]
            packed.append(jnp.where(wide_low, even, odd))
        packed = jnp.concatenate(packed, axis=0).astype(jnp.bfloat16)
        placed = jnp.dot(place_ref[...], packed, preferred_element_type=jnp.float32)
        placed = placed.astype(jnp.bfloat16).reshape(GATHER_F // 2, SEQ, 8, HD)
        for j in range(GATHER_F // 2):
            for s in range(SEQ):
                for halo in range(3):
                    owner = s + 1 - halo
                    if 0 <= owner < SEQ:
                        out_ref[owner, halo, i * (GATHER_F // 2) + j] = placed[j, s]
        return carry

    lax.fori_loop(0, FRM // GATHER_F, finish, 0)


def attend(meta, q, own, other):
    vmem = pl.BlockSpec(memory_space=pltpu.VMEM)
    return pl.pallas_call(
        attend_kernel,
        in_specs=[pl.BlockSpec(memory_space=pltpu.SMEM), vmem, vmem, vmem],
        out_specs=vmem,
        out_shape=pltpu.VMEM((SEQ, 3, FRM // 2, 8, HD), jnp.bfloat16),
        scratch_shapes=[
            pltpu.VMEM((MAX_BLOCKS, 2, BLOCK_K, TILE_Q), jnp.float32),
            pltpu.VMEM((FRM * FRAME_Q, HD), jnp.float32),
            pltpu.VMEM((GATHER_F * 32, GATHER_F * 24), jnp.bfloat16),
        ],
        compiler_params=pltpu.CompilerParams(vmem_limit_bytes=24 * MIB),
    )(meta, q, own, other)


def merge_kernel(in_ref, out_ref):
    low = lax.broadcasted_iota(jnp.int32, (FRM // 2, 8, HD), 2) < LAT
    for halo in range(3):
        total = in_ref[0, halo].astype(jnp.float32)
        for head in range(1, SEQ):
            total = total + in_ref[head, halo].astype(jnp.float32)
        before = jnp.concatenate([total[:1], total[:-1]], axis=0)
        out_ref[:, 0, halo] = jnp.where(low, total, before).astype(jnp.bfloat16)
        out_ref[:, 1, halo] = total.astype(jnp.bfloat16)


def merge(parts):
    vmem = pl.BlockSpec(memory_space=pltpu.VMEM)
    return pl.pallas_call(
        merge_kernel,
        in_specs=[vmem],
        out_specs=vmem,
        out_shape=pltpu.VMEM((FRM // 2, 2, 3, 8, HD), jnp.bfloat16),
        compiler_params=pltpu.CompilerParams(vmem_limit_bytes=12 * MIB),
    )(parts)


def assembly():
    out = np.zeros((3, 2, 3, 16, PARTS, 2, 3, 8), np.float32)
    for near in range(3):
        for token in range(16):
            source = token + near - 1
            if 0 <= source < 16:
                part = min(max(source - 1, 0) // STEP, PARTS - 1)
                for c in range(2):
                    for h in range(3):
                        out[near, c, h, token, part, c, h, source - part * STEP] = 1
    return out.reshape(3 * 96, 144)


def spreading():
    out = np.zeros((3, 2, 2, 2, LC, 2, 2, 2, 128), np.float32)
    for parity in range(2):
        for tap in range(3):
            column = parity + tap - 1
            near, b = 1 + column // 2, column % 2
            for pair in range(2):
                for a in range(2):
                    for ch in range(LC):
                        out[near, pair, a, b, ch, pair, a, parity, tap * LC + ch] = 1
    return out.reshape(3 * HD, 8 * 128)


def reordering():
    out = np.zeros((3, 16, 2, 2, 4, 2, 2, 4, 16), np.float32)
    for tap in range(3):
        for row in range(4):
            source = (row + tap + 1) // 2
            for frame in range(2):
                for parity in range(2):
                    for column in range(16):
                        out[tap, column, parity, frame, row, frame, parity, source, column] = 1
    return out.reshape(3, 256, 256)


def decode_kernel(
    clip_ref, place_ref, in_ref, gather_ref, spread_ref, order_ref, b_head_ref, w_in_ref, b_in_ref,
    gain_ref, w_up_ref, b_up_ref, out_ref,
):
    first_frame = 2 * place_ref[0]
    core = lax.rem(place_ref[0], 2)
    no_above = place_ref[1] == 0
    no_below = place_ref[1] == SEQ - 1
    total = in_ref[0].astype(jnp.float32)
    for g in range(1, GROUPS):
        total = total + in_ref[g].astype(jnp.float32)
    total = total + b_head_ref[...]
    total = total.reshape(144, HD)
    total = jnp.where(core == 0, pltpu.roll(total, LAT, 1), total)
    row = lax.broadcasted_iota(jnp.int32, (144, HD), 0)
    patch = lax.rem(lax.shift_right_logical(row, 3), 3)
    outside = ((patch == 0) & no_above) | ((patch == 2) & no_below)
    tokens = jnp.where(outside, 0.0, total).astype(jnp.bfloat16)
    tokens = jnp.dot(gather_ref[...], tokens, preferred_element_type=jnp.float32)
    tokens = tokens.astype(jnp.bfloat16)
    near = jnp.concatenate([tokens[i * 96 : (i + 1) * 96] for i in range(3)], axis=1)
    cells = jnp.dot(near, spread_ref[...], preferred_element_type=jnp.float32).astype(jnp.bfloat16)

    hidden = jnp.zeros((256, C1), jnp.float32)
    for time_tap in (2, 1, 0):
        part = jnp.zeros((256, C1), jnp.float32)
        for row_tap in range(3):
            pieces = []
            for f in range(2):
                pair, c = divmod(f + time_tap, 2)
                for parity in range(2):
                    for r in range(4):
                        h, a = divmod(r + row_tap, 2)
                        e = (pair * 2 + a) * 2 + parity
                        rows = slice((c * 3 + h) * 16, (c * 3 + h + 1) * 16)
                        pieces.append(cells[rows, e * 128 : e * 128 + 3 * LC])
            columns = jnp.concatenate(pieces, axis=0)
            tap = (time_tap * 3 + row_tap) * 3 * LC
            part = part + jnp.dot(
                columns, w_in_ref[tap : tap + 3 * LC, :], preferred_element_type=jnp.float32
            )
        if time_tap == 2:
            hidden = part + b_in_ref[...]
        else:
            kept = []
            for f in range(2):
                earlier = first_frame + (f + time_tap - 2)
                same = clip_ref[jnp.maximum(earlier, 0)] == clip_ref[first_frame + f]
                keep = (earlier >= 0) & same
                kept.append(jnp.where(keep, part[f * 128 : (f + 1) * 128], 0.0))
            hidden = hidden + jnp.concatenate(kept, axis=0)
    mean_square = jnp.mean(hidden * hidden, axis=-1, keepdims=True)
    normed = hidden * lax.rsqrt(mean_square + 1e-06) * gain_ref[...]
    active = normed / (1.0 + jnp.exp(-normed))
    row = lax.broadcasted_iota(jnp.int32, (256, C1), 0)
    grid_row = lax.bitwise_and(lax.shift_right_logical(row, 4), 3)
    outside = ((grid_row == 0) & no_above) | ((grid_row == 3) & no_below)
    active = jnp.where(outside, 0.0, active).astype(jnp.bfloat16)

    taps = [jnp.zeros((256, CO), jnp.float32) for _ in range(3)]
    for row_tap in range(3):
        placed = jnp.dot(order_ref[row_tap], active, preferred_element_type=jnp.float32)
        placed = placed.astype(jnp.bfloat16)
        for col_tap in range(3):
            tap = (row_tap * 3 + col_tap) * C1
            taps[col_tap] = taps[col_tap] + lax.dot_general(
                placed, w_up_ref[:, tap : tap + C1], NT, preferred_element_type=jnp.float32
            )
    edge = jnp.zeros((8, CO), jnp.float32)
    before = jnp.concatenate([edge, taps[0][:-8]], axis=0)
    after = jnp.concatenate([taps[2][8:], edge], axis=0)
    even = before + taps[1] + taps[2] + b_up_ref[...]
    odd = taps[0] + taps[1] + after + b_up_ref[...]
    both = jnp.concatenate([even, odd], axis=1).astype(jnp.bfloat16).astype(jnp.float32)
    for column in range(32):
        piece = both[column * 8 : column * 8 + 8]
        lanes = slice(column * 2 * CO, (column + 1) * 2 * CO)
        out_ref[0, :, lanes] = piece[:4].astype(jnp.bfloat16)
        out_ref[1, :, lanes] = piece[4:].astype(jnp.bfloat16)


def decode(clip_ids, place, back, b_head, w_in, b_in, gain_in, w_up, b_up):
    vmem = pl.BlockSpec(memory_space=pltpu.VMEM)
    constants = [jnp.asarray(x, jnp.bfloat16) for x in (assembly(), spreading(), reordering())]
    return pl.pallas_call(
        decode_kernel,
        in_specs=[pl.BlockSpec(memory_space=pltpu.SMEM)] * 2 + [vmem] * 10,
        out_specs=vmem,
        out_shape=jax.ShapeDtypeStruct((2, 4, 64 * CO), jnp.bfloat16),
        compiler_params=pltpu.CompilerParams(vmem_limit_bytes=12 * MIB),
    )(
        clip_ids,
        place,
        back,
        *constants,
        jnp.concatenate([b_head, b_head])[None],
        w_in,
        b_in[None],
        gain_in[None],
        w_up.T,
        b_up[None],
    )


def shards(queries, keys, values, clip_ids, w_head, b_head, w_in, b_in, gain_in, w_up, b_up):
    frame_position = lax.axis_index("frm")
    row_position = lax.axis_index("seq")
    core = lax.rem(frame_position, 2)

    slots = pack(queries, keys, values, w_head).reshape(FRM * SEQ, SLOT, HD)
    own = lax.all_to_all(slots, ("frm", "seq"), 0, 0, tiled=True)
    own_kv, own_q = prepare(own.reshape(FRM, SEQ, SLOT, HD))
    other_kv = lax.ppermute(own_kv, "frm", [(i, i ^ 1) for i in range(FRM)])

    below = jnp.sum(clip_ids[None, :] < clip_ids[:, None], axis=1, dtype=jnp.int32)
    upto = jnp.sum(clip_ids[None, :] <= clip_ids[:, None], axis=1, dtype=jnp.int32)
    kind = lax.broadcasted_iota(jnp.int32, (4, 2 * FRM), 0)
    meta = jnp.where(kind == 0, clip_ids, jnp.where(kind == 1, below, jnp.where(kind == 2, upto, core)))
    mixed = attend(meta, own_q, own_kv, other_kv).reshape(SEQ, -1, HD)
    by_row = lax.all_to_all(mixed, "seq", 0, 0, tiled=True)
    merged = merge(by_row.reshape(SEQ, 3, FRM // 2, 8, HD)).reshape(FRM, 24, HD)
    back = lax.all_to_all(merged, "frm", 0, 0, tiled=True)

    back = back[: 2 * PARTS * GROUPS].reshape(GROUPS, 2 * PARTS, 24, HD)
    place = jnp.where(jnp.arange(2) == 0, frame_position, row_position)
    return decode(clip_ids, place, back, b_head, w_in, b_in, gain_in, w_up, b_up)


def solution(mesh):
    in_specs = (
        P("frm", "seq", None),
        P("frm", "seq", None),
        P("frm", "seq", None),
        P(),
        P(),
        P(),
        P(),
        P(),
        P(),
        P(),
        P(),
    )
    out_specs = P("frm", "seq", None)
    return jax.shard_map(shards, mesh=mesh, in_specs=in_specs, out_specs=out_specs, check_vma=False)
```

time: 145 us -> 129 us (0.89)
  local copies, waits for them, and re-layouts: 12.4 us -> 0.09 us
  Pallas kernels: 22.9 us -> 24.9 us
  starting transfers between devices: 6.56 us -> 4.7 us
  other arithmetic: 2.18 us -> 0.34 us
  matrix products: 1.69 us -> 0 us
    pallas_call x2 -> x4, Pallas kernels: 2.68 us -> 9.74 us  [the longest x1 3.84 us: decode(): pl.pallas_call(decode_kernel, in_specs=[pl.BlockSpec(memory_space=pltpu.S...]
    unnamed x33 -> x20, local copies, waits for them, and re-layouts: 5.54 us -> 0.06 us
    pallas_call x1, Pallas kernels: 20.2 us -> 15.2 us  [attend(): pl.pallas_call(attend_kernel, in_specs=[pl.BlockSpec(memory_space=pltpu.S...]
    all_to_all x1, starting transfers between devices: 5.59 us -> 3.65 us  [shards(): back = lax.all_to_all(merged, 'frm', 0, 0, tiled=True)]
    dot_general x2 -> x0, matrix products: 1.69 us -> none  [the longest x1 1.31 us: shards(): jnp.dot(columns.reshape(-1, 9 * C1), w_up, preferred_element_type=jnp.flo...]
    concatenate x3 -> x0, local copies, waits for them, and re-layouts: 1.69 us -> none  [the longest x1 1.47 us: conv_layer(): columns = jnp.concatenate(tap_list, axis=-1)]
  transfers between devices with their start and end apart: 2 -> 2, of which waited for: 2 -> 2; matrix products, arithmetic and copies ran while one was open for 1% -> 0% of each run, Pallas kernels for 0% -> 0%
where the time goes in v3:
time: 129 us
  blocking collectives  84.8 us (66%)
  Pallas kernels  24.9 us (19%)
  waiting for transfers between devices  13.8 us (11%)
  starting transfers between devices  4.7 us (4%)
    all_to_all x1, blocking collectives, shards(): own = lax.all_to_all(slots, ('frm', 'seq'), 0, 0, tiled=True)  70.1 us
    pallas_call x1, Pallas kernels, attend(): pl.pallas_call(attend_kernel, in_specs=[pl.BlockSpec(memory_space=pltpu.S...  15.2 us
    all_to_all x1, blocking collectives, shards(): by_row = lax.all_to_all(mixed, 'seq', 0, 0, tiled=True)  14.7 us
    all_to_all x1, waiting for transfers between devices, shards(): back = lax.all_to_all(merged, 'frm', 0, 0, tiled=True)  11 us
    pallas_call x1, Pallas kernels, decode(): pl.pallas_call(decode_kernel, in_specs=[pl.BlockSpec(memory_space=pltpu.S...  3.84 us
    all_to_all x1, starting transfers between devices, shards(): back = lax.all_to_all(merged, 'frm', 0, 0, tiled=True)  3.65 us
    ppermute x1, waiting for transfers between devices, shards(): other_kv = lax.ppermute(own_kv, 'frm', [(i, i ^ 1) for i in range(FRM)])  2.76 us
  transfers between devices with their start and end apart: 2, of which 2 were waited for; matrix products, arithmetic and copies ran while one was open for 0% of the time, Pallas kernels for 0%

profile of v3, /device:TPU:1, one launch (start us, length us, event | category | flops | bytes accessed | tf_op | source)
XLA Modules:
  0.0 128.9 jit_solution(7196938227128145068)
XLA Ops:
  0.0 2.6 %shard_map.136 = bf16[16,2,8,32,128]{4,3,2,1,0:T(8,128)(2,1)S(1)} custom-call(bf16[2,16,5120]{2,1,0:T(8,128)(2,1)} %q_hbm.1, bf16[2,16,5120]{2,1,0:T(8,128)(2,1)} %k_hbm.1, bf16[2,16,5120]{2,1,0:T(8,128)(2,1)} %v_hbm.1, bf16[64,5120]{1,0:T(8,128)(2,1)} %bitcast.18), custom_call_target="tpu_custom_call" | custom-call | tf_op jit(solution)/shard_map/pallas_call | solution.py:79
  2.6 70.1 %all_to_all.15 = bf16[256,32,128]{2,1,0:T(8,128)(2,1)S(1)} all-to-all(bf16[256,32,128]{2,1,0:T(8,128)(2,1)S(1)} %bitcast.11), channel_id=1, replica_groups=mesh['seq'=8,'frm'=32] {'frm','seq'}, dimensions={0} | all-to-all | bytes 4194304 | tf_op jit(solution)/shard_map/all_to_all | solution.py:406
  72.7 0.0 copy-start.5
  72.7 2.5 %shard_map.137 = (bf16[32,192,128]{2,1,0:T(8,128)(2,1)S(1)}, bf16[1536,128]{1,0:T(8,128)(2,1)S(1)}) custom-call(bf16[32,8,32,128]{3,2,1,0:T(8,128)(2,1)S(1)} %bitcast.12), custom_call_target="tpu_custom_call" | custom-call | tf_op jit(solution)/shard_map/pallas_call | solution.py:121
  75.3 1.1 collective-permute-start
  76.3 0.0 copy-done.5
  76.3 0.2 convert_reduce_fusion.1
  76.5 0.1 select_select_fusion.meta_ref
  76.6 2.8 %collective-permute-done.other_ref = bf16[32,192,128]{2,1,0:T(8,128)(2,1)S(1)} collective-permute-done((bf16[32,192,128]{2,1,0:T(8,128)(2,1)S(1)}, bf16[32,192,128]{2,1,0:T(8,128)(2,1)S(1)}, u32[]{:S(2)}, u32[]{:S(2)}) %collective-permute-start) | collective-permute-done | bytes 1572896 | tf_op jit(solution)/shard_map/ppermute | solution.py:408
  79.4 15.2 %shard_map.138 = bf16[8,3,16,8,128]{4,3,2,1,0:T(8,128)(2,1)S(1)} custom-call(s32[4,64]{1,0:T(4,128)S(1)} %select_select_fusion.meta_ref, bf16[1536,128]{1,0:T(8,128)(2,1)S(1)} %get-tuple-element.7.q_ref, bf16[32,192,128]{2,1,0:T(8,128)(2,1)S(1)} %get-tuple-element.8.own_ref, bf16[32,192,128]{2,1,0:T(8,128)(2,1)S(1)} %collective-permute-done.other_ref), custom_call_target="tpu_custom_call" | custom-call | tf_op jit(solution)/shard_map/pallas_call | solution.py:222
  94.6 0.0 copy-start.7
  94.6 0.0 copy-start.8
  94.6 0.0 copy-start.9
  94.6 0.0 copy-start
  94.6 0.0 copy-start.1
  94.6 0.0 copy-start.2
  94.6 0.0 copy-start.3
  94.6 0.0 copy-start.4
  94.7 0.0 copy-start.6
  94.7 14.7 %all_to_all.16 = bf16[8,384,128]{2,1,0:T(8,128)(2,1)S(1)} all-to-all(bf16[8,384,128]{2,1,0:T(8,128)(2,1)S(1)} %bitcast.14), channel_id=1, replica_groups=mesh['seq'=8,'frm'=32] {'seq'}, dimensions={0} | all-to-all | bytes 1572864 | tf_op jit(solution)/shard_map/all_to_all | solution.py:415
  109.3 0.8 shard_map.139
  110.1 3.7 %all-to-all-start.2 = ((bf16[32,24,128]{2,1,0:T(8,128)(2,1)}), bf16[32,24,128]{2,1,0:T(8,128)(2,1)S(1)}, u32[]{:S(2)}, u32[]{:S(2)}) async-start(bf16[32,24,128]{2,1,0:T(8,128)(2,1)} %bitcast.5), calls=%async_computation.2 | async-start | bytes 393216 | tf_op jit(solution)/shard_map/all_to_all | solution.py:417
  113.8 0.0 copy-done.7
  113.8 0.0 copy-done.8
  113.9 0.0 copy-done.9
  113.9 0.1 maximum_bitcast_fusion.b_head_ref
  113.9 11.0 %all-to-all-done.2 = bf16[32,24,128]{2,1,0:T(8,128)(2,1)S(1)} async-done(((bf16[32,24,128]{2,1,0:T(8,128)(2,1)}), bf16[32,24,128]{2,1,0:T(8,128)(2,1)S(1)}, u32[]{:S(2)}, u32[]{:S(2)}) %all-to-all-start.2) | async-done | bytes 196640 | tf_op jit(solution)/shard_map/all_to_all | solution.py:417
  125.0 0.0 copy-done
  125.0 0.0 copy-done.1
  125.0 0.0 copy-done.2
  125.0 0.0 copy-done.3
  125.1 0.0 copy-done.4
  125.1 0.0 copy-done.6
  125.1 3.8 %shard_map.140 = bf16[2,4,12288]{2,1,0:T(4,128)(2,1)} custom-call(s32[64]{0:T(128)S(1)} %copy-done.5, s32[2]{0:T(128)S(1)} %compare_select_fusion.place_ref, bf16[5,6,24,128]{3,2,1,0:T(8,128)(2,1)S(1)} %bitcast.16, bf16[288,144]{1,0:T(8,128)(2,1)S(1)} %copy-done.4, bf16[384,1024]{1,0:T(8,128)(2,1)S(1)} %copy-done.1, bf16[3,256,256]{2,1,0:T(8,128)(2,1)S(1)} %copy-done.2, ...), custom_call_target="tpu_custom_call" | custom-call | tf_op jit(solution)/shard_map/pallas_call | solution.py:380
  (6 shorter events, 0.0 us)
Async XLA Ops:
  72.7 3.6 %copy-start.5 = (s32[64]{0:T(128)S(1)}, s32[64]{0:T(128)}, u32[]{:S(2)}) copy-start(s32[64]{0:T(128)} %clip_ref.1) | copy-start | bytes 772
  75.3 4.1 %collective-permute-start = (bf16[32,192,128]{2,1,0:T(8,128)(2,1)S(1)}, bf16[32,192,128]{2,1,0:T(8,128)(2,1)S(1)}, u32[]{:S(2)}, u32[]{:S(2)}) collective-permute-start(bf16[32,192,128]{2,1,0:T(8,128)(2,1)S(1)} %get-tuple-element.8.own_ref), channel_id=1, source_target_pairs={{0,1},{1,0},{2,3},{3,2},{4,5},{5,4},{6,7},{7,6},{8,9},{9,8},{10,11... | collective-permute-start | bytes 4718600 | tf_op jit(solution)/shard_map/ppermute | solution.py:408
  94.6 19.2 %copy-start.7 = (f32[384]{0:T(512)S(1)}, f32[384]{0:T(512)}, u32[]{:S(2)}) copy-start(f32[384]{0:T(512)} %param.21) | copy-start | bytes 4612
  94.6 19.3 %copy-start.8 = (f32[384]{0:T(512)S(1)}, f32[384]{0:T(512)}, u32[]{:S(2)}) copy-start(f32[384]{0:T(512)} %param.22) | copy-start | bytes 4612
  94.6 19.3 %copy-start.9 = (f32[64]{0:T(128)S(1)}, f32[64]{0:T(128)}, u32[]{:S(2)}) copy-start(f32[64]{0:T(128)} %param.19) | copy-start | bytes 772
  94.6 30.4 %copy-start = (bf16[3456,192]{0,1:T(8,128)(2,1)S(1)}, bf16[3456,192]{0,1:T(8,128)(2,1)}, u32[]{:S(2)}) copy-start(bf16[3456,192]{0,1:T(8,128)(2,1)} %param.23) | copy-start | bytes 3981316
  94.6 30.4 %copy-start.1 = (bf16[384,1024]{1,0:T(8,128)(2,1)S(1)}, bf16[384,1024]{1,0:T(8,128)(2,1)}, u32[]{:S(2)}) copy-start(bf16[384,1024]{1,0:T(8,128)(2,1)} %constant.27.clone.spread_ref) | copy-start | bytes 2359300
  94.6 30.4 %copy-start.2 = (bf16[3,256,256]{2,1,0:T(8,128)(2,1)S(1)}, bf16[3,256,256]{2,1,0:T(8,128)(2,1)}, u32[]{:S(2)}) copy-start(bf16[3,256,256]{2,1,0:T(8,128)(2,1)} %constant.28.clone.order_ref) | copy-start | bytes 1179652
  94.6 30.4 %copy-start.3 = (bf16[432,384]{1,0:T(8,128)(2,1)S(1)}, bf16[432,384]{1,0:T(8,128)(2,1)}, u32[]{:S(2)}) copy-start(bf16[432,384]{1,0:T(8,128)(2,1)} %w_in_ref.1) | copy-start | bytes 995332
  94.6 30.4 %copy-start.4 = (bf16[288,144]{1,0:T(8,128)(2,1)S(1)}, bf16[288,144]{1,0:T(8,128)(2,1)}, u32[]{:S(2)}) copy-start(bf16[288,144]{1,0:T(8,128)(2,1)} %constant.26.clone.gather_ref) | copy-start | bytes 248836
  94.7 30.4 %copy-start.6 = (f32[192]{0:T(256)S(1)}, f32[192]{0:T(256)}, u32[]{:S(2)}) copy-start(f32[192]{0:T(256)} %param.24) | copy-start | bytes 2308
  110.1 14.9 %all-to-all-start.2 = ((bf16[32,24,128]{2,1,0:T(8,128)(2,1)}), bf16[32,24,128]{2,1,0:T(8,128)(2,1)S(1)}, u32[]{:S(2)}, u32[]{:S(2)}) async-start(bf16[32,24,128]{2,1,0:T(8,128)(2,1)} %bitcast.5), calls=%async_computation.2 | async-start | bytes 393216 | tf_op jit(solution)/shard_map/all_to_all | solution.py:417

commit v4 on v3

--- a/solution.py
+++ b/solution.py
@@ -23,12 +23,13 @@
 LAT = 64
 SPAN = SEQ * HD
 FRAME_Q = SEQ * SHARE
-GATHER_F = 4
-GATHER_Q = GATHER_F * FRAME_Q
+GATHER_F = 8
+GATHER_R = GATHER_F // 2 * SHARE
 TILE_Q = 256
 TILES = FRM * FRAME_Q // TILE_Q
 TILE_SPAN = -(-TILE_Q // FRAME_Q) + 1
-BLOCK_F = 9
+BLOCK_F = 17
+GROUP = 2
 BLOCK_K = BLOCK_F * 128
 MAX_BLOCKS = -(-FRM // BLOCK_F)
 COEF = math.log2(math.e) / math.sqrt(HD)
@@ -113,7 +114,7 @@
         q_ref[pl.ds(rows, 2 * FRAME_Q), :] = q.astype(jnp.bfloat16)
         return carry
 
-    lax.fori_loop(0, FRM // 2, body, 0)
+    lax.fori_loop(0, FRM // 2, body, 0, unroll=16)
 
 
 def prepare(own):
@@ -133,15 +134,20 @@
 
 def attend_kernel(meta_ref, q_ref, own_ref, other_ref, out_ref, s_ref, done_ref, place_ref):
     core = meta_ref[3, 0]
-    row = lax.broadcasted_iota(jnp.int32, (GATHER_F * 32, GATHER_F * 24), 0)
-    col = lax.broadcasted_iota(jnp.int32, (GATHER_F * 32, GATHER_F * 24), 1)
-    inner = lax.bitwise_and(row, 7)
-    hit = (col == SHARE * lax.shift_right_logical(row, 3) + inner) & (inner < SHARE)
-    place_ref[...] = jnp.where(hit, 1.0, 0.0).astype(jnp.bfloat16)
+    share = lax.broadcasted_iota(jnp.int32, (SEQ * GATHER_R, 1), 0)
+    source = jnp.zeros_like(share)
+    for size, unit, stop in ((GATHER_R, SHARE, SEQ), (SHARE, FRAME_Q, GATHER_F // 2)):
+        count = jnp.zeros_like(share)
+        for i in range(1, stop):
+            count = count + jnp.where(share >= size * i, 1, 0)
+        share = share - count * size
+        source = source + count * unit
+    col = lax.broadcasted_iota(jnp.int32, (SEQ * GATHER_R, SEQ * GATHER_R), 1)
+    place_ref[...] = jnp.where(col == source + share, 1.0, 0.0).astype(jnp.bfloat16)
     ones = jnp.ones((16, BLOCK_K), jnp.bfloat16)
     lane = lax.broadcasted_iota(jnp.int32, (8, TILE_Q), 1)
 
-    def tile(t, carry):
+    def setup(t):
         rows = pl.multiple_of(t * TILE_Q, TILE_Q)
         q = q_ref[pl.ds(rows, TILE_Q), :]
         begin_f = lax.div(rows, FRAME_Q)
@@ -154,67 +160,98 @@
             f = begin_f + j
             clip = meta_ref[0, jnp.minimum(2 * f + core, 2 * FRM - 1)]
             q_clip = jnp.where(lane + rows >= f * FRAME_Q, clip, q_clip)
-
-        def score(b, top):
-            begin = first + b * BLOCK_F
-            start = jnp.minimum(begin, FRM - BLOCK_F)
-            biases = []
+        return rows, q, q_clip, first, blocks
+
+    def score(b, q, q_clip, first, buffer, top):
+        begin = first + b * BLOCK_F
+        start = jnp.minimum(begin, FRM - BLOCK_F)
+        biases = []
+        for j in range(BLOCK_F):
+            pair = []
+            for p in range(2):
+                clip = meta_ref[0, 2 * (start + j) + p]
+                clip = jnp.where(start + j >= begin, clip, -1)
+                pair.append(jnp.where(q_clip == clip, 0.0, FAR))
+            biases.append(jnp.concatenate(pair, axis=0)[None])
+        for side, ref in enumerate((own_ref, other_ref)):
+            k = ref[pl.ds(start, BLOCK_F), 0:128, :].reshape(BLOCK_K, HD)
+            s = lax.dot_general(k, q, NT, preferred_element_type=jnp.float32)
             for j in range(BLOCK_F):
-                pair = []
-                for p in range(2):
-                    clip = meta_ref[0, 2 * (start + j) + p]
-                    clip = jnp.where(start + j >= begin, clip, -1)
-                    pair.append(jnp.where(q_clip == clip, 0.0, FAR))
-                biases.append(jnp.concatenate(pair, axis=0)[None])
-            for side, ref in enumerate((own_ref, other_ref)):
-                k = ref[pl.ds(start, BLOCK_F), 0:128, :].reshape(BLOCK_K, HD)
-                s = lax.dot_general(k, q, NT, preferred_element_type=jnp.float32)
-                for j in range(BLOCK_F):
-                    part = s[j * 128 : (j + 1) * 128].reshape(SEQ, 16, TILE_Q) + biases[j]
-                    s_ref[b, side, j * 128 : (j + 1) * 128, :] = part.reshape(128, TILE_Q)
-                    top = jnp.maximum(top, jnp.max(part.reshape(16, 8, TILE_Q), axis=0))
-            return top
-
-        top = lax.fori_loop(0, blocks, score, jnp.full((8, TILE_Q), FAR, jnp.float32))
-        top = jnp.max(top, axis=0, keepdims=True)
-
-        def mix(b, total):
-            start = jnp.minimum(first + b * BLOCK_F, FRM - BLOCK_F)
-            for side, ref in enumerate((own_ref, other_ref)):
-                weights = jnp.exp2((s_ref[b, side] - top) * COEF).astype(jnp.bfloat16)
-                vt = [ref[start + j, 128 : 128 + LAT, :] for j in range(BLOCK_F)]
-                vt = jnp.concatenate([jnp.concatenate(vt, axis=1), ones], axis=0)
-                total = total + jnp.dot(vt, weights, preferred_element_type=jnp.float32)
-            return total
-
-        total = lax.fori_loop(0, blocks, mix, jnp.zeros((LAT + 16, TILE_Q), jnp.float32))
+                part = s[j * 128 : (j + 1) * 128].reshape(SEQ, 16, TILE_Q) + biases[j]
+                buffer[side, j * 128 : (j + 1) * 128, :] = part.reshape(128, TILE_Q)
+                top = jnp.maximum(top, jnp.max(part.reshape(16, 8, TILE_Q), axis=0))
+        return top
+
+    def mix(b, first, top, buffer, total):
+        start = jnp.minimum(first + b * BLOCK_F, FRM - BLOCK_F)
+        for side, ref in enumerate((own_ref, other_ref)):
+            weights = jnp.exp2((buffer[side] - top) * COEF).astype(jnp.bfloat16)
+            vt = [ref[start + j, 128 : 128 + LAT, :] for j in range(BLOCK_F)]
+            vt = jnp.concatenate([jnp.concatenate(vt, axis=1), ones], axis=0)
+            total = total + jnp.dot(vt, weights, preferred_element_type=jnp.float32)
+        return total
+
+    def store(rows, total):
         mixed = total[:LAT] / total[LAT : LAT + 1]
         done_ref[pl.ds(rows, TILE_Q), :] = jnp.concatenate([mixed, mixed], axis=0).T
+
+    none = jnp.full((8, TILE_Q), FAR, jnp.float32)
+    zero = jnp.zeros((LAT + 16, TILE_Q), jnp.float32)
+
+    def pair(i, carry):
+        tiles = [setup(GROUP * i + n) for n in range(GROUP)]
+        one = tiles[0][4] == 1
+        for n in range(1, GROUP):
+            one = one & (tiles[n][4] == 1)
+
+        @pl.when(one)
+        def _():
+            tops = []
+            for n, (rows, q, q_clip, first, blocks) in enumerate(tiles):
+                top = score(0, q, q_clip, first, s_ref.at[n], none)
+                tops.append(jnp.max(top, axis=0, keepdims=True))
+            for n, (rows, q, q_clip, first, blocks) in enumerate(tiles):
+                store(rows, mix(0, first, tops[n], s_ref.at[n], zero))
+
+        @pl.when(jnp.logical_not(one))
+        def _():
+            def single(n, carry):
+                rows, q, q_clip, first, blocks = setup(GROUP * i + n)
+                top = lax.fori_loop(
+                    0, blocks, lambda b, top: score(b, q, q_clip, first, s_ref.at[b], top), none
+                )
+                top = jnp.max(top, axis=0, keepdims=True)
+                store(
+                    rows,
+                    lax.fori_loop(
+                        0, blocks, lambda b, total: mix(b, first, top, s_ref.at[b], total), zero
+                    ),
+                )
+                return carry
+
+            lax.fori_loop(0, GROUP, single, 0)
+
         return carry
 
-    lax.fori_loop(0, TILES, tile, 0)
+    lax.fori_loop(0, TILES // GROUP, pair, 0)
 
     wide_low = lax.broadcasted_iota(jnp.int32, (FRAME_Q, HD), 1) < LAT
-
-    def finish(i, carry):
-        ratio = done_ref[pl.ds(pl.multiple_of(i * GATHER_Q, GATHER_Q), GATHER_Q), :]
+    for i in range(FRM // GATHER_F):
         packed = []
-        for j in range(0, GATHER_F, 2):
-            even = ratio[j * FRAME_Q : (j + 1) * FRAME_Q]
-            odd = ratio[(j + 1) * FRAME_Q : (j + 2) * FRAME_Q]
-            packed.append(jnp.where(wide_low, even, odd))
+        for j in range(GATHER_F // 2):
+            even = (i * GATHER_F + 2 * j) * FRAME_Q
+            odd = even + FRAME_Q
+            packed.append(
+                jnp.where(wide_low, done_ref[even:odd, :], done_ref[odd : odd + FRAME_Q, :])
+            )
         packed = jnp.concatenate(packed, axis=0).astype(jnp.bfloat16)
         placed = jnp.dot(place_ref[...], packed, preferred_element_type=jnp.float32)
-        placed = placed.astype(jnp.bfloat16).reshape(GATHER_F // 2, SEQ, 8, HD)
-        for j in range(GATHER_F // 2):
-            for s in range(SEQ):
-                for halo in range(3):
-                    owner = s + 1 - halo
-                    if 0 <= owner < SEQ:
-                        out_ref[owner, halo, i * (GATHER_F // 2) + j] = placed[j, s]
-        return carry
-
-    lax.fori_loop(0, FRM // GATHER_F, finish, 0)
+        for s in range(SEQ):
+            piece = placed[s * GATHER_R : (s + 1) * GATHER_R].astype(jnp.bfloat16)
+            for halo in range(3):
+                owner = s + 1 - halo
+                if 0 <= owner < SEQ:
+                    out_ref[owner, halo, i] = piece
 
 
 def attend(meta, q, own, other):
@@ -223,22 +260,25 @@
         attend_kernel,
         in_specs=[pl.BlockSpec(memory_space=pltpu.SMEM), vmem, vmem, vmem],
         out_specs=vmem,
-        out_shape=pltpu.VMEM((SEQ, 3, FRM // 2, 8, HD), jnp.bfloat16),
+        out_shape=pltpu.VMEM((SEQ, 3, FRM // GATHER_F, GATHER_R, HD), jnp.bfloat16),
         scratch_shapes=[
-            pltpu.VMEM((MAX_BLOCKS, 2, BLOCK_K, TILE_Q), jnp.float32),
+            pltpu.VMEM((max(GROUP, MAX_BLOCKS), 2, BLOCK_K, TILE_Q), jnp.float32),
             pltpu.VMEM((FRM * FRAME_Q, HD), jnp.float32),
-            pltpu.VMEM((GATHER_F * 32, GATHER_F * 24), jnp.bfloat16),
+            pltpu.VMEM((SEQ * GATHER_R, SEQ * GATHER_R), jnp.bfloat16),
         ],
         compiler_params=pltpu.CompilerParams(vmem_limit_bytes=24 * MIB),
     )(meta, q, own, other)
 
 
-def merge_kernel(in_ref, out_ref):
+def merge_kernel(in_ref, widen_ref, out_ref):
     low = lax.broadcasted_iota(jnp.int32, (FRM // 2, 8, HD), 2) < LAT
     for halo in range(3):
         total = in_ref[0, halo].astype(jnp.float32)
         for head in range(1, SEQ):
             total = total + in_ref[head, halo].astype(jnp.float32)
+        total = total.reshape(FRM // 2 * SHARE, HD).astype(jnp.bfloat16)
+        total = jnp.dot(widen_ref[...], total, preferred_element_type=jnp.float32)
+        total = total.reshape(FRM // 2, 8, HD)
         before = jnp.concatenate([total[:1], total[:-1]], axis=0)
         out_ref[:, 0, halo] = jnp.where(low, total, before).astype(jnp.bfloat16)
         out_ref[:, 1, halo] = total.astype(jnp.bfloat16)
@@ -246,13 +286,18 @@
 
 def merge(parts):
     vmem = pl.BlockSpec(memory_space=pltpu.VMEM)
+    widen = np.zeros((FRM // 2, 8, FRM // 2, SHARE), np.float32)
+    for f in range(FRM // 2):
+        for t in range(SHARE):
+            widen[f, t, f, t] = 1
+    widen = jnp.asarray(widen.reshape(FRM // 2 * 8, FRM // 2 * SHARE), jnp.bfloat16)
     return pl.pallas_call(
         merge_kernel,
-        in_specs=[vmem],
+        in_specs=[vmem, vmem],
         out_specs=vmem,
         out_shape=pltpu.VMEM((FRM // 2, 2, 3, 8, HD), jnp.bfloat16),
         compiler_params=pltpu.CompilerParams(vmem_limit_bytes=12 * MIB),
-    )(parts)
+    )(parts, widen)
 
 
 def assembly():
@@ -294,9 +339,11 @@
 
 
 def decode_kernel(
-    clip_ref, place_ref, in_ref, gather_ref, spread_ref, order_ref, b_head_ref, w_in_ref, b_in_ref,
-    gain_ref, w_up_ref, b_up_ref, out_ref,
+    clip_ref, place_ref, in_ref, gather_ref, spread_ref, order_ref, b_head_ref, w_in_hbm, b_in_ref,
+    gain_ref, w_up_ref, b_up_ref, out_ref, w_in_ref, w_in_sem,
 ):
+    w_in_copy = pltpu.make_async_copy(w_in_hbm, w_in_ref, w_in_sem)
+    w_in_copy.start()
     first_frame = 2 * place_ref[0]
     core = lax.rem(place_ref[0], 2)
     no_above = place_ref[1] == 0
@@ -316,6 +363,7 @@
     near = jnp.concatenate([tokens[i * 96 : (i + 1) * 96] for i in range(3)], axis=1)
     cells = jnp.dot(near, spread_ref[...], preferred_element_type=jnp.float32).astype(jnp.bfloat16)
 
+    w_in_copy.wait()
     hidden = jnp.zeros((256, C1), jnp.float32)
     for time_tap in (2, 1, 0):
         part = jnp.zeros((256, C1), jnp.float32)
@@ -379,9 +427,13 @@
     constants = [jnp.asarray(x, jnp.bfloat16) for x in (assembly(), spreading(), reordering())]
     return pl.pallas_call(
         decode_kernel,
-        in_specs=[pl.BlockSpec(memory_space=pltpu.SMEM)] * 2 + [vmem] * 10,
+        in_specs=[pl.BlockSpec(memory_space=pltpu.SMEM)] * 2
+        + [vmem] * 5
+        + [pl.BlockSpec(memory_space=pltpu.HBM)]
+        + [vmem] * 4,
         out_specs=vmem,
         out_shape=jax.ShapeDtypeStruct((2, 4, 64 * CO), jnp.bfloat16),
+        scratch_shapes=[pltpu.VMEM((27 * LC, C1), jnp.bfloat16), pltpu.SemaphoreType.DMA],
         compiler_params=pltpu.CompilerParams(vmem_limit_bytes=12 * MIB),
     )(
         clip_ids,
@@ -389,7 +441,7 @@
         back,
         *constants,
         jnp.concatenate([b_head, b_head])[None],
-        w_in,
+        pltpu.with_memory_space_constraint(w_in, pltpu.HBM),
         b_in[None],
         gain_in[None],
         w_up.T,
@@ -413,7 +465,7 @@
     meta = jnp.where(kind == 0, clip_ids, jnp.where(kind == 1, below, jnp.where(kind == 2, upto, core)))
     mixed = attend(meta, own_q, own_kv, other_kv).reshape(SEQ, -1, HD)
     by_row = lax.all_to_all(mixed, "seq", 0, 0, tiled=True)
-    merged = merge(by_row.reshape(SEQ, 3, FRM // 2, 8, HD)).reshape(FRM, 24, HD)
+    merged = merge(by_row.reshape(SEQ, 3, FRM // GATHER_F, GATHER_R, HD)).reshape(FRM, 24, HD)
     back = lax.all_to_all(merged, "frm", 0, 0, tiled=True)
 
     back = back[: 2 * PARTS * GROUPS].reshape(GROUPS, 2 * PARTS, 24, HD)

time: 129 us -> 127 us (0.984)
  Pallas kernels: 24.9 us -> 22.5 us
  blocking collectives: 84.8 us -> 83 us
  starting transfers between devices: 4.7 us -> 6.06 us
    all_to_all x1, blocking collectives: 14.7 us -> 12.9 us  [shards(): by_row = lax.all_to_all(mixed, 'seq', 0, 0, tiled=True)]
    pallas_call x1, Pallas kernels: 2.53 us -> 0.81 us  [prepare(): pl.pallas_call(prepare_kernel, in_specs=[vmem], out_specs=[vmem, vmem], o...]
    pallas_call x1, Pallas kernels: 15.2 us -> 13.5 us  [attend(): pl.pallas_call(attend_kernel, in_specs=[pl.BlockSpec(memory_space=pltpu.S...]
    all_to_all x1, starting transfers between devices: 3.65 us -> 5 us  [shards(): back = lax.all_to_all(merged, 'frm', 0, 0, tiled=True)]
where the time goes in v4:
time: 127 us
  blocking collectives  83 us (65%)
  Pallas kernels  22.5 us (18%)
  waiting for transfers between devices  14.5 us (11%)
  starting transfers between devices  6.06 us (5%)
    all_to_all x1, blocking collectives, shards(): own = lax.all_to_all(slots, ('frm', 'seq'), 0, 0, tiled=True)  70.1 us
    pallas_call x1, Pallas kernels, attend(): pl.pallas_call(attend_kernel, in_specs=[pl.BlockSpec(memory_space=pltpu.S...  13.5 us
    all_to_all x1, blocking collectives, shards(): by_row = lax.all_to_all(mixed, 'seq', 0, 0, tiled=True)  12.9 us
    all_to_all x1, waiting for transfers between devices, shards(): back = lax.all_to_all(merged, 'frm', 0, 0, tiled=True)  11.7 us
    all_to_all x1, starting transfers between devices, shards(): back = lax.all_to_all(merged, 'frm', 0, 0, tiled=True)  5 us
    pallas_call x1, Pallas kernels, decode(): pl.pallas_call(decode_kernel, in_specs=[pl.BlockSpec(memory_space=pltpu.S...  4.67 us
    ppermute x1, waiting for transfers between devices, shards(): other_kv = lax.ppermute(own_kv, 'frm', [(i, i ^ 1) for i in range(FRM)])  2.76 us
    pallas_call x1, Pallas kernels, pack(): pl.pallas_call(pack_kernel, in_specs=[hbm, hbm, hbm, hbm], out_specs=pl.B...  2.57 us
  transfers between devices with their start and end apart: 2, of which 2 were waited for; matrix products, arithmetic and copies ran while one was open for 0% of the time, Pallas kernels for 0%

profile of v4, /device:TPU:1, one launch (start us, length us, event | category | flops | bytes accessed | tf_op | source)
XLA Modules:
  0.0 126.7 jit_solution(13178358885952507492)
XLA Ops:
  0.0 2.6 %shard_map.145 = bf16[16,2,8,32,128]{4,3,2,1,0:T(8,128)(2,1)S(1)} custom-call(bf16[2,16,5120]{2,1,0:T(8,128)(2,1)} %q_hbm.1, bf16[2,16,5120]{2,1,0:T(8,128)(2,1)} %k_hbm.1, bf16[2,16,5120]{2,1,0:T(8,128)(2,1)} %v_hbm.1, bf16[64,5120]{1,0:T(8,128)(2,1)} %bitcast.18), custom_call_target="tpu_custom_call" | custom-call | tf_op jit(solution)/shard_map/pallas_call | solution.py:80
  2.6 70.1 %all_to_all.15 = bf16[256,32,128]{2,1,0:T(8,128)(2,1)S(1)} all-to-all(bf16[256,32,128]{2,1,0:T(8,128)(2,1)S(1)} %bitcast.11), channel_id=1, replica_groups=mesh['seq'=8,'frm'=32] {'frm','seq'}, dimensions={0} | all-to-all | bytes 4194304 | tf_op jit(solution)/shard_map/all_to_all | solution.py:458
  72.7 0.0 copy-start.5
  72.7 0.8 shard_map.146
  73.5 1.1 collective-permute-start
  74.6 0.0 copy-done.5
  74.6 0.2 convert_reduce_fusion.1
  74.8 0.1 select_select_fusion.meta_ref
  74.9 2.8 %collective-permute-done.other_ref = bf16[32,192,128]{2,1,0:T(8,128)(2,1)S(1)} collective-permute-done((bf16[32,192,128]{2,1,0:T(8,128)(2,1)S(1)}, bf16[32,192,128]{2,1,0:T(8,128)(2,1)S(1)}, u32[]{:S(2)}, u32[]{:S(2)}) %collective-permute-start) | collective-permute-done | bytes 1572896 | tf_op jit(solution)/shard_map/ppermute | solution.py:460
  77.6 0.0 copy-start.4
  77.6 0.0 copy-start.7
  77.6 0.0 copy-start.8
  77.6 0.0 copy-start.9
  77.6 13.5 %shard_map.147 = bf16[8,3,4,24,128]{4,3,2,1,0:T(8,128)(2,1)S(1)} custom-call(s32[4,64]{1,0:T(4,128)S(1)} %select_select_fusion.meta_ref, bf16[1536,128]{1,0:T(8,128)(2,1)S(1)} %get-tuple-element.7.q_ref, bf16[32,192,128]{2,1,0:T(8,128)(2,1)S(1)} %get-tuple-element.8.own_ref, bf16[32,192,128]{2,1,0:T(8,128)(2,1)S(1)} %collective-permute-done.other_ref), custom_call_target="tpu_custom_call" | custom-call | tf_op jit(solution)/shard_map/pallas_call | solution.py:259
  91.2 0.0 copy-start
  91.2 0.0 copy-start.1
  91.2 0.0 copy-start.2
  91.2 0.0 copy-start.3
  91.2 0.0 copy-start.6
  91.2 12.9 %all_to_all.16 = bf16[8,288,128]{2,1,0:T(8,128)(2,1)S(1)} all-to-all(bf16[8,288,128]{2,1,0:T(8,128)(2,1)S(1)} %bitcast.13), channel_id=1, replica_groups=mesh['seq'=8,'frm'=32] {'seq'}, dimensions={0} | all-to-all | bytes 1179648 | tf_op jit(solution)/shard_map/all_to_all | solution.py:467
  104.1 0.0 copy-done.4
  104.1 0.9 shard_map.148
  105.0 5.0 %all-to-all-start.2 = ((bf16[32,24,128]{2,1,0:T(8,128)(2,1)}), bf16[32,24,128]{2,1,0:T(8,128)(2,1)S(1)}, u32[]{:S(2)}, u32[]{:S(2)}) async-start(bf16[32,24,128]{2,1,0:T(8,128)(2,1)} %bitcast.5), calls=%async_computation.2 | async-start | bytes 393216 | tf_op jit(solution)/shard_map/all_to_all | solution.py:469
  110.0 0.0 copy-done.7
  110.1 0.0 copy-done.8
  110.1 0.0 copy-done.9
  110.1 0.1 maximum_bitcast_fusion.b_head_ref
  110.2 11.7 %all-to-all-done.2 = bf16[32,24,128]{2,1,0:T(8,128)(2,1)S(1)} async-done(((bf16[32,24,128]{2,1,0:T(8,128)(2,1)}), bf16[32,24,128]{2,1,0:T(8,128)(2,1)S(1)}, u32[]{:S(2)}, u32[]{:S(2)}) %all-to-all-start.2) | async-done | bytes 196640 | tf_op jit(solution)/shard_map/all_to_all | solution.py:469
  121.9 0.0 copy-done
  122.0 0.0 copy-done.1
  122.0 0.0 copy-done.2
  122.0 0.0 copy-done.3
  122.0 0.0 copy-done.6
  122.0 4.7 %shard_map.149 = bf16[2,4,12288]{2,1,0:T(4,128)(2,1)} custom-call(s32[64]{0:T(128)S(1)} %copy-done.5, s32[2]{0:T(128)S(1)} %compare_select_fusion.place_ref, bf16[5,6,24,128]{3,2,1,0:T(8,128)(2,1)S(1)} %bitcast.16, bf16[288,144]{1,0:T(8,128)(2,1)S(1)} %copy-done.3, bf16[384,1024]{1,0:T(8,128)(2,1)S(1)} %copy-done.1, bf16[3,256,256]{2,1,0:T(8,128)(2,1)S(1)} %copy-done.2, ...), custom_call_target="tpu_custom_call" | custom-call | tf_op jit(solution)/shard_map/pallas_call | solution.py:428
  (6 shorter events, 0.0 us)
Async XLA Ops:
  72.7 1.9 %copy-start.5 = (s32[64]{0:T(128)S(1)}, s32[64]{0:T(128)}, u32[]{:S(2)}) copy-start(s32[64]{0:T(128)} %clip_ref.1) | copy-start | bytes 772
  73.5 4.1 %collective-permute-start = (bf16[32,192,128]{2,1,0:T(8,128)(2,1)S(1)}, bf16[32,192,128]{2,1,0:T(8,128)(2,1)S(1)}, u32[]{:S(2)}, u32[]{:S(2)}) collective-permute-start(bf16[32,192,128]{2,1,0:T(8,128)(2,1)S(1)} %get-tuple-element.8.own_ref), channel_id=1, source_target_pairs={{0,1},{1,0},{2,3},{3,2},{4,5},{5,4},{6,7},{7,6},{8,9},{9,8},{10,11... | collective-permute-start | bytes 4718600 | tf_op jit(solution)/shard_map/ppermute | solution.py:460
  77.6 26.5 %copy-start.4 = (bf16[128,96]{1,0:T(8,128)(2,1)S(1)}, bf16[128,96]{1,0:T(8,128)(2,1)}, u32[]{:S(2)}) copy-start(bf16[128,96]{1,0:T(8,128)(2,1)} %constant.28.clone.widen_ref) | copy-start | bytes 73732
  77.6 32.4 %copy-start.7 = (f32[384]{0:T(512)S(1)}, f32[384]{0:T(512)}, u32[]{:S(2)}) copy-start(f32[384]{0:T(512)} %param.22) | copy-start | bytes 4612
  77.6 32.4 %copy-start.8 = (f32[384]{0:T(512)S(1)}, f32[384]{0:T(512)}, u32[]{:S(2)}) copy-start(f32[384]{0:T(512)} %param.23) | copy-start | bytes 4612
  77.6 32.5 %copy-start.9 = (f32[64]{0:T(128)S(1)}, f32[64]{0:T(128)}, u32[]{:S(2)}) copy-start(f32[64]{0:T(128)} %param.20) | copy-start | bytes 772
  91.2 30.8 %copy-start = (bf16[3456,192]{0,1:T(8,128)(2,1)S(1)}, bf16[3456,192]{0,1:T(8,128)(2,1)}, u32[]{:S(2)}) copy-start(bf16[3456,192]{0,1:T(8,128)(2,1)} %param.24) | copy-start | bytes 3981316
  91.2 30.8 %copy-start.1 = (bf16[384,1024]{1,0:T(8,128)(2,1)S(1)}, bf16[384,1024]{1,0:T(8,128)(2,1)}, u32[]{:S(2)}) copy-start(bf16[384,1024]{1,0:T(8,128)(2,1)} %constant.30.clone.spread_ref) | copy-start | bytes 2359300
  91.2 30.8 %copy-start.2 = (bf16[3,256,256]{2,1,0:T(8,128)(2,1)S(1)}, bf16[3,256,256]{2,1,0:T(8,128)(2,1)}, u32[]{:S(2)}) copy-start(bf16[3,256,256]{2,1,0:T(8,128)(2,1)} %constant.31.clone.order_ref) | copy-start | bytes 1179652
  91.2 30.8 %copy-start.3 = (bf16[288,144]{1,0:T(8,128)(2,1)S(1)}, bf16[288,144]{1,0:T(8,128)(2,1)}, u32[]{:S(2)}) copy-start(bf16[288,144]{1,0:T(8,128)(2,1)} %constant.29.clone.gather_ref) | copy-start | bytes 248836
  91.2 30.8 %copy-start.6 = (f32[192]{0:T(256)S(1)}, f32[192]{0:T(256)}, u32[]{:S(2)}) copy-start(f32[192]{0:T(256)} %param.25) | copy-start | bytes 2308
  105.0 16.9 %all-to-all-start.2 = ((bf16[32,24,128]{2,1,0:T(8,128)(2,1)}), bf16[32,24,128]{2,1,0:T(8,128)(2,1)S(1)}, u32[]{:S(2)}, u32[]{:S(2)}) async-start(bf16[32,24,128]{2,1,0:T(8,128)(2,1)} %bitcast.5), calls=%async_computation.2 | async-start | bytes 393216 | tf_op jit(solution)/shard_map/all_to_all | solution.py:469

commit v5 on v4

--- a/solution.py
+++ b/solution.py
@@ -1,3 +1,4 @@
+import functools
 import math
 
 import jax
@@ -28,10 +29,8 @@
 TILE_Q = 256
 TILES = FRM * FRAME_Q // TILE_Q
 TILE_SPAN = -(-TILE_Q // FRAME_Q) + 1
-BLOCK_F = 17
+SIZES = (12, 17, 24, 32)
 GROUP = 2
-BLOCK_K = BLOCK_F * 128
-MAX_BLOCKS = -(-FRM // BLOCK_F)
 COEF = math.log2(math.e) / math.sqrt(HD)
 FAR = -1e30
 MIB = 1024 * 1024
@@ -132,8 +131,12 @@
     )(own)
 
 
-def attend_kernel(meta_ref, q_ref, own_ref, other_ref, out_ref, s_ref, done_ref, place_ref):
+def attend_kernel(
+    meta_ref, q_ref, own_ref, other_ref, w_in_hbm, out_ref, w_in_ref, s_ref, done_ref, place_ref, w_in_sem
+):
     core = meta_ref[3, 0]
+    w_in_copy = pltpu.make_async_copy(w_in_hbm, w_in_ref, w_in_sem)
+    w_in_copy.start()
     share = lax.broadcasted_iota(jnp.int32, (SEQ * GATHER_R, 1), 0)
     source = jnp.zeros_like(share)
     for size, unit, stop in ((GATHER_R, SHARE, SEQ), (SHARE, FRAME_Q, GATHER_F // 2)):
@@ -144,7 +147,7 @@
         source = source + count * unit
     col = lax.broadcasted_iota(jnp.int32, (SEQ * GATHER_R, SEQ * GATHER_R), 1)
     place_ref[...] = jnp.where(col == source + share, 1.0, 0.0).astype(jnp.bfloat16)
-    ones = jnp.ones((16, BLOCK_K), jnp.bfloat16)
+    ones = jnp.ones((16, FRM * 128), jnp.bfloat16)
     lane = lax.broadcasted_iota(jnp.int32, (8, TILE_Q), 1)
 
     def setup(t):
@@ -154,40 +157,39 @@
         end_f = lax.div(rows + (TILE_Q - 1), FRAME_Q)
         first = lax.shift_right_logical(meta_ref[1, 2 * begin_f + core], 1)
         last = lax.shift_right_logical(meta_ref[2, 2 * end_f + core] + 1, 1)
-        blocks = lax.div(last - first + (BLOCK_F - 1), BLOCK_F)
         q_clip = jnp.zeros((8, TILE_Q), jnp.int32)
         for j in range(TILE_SPAN):
             f = begin_f + j
             clip = meta_ref[0, jnp.minimum(2 * f + core, 2 * FRM - 1)]
             q_clip = jnp.where(lane + rows >= f * FRAME_Q, clip, q_clip)
-        return rows, q, q_clip, first, blocks
-
-    def score(b, q, q_clip, first, buffer, top):
-        begin = first + b * BLOCK_F
-        start = jnp.minimum(begin, FRM - BLOCK_F)
+        return rows, q, q_clip, first, last - first
+
+    def score(size, q, q_clip, first, buffer):
+        start = jnp.minimum(first, FRM - size)
+        top = jnp.full((8, TILE_Q), FAR, jnp.float32)
         biases = []
-        for j in range(BLOCK_F):
+        for j in range(size):
             pair = []
             for p in range(2):
                 clip = meta_ref[0, 2 * (start + j) + p]
-                clip = jnp.where(start + j >= begin, clip, -1)
                 pair.append(jnp.where(q_clip == clip, 0.0, FAR))
             biases.append(jnp.concatenate(pair, axis=0)[None])
         for side, ref in enumerate((own_ref, other_ref)):
-            k = ref[pl.ds(start, BLOCK_F), 0:128, :].reshape(BLOCK_K, HD)
+            k = ref[pl.ds(start, size), 0:128, :].reshape(size * 128, HD)
             s = lax.dot_general(k, q, NT, preferred_element_type=jnp.float32)
-            for j in range(BLOCK_F):
+            for j in range(size):
                 part = s[j * 128 : (j + 1) * 128].reshape(SEQ, 16, TILE_Q) + biases[j]
                 buffer[side, j * 128 : (j + 1) * 128, :] = part.reshape(128, TILE_Q)
                 top = jnp.maximum(top, jnp.max(part.reshape(16, 8, TILE_Q), axis=0))
         return top
 
-    def mix(b, first, top, buffer, total):
-        start = jnp.minimum(first + b * BLOCK_F, FRM - BLOCK_F)
+    def mix(size, first, top, buffer):
+        start = jnp.minimum(first, FRM - size)
+        total = jnp.zeros((LAT + 16, TILE_Q), jnp.float32)
         for side, ref in enumerate((own_ref, other_ref)):
-            weights = jnp.exp2((buffer[side] - top) * COEF).astype(jnp.bfloat16)
-            vt = [ref[start + j, 128 : 128 + LAT, :] for j in range(BLOCK_F)]
-            vt = jnp.concatenate([jnp.concatenate(vt, axis=1), ones], axis=0)
+            weights = jnp.exp2((buffer[side, : size * 128] - top) * COEF).astype(jnp.bfloat16)
+            vt = [ref[start + j, 128 : 128 + LAT, :] for j in range(size)]
+            vt = jnp.concatenate([jnp.concatenate(vt, axis=1), ones[:, : size * 128]], axis=0)
             total = total + jnp.dot(vt, weights, preferred_element_type=jnp.float32)
         return total
 
@@ -195,42 +197,23 @@
         mixed = total[:LAT] / total[LAT : LAT + 1]
         done_ref[pl.ds(rows, TILE_Q), :] = jnp.concatenate([mixed, mixed], axis=0).T
 
-    none = jnp.full((8, TILE_Q), FAR, jnp.float32)
-    zero = jnp.zeros((LAT + 16, TILE_Q), jnp.float32)
-
     def pair(i, carry):
         tiles = [setup(GROUP * i + n) for n in range(GROUP)]
-        one = tiles[0][4] == 1
+        widest = tiles[0][4]
         for n in range(1, GROUP):
-            one = one & (tiles[n][4] == 1)
-
-        @pl.when(one)
-        def _():
+            widest = jnp.maximum(widest, tiles[n][4])
+
+        def together(size):
             tops = []
-            for n, (rows, q, q_clip, first, blocks) in enumerate(tiles):
-                top = score(0, q, q_clip, first, s_ref.at[n], none)
+            for n, (rows, q, q_clip, first, span) in enumerate(tiles):
+                top = score(size, q, q_clip, first, s_ref.at[n])
                 tops.append(jnp.max(top, axis=0, keepdims=True))
-            for n, (rows, q, q_clip, first, blocks) in enumerate(tiles):
-                store(rows, mix(0, first, tops[n], s_ref.at[n], zero))
-
-        @pl.when(jnp.logical_not(one))
-        def _():
-            def single(n, carry):
-                rows, q, q_clip, first, blocks = setup(GROUP * i + n)
-                top = lax.fori_loop(
-                    0, blocks, lambda b, top: score(b, q, q_clip, first, s_ref.at[b], top), none
-                )
-                top = jnp.max(top, axis=0, keepdims=True)
-                store(
-                    rows,
-                    lax.fori_loop(
-                        0, blocks, lambda b, total: mix(b, first, top, s_ref.at[b], total), zero
-                    ),
-                )
-                return carry
-
-            lax.fori_loop(0, GROUP, single, 0)
-
+            for n, (rows, q, q_clip, first, span) in enumerate(tiles):
+                store(rows, mix(size, first, tops[n], s_ref.at[n]))
+
+        for below, size in zip((0,) + SIZES, SIZES):
+            fits = (widest > below) & (widest <= size)
+            pl.when(fits)(functools.partial(together, size))
         return carry
 
     lax.fori_loop(0, TILES // GROUP, pair, 0)
@@ -252,22 +235,33 @@
                 owner = s + 1 - halo
                 if 0 <= owner < SEQ:
                     out_ref[owner, halo, i] = piece
-
-
-def attend(meta, q, own, other):
+    w_in_copy.wait()
+
+
+def attend(meta, q, own, other, w_in):
     vmem = pl.BlockSpec(memory_space=pltpu.VMEM)
     return pl.pallas_call(
         attend_kernel,
-        in_specs=[pl.BlockSpec(memory_space=pltpu.SMEM), vmem, vmem, vmem],
-        out_specs=vmem,
-        out_shape=pltpu.VMEM((SEQ, 3, FRM // GATHER_F, GATHER_R, HD), jnp.bfloat16),
+        in_specs=[
+            pl.BlockSpec(memory_space=pltpu.SMEM),
+            vmem,
+            vmem,
+            vmem,
+            pl.BlockSpec(memory_space=pltpu.HBM),
+        ],
+        out_specs=[vmem, vmem],
+        out_shape=[
+            pltpu.VMEM((SEQ, 3, FRM // GATHER_F, GATHER_R, HD), jnp.bfloat16),
+            pltpu.VMEM(w_in.shape, jnp.bfloat16),
+        ],
         scratch_shapes=[
-            pltpu.VMEM((max(GROUP, MAX_BLOCKS), 2, BLOCK_K, TILE_Q), jnp.float32),
+            pltpu.VMEM((GROUP, 2, FRM * 128, TILE_Q), jnp.float32),
             pltpu.VMEM((FRM * FRAME_Q, HD), jnp.float32),
             pltpu.VMEM((SEQ * GATHER_R, SEQ * GATHER_R), jnp.bfloat16),
+            pltpu.SemaphoreType.DMA,
         ],
-        compiler_params=pltpu.CompilerParams(vmem_limit_bytes=24 * MIB),
-    )(meta, q, own, other)
+        compiler_params=pltpu.CompilerParams(vmem_limit_bytes=36 * MIB),
+    )(meta, q, own, other, pltpu.with_memory_space_constraint(w_in, pltpu.HBM))
 
 
 def merge_kernel(in_ref, widen_ref, out_ref):
@@ -339,11 +333,9 @@
 
 
 def decode_kernel(
-    clip_ref, place_ref, in_ref, gather_ref, spread_ref, order_ref, b_head_ref, w_in_hbm, b_in_ref,
-    gain_ref, w_up_ref, b_up_ref, out_ref, w_in_ref, w_in_sem,
+    clip_ref, place_ref, in_ref, gather_ref, spread_ref, order_ref, b_head_ref, w_in_ref, b_in_ref,
+    gain_ref, w_up_ref, b_up_ref, out_ref,
 ):
-    w_in_copy = pltpu.make_async_copy(w_in_hbm, w_in_ref, w_in_sem)
-    w_in_copy.start()
     first_frame = 2 * place_ref[0]
     core = lax.rem(place_ref[0], 2)
     no_above = place_ref[1] == 0
@@ -363,7 +355,6 @@
     near = jnp.concatenate([tokens[i * 96 : (i + 1) * 96] for i in range(3)], axis=1)
     cells = jnp.dot(near, spread_ref[...], preferred_element_type=jnp.float32).astype(jnp.bfloat16)
 
-    w_in_copy.wait()
     hidden = jnp.zeros((256, C1), jnp.float32)
     for time_tap in (2, 1, 0):
         part = jnp.zeros((256, C1), jnp.float32)
@@ -427,13 +418,9 @@
     constants = [jnp.asarray(x, jnp.bfloat16) for x in (assembly(), spreading(), reordering())]
     return pl.pallas_call(
         decode_kernel,
-        in_specs=[pl.BlockSpec(memory_space=pltpu.SMEM)] * 2
-        + [vmem] * 5
-        + [pl.BlockSpec(memory_space=pltpu.HBM)]
-        + [vmem] * 4,
+        in_specs=[pl.BlockSpec(memory_space=pltpu.SMEM)] * 2 + [vmem] * 10,
         out_specs=vmem,
         out_shape=jax.ShapeDtypeStruct((2, 4, 64 * CO), jnp.bfloat16),
-        scratch_shapes=[pltpu.VMEM((27 * LC, C1), jnp.bfloat16), pltpu.SemaphoreType.DMA],
         compiler_params=pltpu.CompilerParams(vmem_limit_bytes=12 * MIB),
     )(
         clip_ids,
@@ -441,7 +428,7 @@
         back,
         *constants,
         jnp.concatenate([b_head, b_head])[None],
-        pltpu.with_memory_space_constraint(w_in, pltpu.HBM),
+        w_in,
         b_in[None],
         gain_in[None],
         w_up.T,
@@ -463,8 +450,8 @@
     upto = jnp.sum(clip_ids[None, :] <= clip_ids[:, None], axis=1, dtype=jnp.int32)
     kind = lax.broadcasted_iota(jnp.int32, (4, 2 * FRM), 0)
     meta = jnp.where(kind == 0, clip_ids, jnp.where(kind == 1, below, jnp.where(kind == 2, upto, core)))
-    mixed = attend(meta, own_q, own_kv, other_kv).reshape(SEQ, -1, HD)
-    by_row = lax.all_to_all(mixed, "seq", 0, 0, tiled=True)
+    mixed, w_in = attend(meta, own_q, own_kv, other_kv, w_in)
+    by_row = lax.all_to_all(mixed.reshape(SEQ, -1, HD), "seq", 0, 0, tiled=True)
     merged = merge(by_row.reshape(SEQ, 3, FRM // GATHER_F, GATHER_R, HD)).reshape(FRM, 24, HD)
     back = lax.all_to_all(merged, "frm", 0, 0, tiled=True)
 

time: 127 us -> 124 us (0.976); the launches traced: 127 us -> 125 us
  Pallas kernels: 22.5 us -> 19.7 us
    pallas_call x1, Pallas kernels: 13.5 us -> 11.6 us  [attend(): pl.pallas_call(attend_kernel, in_specs=[pl.BlockSpec(memory_space=pltpu.S...]
where the time goes in v5:
time: 124 us; the launch traced here: 125 us
  blocking collectives  83.2 us (67%)
  Pallas kernels  19.7 us (16%)
  waiting for transfers between devices  14.5 us (12%)
  starting transfers between devices  6.24 us (5%)
    all_to_all x1, blocking collectives, shards(): own = lax.all_to_all(slots, ('frm', 'seq'), 0, 0, tiled=True)  70.1 us
    all_to_all x1, blocking collectives, shards(): by_row = lax.all_to_all(mixed.reshape(SEQ, -1, HD), 'seq', 0, 0, tiled=True)  13 us
    all_to_all x1, waiting for transfers between devices, shards(): back = lax.all_to_all(merged, 'frm', 0, 0, tiled=True)  11.7 us
    pallas_call x1, Pallas kernels, attend(): pl.pallas_call(attend_kernel, in_specs=[pl.BlockSpec(memory_space=pltpu.S...  11.6 us
    all_to_all x1, starting transfers between devices, shards(): back = lax.all_to_all(merged, 'frm', 0, 0, tiled=True)  5.01 us
    pallas_call x1, Pallas kernels, decode(): pl.pallas_call(decode_kernel, in_specs=[pl.BlockSpec(memory_space=pltpu.S...  3.83 us
    ppermute x1, waiting for transfers between devices, shards(): other_kv = lax.ppermute(own_kv, 'frm', [(i, i ^ 1) for i in range(FRM)])  2.76 us
    pallas_call x1, Pallas kernels, pack(): pl.pallas_call(pack_kernel, in_specs=[hbm, hbm, hbm, hbm], out_specs=pl.B...  2.57 us
  transfers between devices with their start and end apart: 2, of which 2 were waited for; matrix products, arithmetic and copies ran while one was open for 0% of the time, Pallas kernels for 0%

profile of v5, /device:TPU:1, one launch (start us, length us, event | category | flops | bytes accessed | tf_op | source)
XLA Modules:
  0.0 125.2 jit_solution(7361046073749922552)
XLA Ops:
  0.0 2.6 %shard_map.145 = bf16[16,2,8,32,128]{4,3,2,1,0:T(8,128)(2,1)S(1)} custom-call(bf16[2,16,5120]{2,1,0:T(8,128)(2,1)} %q_hbm.1, bf16[2,16,5120]{2,1,0:T(8,128)(2,1)} %k_hbm.1, bf16[2,16,5120]{2,1,0:T(8,128)(2,1)} %v_hbm.1, bf16[64,5120]{1,0:T(8,128)(2,1)} %bitcast.18), custom_call_target="tpu_custom_call" | custom-call | tf_op jit(solution)/shard_map/pallas_call | solution.py:79
  2.6 70.1 %all_to_all.15 = bf16[256,32,128]{2,1,0:T(8,128)(2,1)S(1)} all-to-all(bf16[256,32,128]{2,1,0:T(8,128)(2,1)S(1)} %bitcast.11), channel_id=1, replica_groups=mesh['seq'=8,'frm'=32] {'frm','seq'}, dimensions={0} | all-to-all | bytes 4194304 | tf_op jit(solution)/shard_map/all_to_all | solution.py:445
  72.7 0.0 copy-start.7
  72.7 0.8 shard_map.146
  73.5 1.2 collective-permute-start
  74.8 0.0 copy-done.7
  74.8 0.2 convert_reduce_fusion.1
  75.0 0.1 select_select_fusion.meta_ref
  75.0 2.8 %collective-permute-done.other_ref = bf16[32,192,128]{2,1,0:T(8,128)(2,1)S(1)} collective-permute-done((bf16[32,192,128]{2,1,0:T(8,128)(2,1)S(1)}, bf16[32,192,128]{2,1,0:T(8,128)(2,1)S(1)}, u32[]{:S(2)}, u32[]{:S(2)}) %collective-permute-start) | collective-permute-done | bytes 1572896 | tf_op jit(solution)/shard_map/ppermute | solution.py:447
  77.8 0.0 copy-start.6
  77.8 0.0 copy-start.9
  77.8 0.0 copy-start.10
  77.8 0.0 copy-start.11
  77.8 11.6 %shard_map.147 = (bf16[8,3,4,24,128]{4,3,2,1,0:T(8,128)(2,1)S(1)}, bf16[432,384]{1,0:T(8,128)(2,1)S(1)}) custom-call(s32[4,64]{1,0:T(4,128)S(1)} %select_select_fusion.meta_ref, bf16[1536,128]{1,0:T(8,128)(2,1)S(1)} %get-tuple-element.9.q_ref, bf16[32,192,128]{2,1,0:T(8,128)(2,1)S(1)} %get-tuple-element.10.own_ref, ...), custom_call_target="tpu_custom_call" | custom-call | tf_op jit(solution)/shard_map/pallas_call | solution.py:243
  89.4 0.0 copy-start.3
  89.4 0.0 copy-start
  89.4 0.0 copy-start.1
  89.4 0.0 copy-start.2
  89.5 0.0 copy-start.5
  89.5 0.0 copy-start.8
  89.5 13.0 %all_to_all.16 = bf16[8,288,128]{2,1,0:T(8,128)(2,1)S(1)} all-to-all(bf16[8,288,128]{2,1,0:T(8,128)(2,1)S(1)} %bitcast.16), channel_id=1, replica_groups=mesh['seq'=8,'frm'=32] {'seq'}, dimensions={0} | all-to-all | bytes 1179648 | tf_op jit(solution)/shard_map/all_to_all | solution.py:454
  102.5 0.0 copy-done.6
  102.5 0.9 shard_map.148
  103.4 0.0 copy-done.3
  103.4 5.0 %all-to-all-start.2 = ((bf16[32,24,128]{2,1,0:T(8,128)(2,1)}), bf16[32,24,128]{2,1,0:T(8,128)(2,1)S(1)}, u32[]{:S(2)}, u32[]{:S(2)}) async-start(bf16[32,24,128]{2,1,0:T(8,128)(2,1)} %bitcast.5), calls=%async_computation.2 | async-start | bytes 393216 | tf_op jit(solution)/shard_map/all_to_all | solution.py:456
  108.4 0.0 copy-done.9
  108.4 0.0 copy-done.10
  108.5 0.0 copy-done.11
  108.5 0.1 maximum_bitcast_fusion.b_head_ref
  108.6 11.7 %all-to-all-done.2 = bf16[32,24,128]{2,1,0:T(8,128)(2,1)S(1)} async-done(((bf16[32,24,128]{2,1,0:T(8,128)(2,1)}), bf16[32,24,128]{2,1,0:T(8,128)(2,1)S(1)}, u32[]{:S(2)}, u32[]{:S(2)}) %all-to-all-start.2) | async-done | bytes 196640 | tf_op jit(solution)/shard_map/all_to_all | solution.py:456
  120.3 0.0 copy-done
  120.3 0.0 copy-done.1
  120.3 0.0 copy-done.2
  120.3 0.0 copy-done.5
  120.4 0.0 copy-done.8
  120.4 0.0 copy-start.4
  120.4 1.0 copy-done.4
  121.3 3.8 %shard_map.149 = bf16[2,4,12288]{2,1,0:T(4,128)(2,1)} custom-call(s32[64]{0:T(128)S(1)} %copy-done.7, s32[2]{0:T(128)S(1)} %compare_select_fusion.place_ref, bf16[5,6,24,128]{3,2,1,0:T(8,128)(2,1)S(1)} %bitcast.15, bf16[288,144]{1,0:T(8,128)(2,1)S(1)} %copy-done.5, bf16[384,1024]{1,0:T(8,128)(2,1)S(1)} %copy-done.1, bf16[3,256,256]{2,1,0:T(8,128)(2,1)S(1)} %copy-done.2, ...), custom_call_target="tpu_custom_call" | custom-call | tf_op jit(solution)/shard_map/pallas_call | solution.py:419
  (6 shorter events, 0.0 us)
Async XLA Ops:
  72.7 2.1 %copy-start.7 = (s32[64]{0:T(128)S(1)}, s32[64]{0:T(128)}, u32[]{:S(2)}) copy-start(s32[64]{0:T(128)} %clip_ref.1) | copy-start | bytes 772
  73.5 4.3 %collective-permute-start = (bf16[32,192,128]{2,1,0:T(8,128)(2,1)S(1)}, bf16[32,192,128]{2,1,0:T(8,128)(2,1)S(1)}, u32[]{:S(2)}, u32[]{:S(2)}) collective-permute-start(bf16[32,192,128]{2,1,0:T(8,128)(2,1)S(1)} %get-tuple-element.10.own_ref), channel_id=1, source_target_pairs={{0,1},{1,0},{2,3},{3,2},{4,5},{5,4},{6,7},{7,6},{8,9},{9,8},{10,11... | collective-permute-start | bytes 4718600 | tf_op jit(solution)/shard_map/ppermute | solution.py:447
  77.8 24.7 %copy-start.6 = (bf16[128,96]{1,0:T(8,128)(2,1)S(1)}, bf16[128,96]{1,0:T(8,128)(2,1)}, u32[]{:S(2)}) copy-start(bf16[128,96]{1,0:T(8,128)(2,1)} %constant.28.clone.widen_ref) | copy-start | bytes 73732
  77.8 30.6 %copy-start.9 = (f32[384]{0:T(512)S(1)}, f32[384]{0:T(512)}, u32[]{:S(2)}) copy-start(f32[384]{0:T(512)} %param.22) | copy-start | bytes 4612
  77.8 30.6 %copy-start.10 = (f32[384]{0:T(512)S(1)}, f32[384]{0:T(512)}, u32[]{:S(2)}) copy-start(f32[384]{0:T(512)} %param.23) | copy-start | bytes 4612
  77.8 30.7 %copy-start.11 = (f32[64]{0:T(128)S(1)}, f32[64]{0:T(128)}, u32[]{:S(2)}) copy-start(f32[64]{0:T(128)} %param.20) | copy-start | bytes 772
  89.4 14.0 %copy-start.3 = (bf16[432,384]{1,0:T(8,128)(2,1)}, bf16[432,384]{1,0:T(8,128)(2,1)S(1)}, u32[]{:S(2)}) copy-start(bf16[432,384]{1,0:T(8,128)(2,1)S(1)} %get-tuple-element.12.w_in_ref) | copy-start | bytes 995332
  89.4 30.9 %copy-start = (bf16[3456,192]{0,1:T(8,128)(2,1)S(1)}, bf16[3456,192]{0,1:T(8,128)(2,1)}, u32[]{:S(2)}) copy-start(bf16[3456,192]{0,1:T(8,128)(2,1)} %param.24) | copy-start | bytes 3981316
  89.4 30.9 %copy-start.1 = (bf16[384,1024]{1,0:T(8,128)(2,1)S(1)}, bf16[384,1024]{1,0:T(8,128)(2,1)}, u32[]{:S(2)}) copy-start(bf16[384,1024]{1,0:T(8,128)(2,1)} %constant.30.clone.spread_ref) | copy-start | bytes 2359300
  89.4 30.9 %copy-start.2 = (bf16[3,256,256]{2,1,0:T(8,128)(2,1)S(1)}, bf16[3,256,256]{2,1,0:T(8,128)(2,1)}, u32[]{:S(2)}) copy-start(bf16[3,256,256]{2,1,0:T(8,128)(2,1)} %constant.31.clone.order_ref) | copy-start | bytes 1179652
  89.5 30.9 %copy-start.5 = (bf16[288,144]{1,0:T(8,128)(2,1)S(1)}, bf16[288,144]{1,0:T(8,128)(2,1)}, u32[]{:S(2)}) copy-start(bf16[288,144]{1,0:T(8,128)(2,1)} %constant.29.clone.gather_ref) | copy-start | bytes 248836
  89.5 30.9 %copy-start.8 = (f32[192]{0:T(256)S(1)}, f32[192]{0:T(256)}, u32[]{:S(2)}) copy-start(f32[192]{0:T(256)} %param.25) | copy-start | bytes 2308
  103.4 16.9 %all-to-all-start.2 = ((bf16[32,24,128]{2,1,0:T(8,128)(2,1)}), bf16[32,24,128]{2,1,0:T(8,128)(2,1)S(1)}, u32[]{:S(2)}, u32[]{:S(2)}) async-start(bf16[32,24,128]{2,1,0:T(8,128)(2,1)} %bitcast.5), calls=%async_computation.2 | async-start | bytes 393216 | tf_op jit(solution)/shard_map/all_to_all | solution.py:456
  120.4 1.0 copy-start.4

commit v6 on v5

--- a/solution.py
+++ b/solution.py
@@ -29,7 +29,7 @@
 TILE_Q = 256
 TILES = FRM * FRAME_Q // TILE_Q
 TILE_SPAN = -(-TILE_Q // FRAME_Q) + 1
-SIZES = (12, 17, 24, 32)
+SIZES = (12, 17, 22, 27, 32)
 GROUP = 2
 COEF = math.log2(math.e) / math.sqrt(HD)
 FAR = -1e30
@@ -69,8 +69,8 @@
                 for part in range(PARTS):
                     own = q if part == 0 else pltpu.roll(q, 16 - part * STEP, 0)
                     tail = jnp.concatenate([packed, own[:8]], axis=0)
-                    out_ref[g * PARTS + part, c, s, 0:16, :] = k
-                    out_ref[g * PARTS + part, c, s, 16:32, :] = tail.astype(jnp.bfloat16)
+                    out_ref[s, g * PARTS + part, c, 0:16, :] = k
+                    out_ref[s, g * PARTS + part, c, 16:32, :] = tail.astype(jnp.bfloat16)
 
 
 def pack(queries, keys, values, w_head):
@@ -80,7 +80,7 @@
         pack_kernel,
         in_specs=[hbm, hbm, hbm, hbm],
         out_specs=pl.BlockSpec(memory_space=pltpu.VMEM),
-        out_shape=pltpu.VMEM((FRM // 2, 2, SEQ, SLOT, HD), jnp.bfloat16),
+        out_shape=pltpu.VMEM((SEQ, FRM // 2, 2, SLOT, HD), jnp.bfloat16),
         scratch_shapes=[
             act,
             act,
@@ -102,12 +102,13 @@
     def body(i, carry):
         for j in range(2):
             f = 2 * i + j
-            kv_ref[f, 0:128, :] = in_ref[f, :, 0:16, :].reshape(128, HD)
-            packed = in_ref[f, :, 16:32, :].astype(jnp.float32)[:, :8]
+            kv_ref[f, 0:128, :] = in_ref[:, f, 0:16, :].reshape(128, HD)
+            packed = in_ref[:, f, 16:32, :].astype(jnp.float32)[:, :8]
             rolled = pltpu.roll(packed.reshape(SEQ * 8, HD), LAT, 1).reshape(SEQ, 8, HD)
             block = jnp.concatenate([packed, rolled], axis=1).reshape(128, HD).T
             kv_ref[f, 128:192, :] = block[:LAT].astype(jnp.bfloat16)
-        q = in_ref[pl.ds(2 * i, 2), :, 16:32, :].reshape(256, HD)
+        q = [in_ref[:, 2 * i + j, 16:32, :].reshape(128, HD) for j in range(2)]
+        q = jnp.concatenate(q, axis=0)
         q = jnp.dot(pick_ref[...], q, preferred_element_type=jnp.float32)
         rows = pl.multiple_of(i * 2 * FRAME_Q, 2 * FRAME_Q)
         q_ref[pl.ds(rows, 2 * FRAME_Q), :] = q.astype(jnp.bfloat16)
@@ -131,12 +132,8 @@
     )(own)
 
 
-def attend_kernel(
-    meta_ref, q_ref, own_ref, other_ref, w_in_hbm, out_ref, w_in_ref, s_ref, done_ref, place_ref, w_in_sem
-):
+def attend_kernel(meta_ref, q_ref, own_ref, other_ref, out_ref, s_ref, done_ref, place_ref):
     core = meta_ref[3, 0]
-    w_in_copy = pltpu.make_async_copy(w_in_hbm, w_in_ref, w_in_sem)
-    w_in_copy.start()
     share = lax.broadcasted_iota(jnp.int32, (SEQ * GATHER_R, 1), 0)
     source = jnp.zeros_like(share)
     for size, unit, stop in ((GATHER_R, SHARE, SEQ), (SHARE, FRAME_Q, GATHER_F // 2)):
@@ -235,10 +232,9 @@
                 owner = s + 1 - halo
                 if 0 <= owner < SEQ:
                     out_ref[owner, halo, i] = piece
-    w_in_copy.wait()
-
-
-def attend(meta, q, own, other, w_in):
+
+
+def attend(meta, q, own, other):
     vmem = pl.BlockSpec(memory_space=pltpu.VMEM)
     return pl.pallas_call(
         attend_kernel,
@@ -247,31 +243,31 @@
             vmem,
             vmem,
             vmem,
-            pl.BlockSpec(memory_space=pltpu.HBM),
         ],
-        out_specs=[vmem, vmem],
-        out_shape=[
-            pltpu.VMEM((SEQ, 3, FRM // GATHER_F, GATHER_R, HD), jnp.bfloat16),
-            pltpu.VMEM(w_in.shape, jnp.bfloat16),
-        ],
+        out_specs=vmem,
+        out_shape=pltpu.VMEM((SEQ, 3, FRM // GATHER_F, GATHER_R, HD), jnp.bfloat16),
         scratch_shapes=[
             pltpu.VMEM((GROUP, 2, FRM * 128, TILE_Q), jnp.float32),
             pltpu.VMEM((FRM * FRAME_Q, HD), jnp.float32),
             pltpu.VMEM((SEQ * GATHER_R, SEQ * GATHER_R), jnp.bfloat16),
-            pltpu.SemaphoreType.DMA,
         ],
         compiler_params=pltpu.CompilerParams(vmem_limit_bytes=36 * MIB),
-    )(meta, q, own, other, pltpu.with_memory_space_constraint(w_in, pltpu.HBM))
-
-
-def merge_kernel(in_ref, widen_ref, out_ref):
+    )(meta, q, own, other)
+
+
+def merge_kernel(in_ref, out_ref):
     low = lax.broadcasted_iota(jnp.int32, (FRM // 2, 8, HD), 2) < LAT
+    row = lax.broadcasted_iota(jnp.int32, (FRM // 2 * 8, FRM // 2 * SHARE), 0)
+    col = lax.broadcasted_iota(jnp.int32, (FRM // 2 * 8, FRM // 2 * SHARE), 1)
+    share = lax.bitwise_and(row, 7)
+    hit = (col == SHARE * lax.shift_right_logical(row, 3) + share) & (share < SHARE)
+    widen = jnp.where(hit, 1.0, 0.0).astype(jnp.bfloat16)
     for halo in range(3):
         total = in_ref[0, halo].astype(jnp.float32)
         for head in range(1, SEQ):
             total = total + in_ref[head, halo].astype(jnp.float32)
         total = total.reshape(FRM // 2 * SHARE, HD).astype(jnp.bfloat16)
-        total = jnp.dot(widen_ref[...], total, preferred_element_type=jnp.float32)
+        total = jnp.dot(widen, total, preferred_element_type=jnp.float32)
         total = total.reshape(FRM // 2, 8, HD)
         before = jnp.concatenate([total[:1], total[:-1]], axis=0)
         out_ref[:, 0, halo] = jnp.where(low, total, before).astype(jnp.bfloat16)
@@ -280,18 +276,13 @@
 
 def merge(parts):
     vmem = pl.BlockSpec(memory_space=pltpu.VMEM)
-    widen = np.zeros((FRM // 2, 8, FRM // 2, SHARE), np.float32)
-    for f in range(FRM // 2):
-        for t in range(SHARE):
-            widen[f, t, f, t] = 1
-    widen = jnp.asarray(widen.reshape(FRM // 2 * 8, FRM // 2 * SHARE), jnp.bfloat16)
     return pl.pallas_call(
         merge_kernel,
-        in_specs=[vmem, vmem],
+        in_specs=[vmem],
         out_specs=vmem,
         out_shape=pltpu.VMEM((FRM // 2, 2, 3, 8, HD), jnp.bfloat16),
         compiler_params=pltpu.CompilerParams(vmem_limit_bytes=12 * MIB),
-    )(parts, widen)
+    )(parts)
 
 
 def assembly():
@@ -333,7 +324,7 @@
 
 
 def decode_kernel(
-    clip_ref, place_ref, in_ref, gather_ref, spread_ref, order_ref, b_head_ref, w_in_ref, b_in_ref,
+    clip_ref, place_ref, in_ref, table_ref, b_head_ref, w_in_ref, b_in_ref,
     gain_ref, w_up_ref, b_up_ref, out_ref,
 ):
     first_frame = 2 * place_ref[0]
@@ -350,10 +341,15 @@
     patch = lax.rem(lax.shift_right_logical(row, 3), 3)
     outside = ((patch == 0) & no_above) | ((patch == 2) & no_below)
     tokens = jnp.where(outside, 0.0, total).astype(jnp.bfloat16)
-    tokens = jnp.dot(gather_ref[...], tokens, preferred_element_type=jnp.float32)
+    gather = table_ref[768:1056, 0:144]
+    tokens = jnp.dot(gather, tokens, preferred_element_type=jnp.float32)
     tokens = tokens.astype(jnp.bfloat16)
     near = jnp.concatenate([tokens[i * 96 : (i + 1) * 96] for i in range(3)], axis=1)
-    cells = jnp.dot(near, spread_ref[...], preferred_element_type=jnp.float32).astype(jnp.bfloat16)
+    cells = []
+    for i in range(4):
+        spread = table_ref[1056 + i * 384 : 1056 + (i + 1) * 384, :]
+        cells.append(jnp.dot(near, spread, preferred_element_type=jnp.float32))
+    cells = jnp.concatenate(cells, axis=1).astype(jnp.bfloat16)
 
     hidden = jnp.zeros((256, C1), jnp.float32)
     for time_tap in (2, 1, 0):
@@ -393,7 +389,8 @@
 
     taps = [jnp.zeros((256, CO), jnp.float32) for _ in range(3)]
     for row_tap in range(3):
-        placed = jnp.dot(order_ref[row_tap], active, preferred_element_type=jnp.float32)
+        order = table_ref[row_tap * 256 : (row_tap + 1) * 256, :]
+        placed = jnp.dot(order, active, preferred_element_type=jnp.float32)
         placed = placed.astype(jnp.bfloat16)
         for col_tap in range(3):
             tap = (row_tap * 3 + col_tap) * C1
@@ -415,10 +412,13 @@
 
 def decode(clip_ids, place, back, b_head, w_in, b_in, gain_in, w_up, b_up):
     vmem = pl.BlockSpec(memory_space=pltpu.VMEM)
-    constants = [jnp.asarray(x, jnp.bfloat16) for x in (assembly(), spreading(), reordering())]
+    table = np.zeros((2592, 256), np.float32)
+    table[:768] = reordering().reshape(768, 256)
+    table[768:1056, :144] = assembly()
+    table[1056:] = spreading().reshape(384, 4, 256).transpose(1, 0, 2).reshape(1536, 256)
     return pl.pallas_call(
         decode_kernel,
-        in_specs=[pl.BlockSpec(memory_space=pltpu.SMEM)] * 2 + [vmem] * 10,
+        in_specs=[pl.BlockSpec(memory_space=pltpu.SMEM)] * 2 + [vmem] * 8,
         out_specs=vmem,
         out_shape=jax.ShapeDtypeStruct((2, 4, 64 * CO), jnp.bfloat16),
         compiler_params=pltpu.CompilerParams(vmem_limit_bytes=12 * MIB),
@@ -426,7 +426,7 @@
         clip_ids,
         place,
         back,
-        *constants,
+        jnp.asarray(table, jnp.bfloat16),
         jnp.concatenate([b_head, b_head])[None],
         w_in,
         b_in[None],
@@ -442,15 +442,15 @@
     core = lax.rem(frame_position, 2)
 
     slots = pack(queries, keys, values, w_head).reshape(FRM * SEQ, SLOT, HD)
-    own = lax.all_to_all(slots, ("frm", "seq"), 0, 0, tiled=True)
-    own_kv, own_q = prepare(own.reshape(FRM, SEQ, SLOT, HD))
+    own = lax.all_to_all(slots, ("seq", "frm"), 0, 0, tiled=True)
+    own_kv, own_q = prepare(own.reshape(SEQ, FRM, SLOT, HD))
     other_kv = lax.ppermute(own_kv, "frm", [(i, i ^ 1) for i in range(FRM)])
 
     below = jnp.sum(clip_ids[None, :] < clip_ids[:, None], axis=1, dtype=jnp.int32)
     upto = jnp.sum(clip_ids[None, :] <= clip_ids[:, None], axis=1, dtype=jnp.int32)
     kind = lax.broadcasted_iota(jnp.int32, (4, 2 * FRM), 0)
     meta = jnp.where(kind == 0, clip_ids, jnp.where(kind == 1, below, jnp.where(kind == 2, upto, core)))
-    mixed, w_in = attend(meta, own_q, own_kv, other_kv, w_in)
+    mixed = attend(meta, own_q, own_kv, other_kv)
     by_row = lax.all_to_all(mixed.reshape(SEQ, -1, HD), "seq", 0, 0, tiled=True)
     merged = merge(by_row.reshape(SEQ, 3, FRM // GATHER_F, GATHER_R, HD)).reshape(FRM, 24, HD)
     back = lax.all_to_all(merged, "frm", 0, 0, tiled=True)

time: 124 us -> 123 us (level)
    all_to_all x1, blocking collectives: 70.1 us -> 68.7 us  [shards(): own = lax.all_to_all(slots, ('seq', 'frm'), 0, 0, tiled=True)]
where the time goes in v6:
time: 123 us; the launch traced here: 124 us
  blocking collectives  82.5 us (67%)
  Pallas kernels  19.2 us (16%)
  waiting for transfers between devices  14.7 us (12%)
  starting transfers between devices  5.58 us (5%)
    all_to_all x1, blocking collectives, shards(): own = lax.all_to_all(slots, ('seq', 'frm'), 0, 0, tiled=True)  68.7 us
    all_to_all x1, blocking collectives, shards(): by_row = lax.all_to_all(mixed.reshape(SEQ, -1, HD), 'seq', 0, 0, tiled=True)  13.8 us
    all_to_all x1, waiting for transfers between devices, shards(): back = lax.all_to_all(merged, 'frm', 0, 0, tiled=True)  11.5 us
    pallas_call x1, Pallas kernels, attend(): pl.pallas_call(attend_kernel, in_specs=[pl.BlockSpec(memory_space=pltpu.S...  11.1 us
    all_to_all x1, starting transfers between devices, shards(): back = lax.all_to_all(merged, 'frm', 0, 0, tiled=True)  5.48 us
    pallas_call x1, Pallas kernels, decode(): pl.pallas_call(decode_kernel, in_specs=[pl.BlockSpec(memory_space=pltpu.S...  3.83 us
    ppermute x1, waiting for transfers between devices, shards(): other_kv = lax.ppermute(own_kv, 'frm', [(i, i ^ 1) for i in range(FRM)])  3.11 us
    pallas_call x1, Pallas kernels, pack(): pl.pallas_call(pack_kernel, in_specs=[hbm, hbm, hbm, hbm], out_specs=pl.B...  2.57 us
  transfers between devices with their start and end apart: 2, of which 2 were waited for; matrix products, arithmetic and copies ran while one was open for 0% of the time, Pallas kernels for 0%

profile of v6, /device:TPU:1, one launch (start us, length us, event | category | flops | bytes accessed | tf_op | source)
XLA Modules:
  0.0 123.5 jit_solution(16206148347978609133)
XLA Ops:
  0.0 2.6 %shard_map.118 = bf16[8,16,2,32,128]{4,3,2,1,0:T(8,128)(2,1)S(1)} custom-call(bf16[2,16,5120]{2,1,0:T(8,128)(2,1)} %q_hbm.1, bf16[2,16,5120]{2,1,0:T(8,128)(2,1)} %k_hbm.1, bf16[2,16,5120]{2,1,0:T(8,128)(2,1)} %v_hbm.1, bf16[64,5120]{1,0:T(8,128)(2,1)} %bitcast.18), custom_call_target="tpu_custom_call" | custom-call | tf_op jit(solution)/shard_map/pallas_call | solution.py:79
  2.6 68.7 %all_to_all.15 = bf16[256,32,128]{2,1,0:T(8,128)(2,1)S(1)} all-to-all(bf16[256,32,128]{2,1,0:T(8,128)(2,1)S(1)} %bitcast.11), channel_id=1, replica_groups=mesh['seq'=8,'frm'=32] {'seq','frm'}, dimensions={0} | all-to-all | bytes 4194304 | tf_op jit(solution)/shard_map/all_to_all | solution.py:445
  71.3 0.0 copy-start.3
  71.3 0.8 shard_map.119
  72.1 0.1 collective-permute-start
  72.3 0.0 copy-done.3
  72.3 0.2 convert_reduce_fusion.1
  72.4 0.1 select_select_fusion.meta_ref
  72.5 3.1 %collective-permute-done.other_ref = bf16[32,192,128]{2,1,0:T(8,128)(2,1)S(1)} collective-permute-done((bf16[32,192,128]{2,1,0:T(8,128)(2,1)S(1)}, bf16[32,192,128]{2,1,0:T(8,128)(2,1)S(1)}, u32[]{:S(2)}, u32[]{:S(2)}) %collective-permute-start) | collective-permute-done | bytes 1572896 | tf_op jit(solution)/shard_map/ppermute | solution.py:447
  75.6 0.0 copy-start.5
  75.6 0.0 copy-start.6
  75.6 0.0 copy-start.7
  75.6 11.1 %shard_map.120 = bf16[8,3,4,24,128]{4,3,2,1,0:T(8,128)(2,1)S(1)} custom-call(s32[4,64]{1,0:T(4,128)S(1)} %select_select_fusion.meta_ref, bf16[1536,128]{1,0:T(8,128)(2,1)S(1)} %get-tuple-element.7.q_ref, bf16[32,192,128]{2,1,0:T(8,128)(2,1)S(1)} %get-tuple-element.8.own_ref, bf16[32,192,128]{2,1,0:T(8,128)(2,1)S(1)} %collective-permute-done.other_ref), custom_call_target="tpu_custom_call" | custom-call | tf_op jit(solution)/shard_map/pallas_call | solution.py:239
  86.7 0.0 copy-start
  86.7 0.0 copy-start.1
  86.7 0.0 copy-start.4
  86.7 13.8 %all_to_all.16 = bf16[8,288,128]{2,1,0:T(8,128)(2,1)S(1)} all-to-all(bf16[8,288,128]{2,1,0:T(8,128)(2,1)S(1)} %bitcast.13), channel_id=1, replica_groups=mesh['seq'=8,'frm'=32] {'seq'}, dimensions={0} | all-to-all | bytes 1179648 | tf_op jit(solution)/shard_map/all_to_all | solution.py:454
  100.6 0.9 shard_map.121
  101.5 5.5 %all-to-all-start.2 = ((bf16[32,24,128]{2,1,0:T(8,128)(2,1)}), bf16[32,24,128]{2,1,0:T(8,128)(2,1)S(1)}, u32[]{:S(2)}, u32[]{:S(2)}) async-start(bf16[32,24,128]{2,1,0:T(8,128)(2,1)} %bitcast.5), calls=%async_computation.2 | async-start | bytes 393216 | tf_op jit(solution)/shard_map/all_to_all | solution.py:456
  107.0 0.0 copy-done.5
  107.0 0.0 copy-done.6
  107.0 0.0 copy-done.7
  107.0 0.1 maximum_bitcast_fusion.b_head_ref
  107.1 11.5 %all-to-all-done.2 = bf16[32,24,128]{2,1,0:T(8,128)(2,1)S(1)} async-done(((bf16[32,24,128]{2,1,0:T(8,128)(2,1)}), bf16[32,24,128]{2,1,0:T(8,128)(2,1)S(1)}, u32[]{:S(2)}, u32[]{:S(2)}) %all-to-all-start.2) | async-done | bytes 196640 | tf_op jit(solution)/shard_map/all_to_all | solution.py:456
  118.7 0.0 copy-done
  118.7 0.0 copy-done.1
  118.7 0.0 copy-done.4
  118.7 0.0 copy-start.2
  118.7 1.0 copy-done.2
  119.7 3.8 %shard_map.122 = bf16[2,4,12288]{2,1,0:T(4,128)(2,1)} custom-call(s32[64]{0:T(128)S(1)} %copy-done.3, s32[2]{0:T(128)S(1)} %compare_select_fusion.place_ref, bf16[5,6,24,128]{3,2,1,0:T(8,128)(2,1)S(1)} %bitcast.16, bf16[2592,256]{1,0:T(8,128)(2,1)S(1)} %copy-done.1, f32[1,128]{1,0:T(1,128)S(1)} %maximum_bitcast_fusion.b_head_ref, ...), custom_call_target="tpu_custom_call" | custom-call | tf_op jit(solution)/shard_map/pallas_call | solution.py:419
  (6 shorter events, 0.0 us)
Async XLA Ops:
  71.3 1.0 copy-start.3
  72.1 3.5 %collective-permute-start = (bf16[32,192,128]{2,1,0:T(8,128)(2,1)S(1)}, bf16[32,192,128]{2,1,0:T(8,128)(2,1)S(1)}, u32[]{:S(2)}, u32[]{:S(2)}) collective-permute-start(bf16[32,192,128]{2,1,0:T(8,128)(2,1)S(1)} %get-tuple-element.8.own_ref), channel_id=1, source_target_pairs={{0,1},{1,0},{2,3},{3,2},{4,5},{5,4},{6,7},{7,6},{8,9},{9,8},{10,11... | collective-permute-start | bytes 4718600 | tf_op jit(solution)/shard_map/ppermute | solution.py:447
  75.6 31.3 %copy-start.5 = (f32[384]{0:T(512)S(1)}, f32[384]{0:T(512)}, u32[]{:S(2)}) copy-start(f32[384]{0:T(512)} %param.19) | copy-start | bytes 4612
  75.6 31.4 %copy-start.6 = (f32[384]{0:T(512)S(1)}, f32[384]{0:T(512)}, u32[]{:S(2)}) copy-start(f32[384]{0:T(512)} %param.20) | copy-start | bytes 4612
  75.6 31.4 %copy-start.7 = (f32[64]{0:T(128)S(1)}, f32[64]{0:T(128)}, u32[]{:S(2)}) copy-start(f32[64]{0:T(128)} %param.17) | copy-start | bytes 772
  86.7 32.0 %copy-start = (bf16[3456,192]{0,1:T(8,128)(2,1)S(1)}, bf16[3456,192]{0,1:T(8,128)(2,1)}, u32[]{:S(2)}) copy-start(bf16[3456,192]{0,1:T(8,128)(2,1)} %param.21) | copy-start | bytes 3981316
  86.7 32.0 %copy-start.1 = (bf16[2592,256]{1,0:T(8,128)(2,1)S(1)}, bf16[2592,256]{1,0:T(8,128)(2,1)}, u32[]{:S(2)}) copy-start(bf16[2592,256]{1,0:T(8,128)(2,1)} %constant.22.clone.table_ref) | copy-start | bytes 3981316
  86.7 32.0 %copy-start.4 = (f32[192]{0:T(256)S(1)}, f32[192]{0:T(256)}, u32[]{:S(2)}) copy-start(f32[192]{0:T(256)} %param.22) | copy-start | bytes 2308
  101.5 17.2 %all-to-all-start.2 = ((bf16[32,24,128]{2,1,0:T(8,128)(2,1)}), bf16[32,24,128]{2,1,0:T(8,128)(2,1)S(1)}, u32[]{:S(2)}, u32[]{:S(2)}) async-start(bf16[32,24,128]{2,1,0:T(8,128)(2,1)} %bitcast.5), calls=%async_computation.2 | async-start | bytes 393216 | tf_op jit(solution)/shard_map/all_to_all | solution.py:456
  118.7 1.0 copy-start.2

commit v7 on v6

--- a/solution.py
+++ b/solution.py
@@ -29,7 +29,7 @@
 TILE_Q = 256
 TILES = FRM * FRAME_Q // TILE_Q
 TILE_SPAN = -(-TILE_Q // FRAME_Q) + 1
-SIZES = (12, 17, 22, 27, 32)
+SIZES = (12, 17, 24, 32)
 GROUP = 2
 COEF = math.log2(math.e) / math.sqrt(HD)
 FAR = -1e30
@@ -255,7 +255,7 @@
     )(meta, q, own, other)
 
 
-def merge_kernel(in_ref, out_ref):
+def merge_kernel(in_ref, w_in_ref, out_ref):
     low = lax.broadcasted_iota(jnp.int32, (FRM // 2, 8, HD), 2) < LAT
     row = lax.broadcasted_iota(jnp.int32, (FRM // 2 * 8, FRM // 2 * SHARE), 0)
     col = lax.broadcasted_iota(jnp.int32, (FRM // 2 * 8, FRM // 2 * SHARE), 1)
@@ -274,15 +274,15 @@
         out_ref[:, 1, halo] = total.astype(jnp.bfloat16)
 
 
-def merge(parts):
+def merge(parts, w_in):
     vmem = pl.BlockSpec(memory_space=pltpu.VMEM)
     return pl.pallas_call(
         merge_kernel,
-        in_specs=[vmem],
+        in_specs=[vmem, vmem],
         out_specs=vmem,
         out_shape=pltpu.VMEM((FRM // 2, 2, 3, 8, HD), jnp.bfloat16),
         compiler_params=pltpu.CompilerParams(vmem_limit_bytes=12 * MIB),
-    )(parts)
+    )(parts, w_in)
 
 
 def assembly():
@@ -452,7 +452,7 @@
     meta = jnp.where(kind == 0, clip_ids, jnp.where(kind == 1, below, jnp.where(kind == 2, upto, core)))
     mixed = attend(meta, own_q, own_kv, other_kv)
     by_row = lax.all_to_all(mixed.reshape(SEQ, -1, HD), "seq", 0, 0, tiled=True)
-    merged = merge(by_row.reshape(SEQ, 3, FRM // GATHER_F, GATHER_R, HD)).reshape(FRM, 24, HD)
+    merged = merge(by_row.reshape(SEQ, 3, FRM // GATHER_F, GATHER_R, HD), w_in).reshape(FRM, 24, HD)
     back = lax.all_to_all(merged, "frm", 0, 0, tiled=True)
 
     back = back[: 2 * PARTS * GROUPS].reshape(GROUPS, 2 * PARTS, 24, HD)

time: 123 us -> 124 us (level); the launches traced: 124 us -> 122 us
  starting transfers between devices: 5.58 us -> 3.91 us
    all_to_all x1, starting transfers between devices: 5.48 us -> 3.9 us  [shards(): back = lax.all_to_all(merged, 'frm', 0, 0, tiled=True)]
where the time goes in v7:
time: 124 us; the launch traced here: 122 us
  blocking collectives  82.1 us (66%)
  Pallas kernels  18.8 us (15%)
  waiting for transfers between devices  14.7 us (12%)
  starting transfers between devices  3.91 us (3%)
  local copies, waits for them, and re-layouts  1.81 us (1%)
    all_to_all x1, blocking collectives, shards(): own = lax.all_to_all(slots, ('seq', 'frm'), 0, 0, tiled=True)  68.7 us
    all_to_all x1, blocking collectives, shards(): by_row = lax.all_to_all(mixed.reshape(SEQ, -1, HD), 'seq', 0, 0, tiled=True)  13.4 us
    all_to_all x1, waiting for transfers between devices, shards(): back = lax.all_to_all(merged, 'frm', 0, 0, tiled=True)  11.5 us
    pallas_call x1, Pallas kernels, attend(): pl.pallas_call(attend_kernel, in_specs=[pl.BlockSpec(memory_space=pltpu.S...  10.7 us
    all_to_all x1, starting transfers between devices, shards(): back = lax.all_to_all(merged, 'frm', 0, 0, tiled=True)  3.9 us
    pallas_call x1, Pallas kernels, decode(): pl.pallas_call(decode_kernel, in_specs=[pl.BlockSpec(memory_space=pltpu.S...  3.83 us
    ppermute x1, waiting for transfers between devices, shards(): other_kv = lax.ppermute(own_kv, 'frm', [(i, i ^ 1) for i in range(FRM)])  3.13 us
    pallas_call x1, Pallas kernels, pack(): pl.pallas_call(pack_kernel, in_specs=[hbm, hbm, hbm, hbm], out_specs=pl.B...  2.57 us
  transfers between devices with their start and end apart: 2, of which 2 were waited for; matrix products, arithmetic and copies ran while one was open for 0% of the time, Pallas kernels for 0%

profile of v7, /device:TPU:1, one launch (start us, length us, event | category | flops | bytes accessed | tf_op | source)
XLA Modules:
  0.0 121.9 jit_solution(671946501924205917)
XLA Ops:
  0.0 2.6 %shard_map.118 = bf16[8,16,2,32,128]{4,3,2,1,0:T(8,128)(2,1)S(1)} custom-call(bf16[2,16,5120]{2,1,0:T(8,128)(2,1)} %q_hbm.1, bf16[2,16,5120]{2,1,0:T(8,128)(2,1)} %k_hbm.1, bf16[2,16,5120]{2,1,0:T(8,128)(2,1)} %v_hbm.1, bf16[64,5120]{1,0:T(8,128)(2,1)} %bitcast.18), custom_call_target="tpu_custom_call" | custom-call | tf_op jit(solution)/shard_map/pallas_call | solution.py:79
  2.6 68.7 %all_to_all.15 = bf16[256,32,128]{2,1,0:T(8,128)(2,1)S(1)} all-to-all(bf16[256,32,128]{2,1,0:T(8,128)(2,1)S(1)} %bitcast.11), channel_id=1, replica_groups=mesh['seq'=8,'frm'=32] {'seq','frm'}, dimensions={0} | all-to-all | bytes 4194304 | tf_op jit(solution)/shard_map/all_to_all | solution.py:445
  71.3 0.0 copy-start.5
  71.3 0.8 shard_map.119
  72.1 0.0 copy-start.3
  72.1 0.7 copy-done.3
  72.9 0.0 collective-permute-start
  72.9 0.0 copy-done.5
  72.9 0.2 convert_reduce_fusion.1
  73.1 0.1 select_select_fusion.meta_ref
  73.2 3.1 %collective-permute-done.other_ref = bf16[32,192,128]{2,1,0:T(8,128)(2,1)S(1)} collective-permute-done((bf16[32,192,128]{2,1,0:T(8,128)(2,1)S(1)}, bf16[32,192,128]{2,1,0:T(8,128)(2,1)S(1)}, u32[]{:S(2)}, u32[]{:S(2)}) %collective-permute-start) | collective-permute-done | bytes 1572896 | tf_op jit(solution)/shard_map/ppermute | solution.py:447
  76.3 0.0 copy-start.4
  76.3 1.0 copy-done.4
  77.3 0.0 copy-start.2
  77.3 10.7 %shard_map.120 = bf16[8,3,4,24,128]{4,3,2,1,0:T(8,128)(2,1)S(1)} custom-call(s32[4,64]{1,0:T(4,128)S(1)} %select_select_fusion.meta_ref, bf16[1536,128]{1,0:T(8,128)(2,1)S(1)} %copy-done.4, bf16[32,192,128]{2,1,0:T(8,128)(2,1)S(1)} %get-tuple-element.8.own_ref, bf16[32,192,128]{2,1,0:T(8,128)(2,1)S(1)} %collective-permute-done.other_ref), custom_call_target="tpu_custom_call" | custom-call | tf_op jit(solution)/shard_map/pallas_call | solution.py:239
  88.0 0.0 copy-start.7
  88.0 0.0 copy-start.8
  88.0 0.0 copy-start.9
  88.0 0.0 copy-start
  88.0 0.0 copy-start.1
  88.0 0.0 copy-start.6
  88.1 13.4 %all_to_all.16 = bf16[8,288,128]{2,1,0:T(8,128)(2,1)S(1)} all-to-all(bf16[8,288,128]{2,1,0:T(8,128)(2,1)S(1)} %bitcast.13), channel_id=1, replica_groups=mesh['seq'=8,'frm'=32] {'seq'}, dimensions={0} | all-to-all | bytes 1179648 | tf_op jit(solution)/shard_map/all_to_all | solution.py:454
  101.5 0.0 copy-done.2
  101.5 0.9 shard_map.121
  102.4 3.9 %all-to-all-start.2 = ((bf16[32,24,128]{2,1,0:T(8,128)(2,1)}), bf16[32,24,128]{2,1,0:T(8,128)(2,1)S(1)}, u32[]{:S(2)}, u32[]{:S(2)}) async-start(bf16[32,24,128]{2,1,0:T(8,128)(2,1)} %bitcast.5), calls=%async_computation.2 | async-start | bytes 393216 | tf_op jit(solution)/shard_map/all_to_all | solution.py:456
  106.3 0.0 copy-done.7
  106.3 0.0 copy-done.8
  106.4 0.0 copy-done.9
  106.4 0.1 maximum_bitcast_fusion.b_head_ref
  106.4 11.5 %all-to-all-done.2 = bf16[32,24,128]{2,1,0:T(8,128)(2,1)S(1)} async-done(((bf16[32,24,128]{2,1,0:T(8,128)(2,1)}), bf16[32,24,128]{2,1,0:T(8,128)(2,1)S(1)}, u32[]{:S(2)}, u32[]{:S(2)}) %all-to-all-start.2) | async-done | bytes 196640 | tf_op jit(solution)/shard_map/all_to_all | solution.py:456
  118.0 0.0 copy-done
  118.0 0.0 copy-done.1
  118.0 0.0 copy-done.6
  118.0 3.8 %shard_map.122 = bf16[2,4,12288]{2,1,0:T(4,128)(2,1)} custom-call(s32[64]{0:T(128)S(1)} %copy-done.5, s32[2]{0:T(128)S(1)} %compare_select_fusion.place_ref, bf16[5,6,24,128]{3,2,1,0:T(8,128)(2,1)S(1)} %bitcast.16, bf16[2592,256]{1,0:T(8,128)(2,1)S(1)} %copy-done.1, f32[1,128]{1,0:T(1,128)S(1)} %maximum_bitcast_fusion.b_head_ref, ...), custom_call_target="tpu_custom_call" | custom-call | tf_op jit(solution)/shard_map/pallas_call | solution.py:419
  (6 shorter events, 0.0 us)
Async XLA Ops:
  71.3 1.6 %copy-start.5 = (s32[64]{0:T(128)S(1)}, s32[64]{0:T(128)}, u32[]{:S(2)}) copy-start(s32[64]{0:T(128)} %clip_ref.1) | copy-start | bytes 772
  72.1 0.8 copy-start.3
  72.9 3.4 %collective-permute-start = (bf16[32,192,128]{2,1,0:T(8,128)(2,1)S(1)}, bf16[32,192,128]{2,1,0:T(8,128)(2,1)S(1)}, u32[]{:S(2)}, u32[]{:S(2)}) collective-permute-start(bf16[32,192,128]{2,1,0:T(8,128)(2,1)S(1)} %get-tuple-element.8.own_ref), channel_id=1, source_target_pairs={{0,1},{1,0},{2,3},{3,2},{4,5},{5,4},{6,7},{7,6},{8,9},{9,8},{10,11... | collective-permute-start | bytes 4718600 | tf_op jit(solution)/shard_map/ppermute | solution.py:447
  76.3 1.0 copy-start.4
  77.3 24.2 %copy-start.2 = (bf16[432,384]{1,0:T(8,128)(2,1)S(1)}, bf16[432,384]{1,0:T(8,128)(2,1)}, u32[]{:S(2)}) copy-start(bf16[432,384]{1,0:T(8,128)(2,1)} %w_in_ref.3) | copy-start | bytes 995332
  88.0 18.3 %copy-start.7 = (f32[384]{0:T(512)S(1)}, f32[384]{0:T(512)}, u32[]{:S(2)}) copy-start(f32[384]{0:T(512)} %param.19) | copy-start | bytes 4612
  88.0 18.3 %copy-start.8 = (f32[384]{0:T(512)S(1)}, f32[384]{0:T(512)}, u32[]{:S(2)}) copy-start(f32[384]{0:T(512)} %param.20) | copy-start | bytes 4612
  88.0 18.3 %copy-start.9 = (f32[64]{0:T(128)S(1)}, f32[64]{0:T(128)}, u32[]{:S(2)}) copy-start(f32[64]{0:T(128)} %param.17) | copy-start | bytes 772
  88.0 30.0 %copy-start = (bf16[3456,192]{0,1:T(8,128)(2,1)S(1)}, bf16[3456,192]{0,1:T(8,128)(2,1)}, u32[]{:S(2)}) copy-start(bf16[3456,192]{0,1:T(8,128)(2,1)} %param.21) | copy-start | bytes 3981316
  88.0 30.0 %copy-start.1 = (bf16[2592,256]{1,0:T(8,128)(2,1)S(1)}, bf16[2592,256]{1,0:T(8,128)(2,1)}, u32[]{:S(2)}) copy-start(bf16[2592,256]{1,0:T(8,128)(2,1)} %constant.22.clone.table_ref) | copy-start | bytes 3981316
  88.0 30.0 %copy-start.6 = (f32[192]{0:T(256)S(1)}, f32[192]{0:T(256)}, u32[]{:S(2)}) copy-start(f32[192]{0:T(256)} %param.22) | copy-start | bytes 2308
  102.4 15.6 %all-to-all-start.2 = ((bf16[32,24,128]{2,1,0:T(8,128)(2,1)}), bf16[32,24,128]{2,1,0:T(8,128)(2,1)S(1)}, u32[]{:S(2)}, u32[]{:S(2)}) async-start(bf16[32,24,128]{2,1,0:T(8,128)(2,1)} %bitcast.5), calls=%async_computation.2 | async-start | bytes 393216 | tf_op jit(solution)/shard_map/all_to_all | solution.py:456
